TPU v7x, 32 devices: a whole 2x2x4 slice. The times are simulated.
32 devices in a mesh: dp: 8 (over z, y), mp: 4 (over x, core).
Axes of the slice: x: 2, y: 2, z: 4, core: 2. Of those that a mesh axis runs over, the one named last changes fastest.
Arguments:
- tokens: bfloat16 [128, 128, 1024], P('dp', 'mp'), may hold values from -6 to 6
- cotangent: bfloat16 [128, 128, 1024], P('dp', 'mp'), may hold values from -6 to 6
- block_lang: int32 [128], P('dp'), may hold values from 0 to 15, as said below
- counts: int32 [128], P('dp'), may hold values from 1 to 128, as said below
- slot_of: int32 [16], replicated, may hold values from 0 to 15, as said below
- ln_gain: bfloat16 [1024, 16], P('mp', 'dp'), may hold values from 0.099609375 to 1.8984375
- w_down: bfloat16 [1024, 16, 512], P('mp', 'dp'), may hold values from -0.1875 to 0.1875
- w_up: bfloat16 [1024, 16, 512], P('mp', 'dp'), may hold values from -0.25 to 0.25
Outputs:
- token_grad: bfloat16 [128, 128, 1024], P('dp', 'mp')
- grad_down: bfloat16 [1024, 16, 512], P('mp', 'dp')
- grad_up: bfloat16 [1024, 16, 512], P('mp', 'dp')
Inputs may be any that keep to these rules, and one draw needn't show every extreme that they name: A permutation: language g's adapter is stored at index slot_of[g], on index slot_of[g] // 2 of dp. `block_lang`: with owner(g) = slot_of[g] // 2, at most 2 blocks of one index of dp name languages of one owner; in every draw some owner receives 2 blocks from every index of dp. `counts`: some block of every index of dp has all 128 rows live.
All inputs are finite; a program needn't handle non-finite values.
Results may differ from a plain program's by a relative error of at most 0.0062.
Values may be sent and summed in bfloat16 or wider, within the bound.
No kernel may reach another device: no remote copies, remote signals or barrier semaphores. Data moves between devices by JAX's collectives and lax.ppermute only.
A program may use at most 128 MiB of HBM per device.

v0:
```python
import jax
import jax.numpy as jnp
from jax import lax
from jax.sharding import PartitionSpec as P


def exact_gelu(values):
    return jax.nn.gelu(values, approximate=False)


def adapter_backward(inputs, cotan, live_rows, gains, down_cols, up_cols):
    values = inputs.astype(jnp.float32)
    row_mean = jnp.mean(values, axis=-1, keepdims=True)
    centered = values - row_mean
    inv_std = lax.rsqrt(jnp.mean(centered * centered, axis=-1, keepdims=True) + 1e-05)
    unit_rows = centered * inv_std
    gain_row = gains.astype(jnp.float32)[None, :]
    normed = (unit_rows * gain_row).astype(jnp.bfloat16)
    inner = jnp.dot(normed, down_cols, preferred_element_type=jnp.float32)
    activation, gelu_back = jax.vjp(exact_gelu, inner)
    act_low = activation.astype(jnp.bfloat16)
    masked = jnp.where(live_rows[:, None], cotan, jnp.zeros((), cotan.dtype))
    grad_act = jnp.dot(masked, up_cols, preferred_element_type=jnp.float32)
    grad_inner = gelu_back(grad_act)[0].astype(jnp.bfloat16)
    grad_normed = lax.dot_general(
        grad_inner, down_cols, (((1,), (1,)), ((), ())), preferred_element_type=jnp.float32
    )
    scaled = grad_normed * gain_row
    token_grad = masked.astype(jnp.float32) + inv_std * (
        scaled
        - jnp.mean(scaled, axis=-1, keepdims=True)
        - unit_rows * jnp.mean(scaled * unit_rows, axis=-1, keepdims=True)
    )
    return (token_grad.astype(jnp.bfloat16), normed, act_low, grad_inner, masked)


def shards(tokens, cotangent, block_lang, counts, slot_of, ln_gain, w_down, w_up):
    block_count, block_rows, features = tokens.shape
    dp_size = lax.axis_size("dp")
    mp_size = lax.axis_size("mp")
    mp_index = lax.axis_index("mp")
    lang_local = w_down.shape[1]
    bottleneck = w_down.shape[2]
    lang_count = slot_of.shape[0]
    capacity = (block_count + dp_size - 1) // dp_size
    slot_count = dp_size * capacity
    bf_zero = jnp.zeros((), jnp.bfloat16)
    gain_full, down_full, up_full = (
        lax.all_gather(ln_gain, "mp", axis=0, tiled=True),
        lax.all_gather(w_down, "mp", axis=0, tiled=True),
        lax.all_gather(w_up, "mp", axis=0, tiled=True),
    )
    lang_match = block_lang[:, None] == jnp.arange(lang_count, dtype=jnp.int32)[None, :]
    slot_ids = jnp.sum(jnp.where(lang_match, slot_of[None, :], 0), axis=1)
    owner_ids = slot_ids // lang_local
    local_ids = slot_ids % lang_local
    block_iota = jnp.arange(block_count, dtype=jnp.int32)
    earlier = (owner_ids[None, :] == owner_ids[:, None]) & (
        block_iota[None, :] < block_iota[:, None]
    )
    dest_ids = owner_ids * capacity + jnp.sum(earlier, axis=1, dtype=jnp.int32)
    slot_iota = jnp.arange(slot_count, dtype=jnp.int32)
    pick_mask = dest_ids[None, :] == slot_iota[:, None]
    has_block = jnp.any(pick_mask, axis=1)
    source_ids = jnp.sum(jnp.where(pick_mask, block_iota[None, :], 0), axis=1)
    send_x = jnp.where(has_block[:, None, None], tokens[source_ids], bf_zero)
    send_dy = jnp.where(has_block[:, None, None], cotangent[source_ids], bf_zero)
    slot_meta = jnp.stack(
        [
            jnp.where(has_block, counts[source_ids], 0),
            jnp.where(has_block, local_ids[source_ids], 0),
        ],
        axis=1,
    ).astype(jnp.bfloat16)
    recv_x, recv_dy, recv_meta = (
        lax.all_to_all(send_x, "dp", split_axis=0, concat_axis=0, tiled=True),
        lax.all_to_all(send_dy, "dp", split_axis=0, concat_axis=0, tiled=True),
        lax.all_to_all(slot_meta, "dp", split_axis=0, concat_axis=0, tiled=True),
    )
    recv_count = recv_meta[:, 0].astype(jnp.int32)
    recv_lang = recv_meta[:, 1].astype(jnp.int32)
    recv_live = recv_count > 0
    group_size = min(16, slot_count)
    group_count = (slot_count + group_size - 1) // group_size + lang_local - 1
    buf_slots = group_count * group_size
    lang_iota = jnp.arange(lang_local, dtype=jnp.int32)
    same_before = (
        (recv_lang[None, :] == recv_lang[:, None])
        & recv_live[None, :]
        & (slot_iota[None, :] < slot_iota[:, None])
    )
    rank_in = jnp.sum(same_before, axis=1, dtype=jnp.int32)
    lang_hits = (recv_lang[None, :] == lang_iota[:, None]) & recv_live[None, :]
    per_lang = jnp.sum(lang_hits, axis=1, dtype=jnp.int32)
    padded = (per_lang + group_size - 1) // group_size * group_size
    region_end = jnp.cumsum(padded)
    region_start = region_end - padded
    buf_pos = (
        jnp.sum(
            jnp.where(recv_lang[:, None] == lang_iota[None, :], region_start[None, :], 0), axis=1
        )
        + rank_in
    )
    buf_iota = jnp.arange(buf_slots, dtype=jnp.int32)
    fill_mask = (buf_pos[None, :] == buf_iota[:, None]) & recv_live[None, :]
    buf_has = jnp.any(fill_mask, axis=1)
    buf_source = jnp.sum(jnp.where(fill_mask, slot_iota[None, :], 0), axis=1)
    buf_x = jnp.where(buf_has[:, None, None], recv_x[buf_source], bf_zero)
    buf_dy = jnp.where(buf_has[:, None, None], recv_dy[buf_source], bf_zero)
    buf_count = jnp.where(buf_has, recv_count[buf_source], 0)
    row_ids = mp_index * block_rows + jnp.arange(block_rows, dtype=jnp.int32)
    buf_live = row_ids[None, :] < buf_count[:, None]
    group_starts = jnp.arange(group_count, dtype=jnp.int32) * group_size
    group_lang = jnp.minimum(
        jnp.sum(region_end[None, :] <= group_starts[:, None], axis=1, dtype=jnp.int32),
        lang_local - 1,
    )
    group_rows = group_size * block_rows

    def one_group(inputs_now):
        group_x, group_dy, group_live, lang_now = inputs_now
        gains = lax.dynamic_index_in_dim(gain_full, lang_now, 1, keepdims=False)
        down_cols = lax.dynamic_index_in_dim(down_full, lang_now, 1, keepdims=False)
        up_cols = lax.dynamic_index_in_dim(up_full, lang_now, 1, keepdims=False)
        return adapter_backward(group_x, group_dy, group_live, gains, down_cols, up_cols)

    token_part, normed_all, act_all, inner_all, masked_all = lax.map(
        one_group,
        (
            buf_x.reshape(group_count, group_rows, features),
            buf_dy.reshape(group_count, group_rows, features),
            buf_live.reshape(group_count, group_rows),
            group_lang,
        ),
    )
    scale = 1.0 / (block_rows * mp_size)
    term_rows = jnp.zeros((features, 2, lang_local, bottleneck), jnp.float32)
    for group in range(group_count):
        normed_cols = normed_all[group]
        masked_cols = masked_all[group]
        down_part = lax.dot_general(
            normed_cols,
            inner_all[group],
            (((0,), (0,)), ((), ())),
            preferred_element_type=jnp.float32,
        )
        up_part = lax.dot_general(
            masked_cols,
            act_all[group],
            (((0,), (0,)), ((), ())),
            preferred_element_type=jnp.float32,
        )
        selector = (lang_iota == group_lang[group]).astype(jnp.float32)
        term_rows = (
            term_rows
            + jnp.stack([down_part, up_part], axis=1)[:, :, None, :] * selector[None, None, :, None]
        )
    reduced = lax.psum_scatter(term_rows * scale, "mp", scatter_dimension=0, tiled=True)
    grad_down = reduced[:, 0].astype(jnp.bfloat16)
    grad_up = reduced[:, 1].astype(jnp.bfloat16)
    grad_buf = token_part.reshape(buf_slots, block_rows, features)
    back_pos = jnp.minimum(buf_pos, buf_slots - 1)
    grad_recv = jnp.where(recv_live[:, None, None], grad_buf[back_pos], bf_zero)
    returned = lax.all_to_all(grad_recv, "dp", split_axis=0, concat_axis=0, tiled=True)
    token_grad = returned[dest_ids]
    return (token_grad, grad_down, grad_up)


def solution(mesh):
    placed = (
        P("dp", "mp", None),
        P("dp", "mp", None),
        P("dp"),
        P("dp"),
        P(),
        P("mp", "dp"),
        P("mp", "dp", None),
        P("mp", "dp", None),
    )
    return jax.shard_map(
        shards,
        mesh=mesh,
        in_specs=placed,
        out_specs=(P("dp", "mp", None), P("mp", "dp", None), P("mp", "dp", None)),
        check_vma=False,
    )
```

profile of v0, /device:TPU:0, one launch (start us, length us, event | category | flops | bytes accessed | tf_op | source)
XLA Modules:
  0.0 238.8 jit_solution(16310842668384766351)
XLA Ops:
  7.2 2.0 copy.21
  12.8 7.3 %all-to-all-start = ((bf16[8,2,2]{1,2,0:T(2,128)(2,1)}), bf16[8,2,2]{1,2,0:T(2,128)(2,1)S(1)}, u32[]{:S(2)}, u32[]{:S(2)}) async-start(bf16[8,2,2]{1,2,0:T(2,128)(2,1)} %copy.19), calls=%async_computation | async-start | bytes 8192 | tf_op jit(solution)/shard_map/all_to_all | solution.py:78
  22.9 3.6 %all-to-all-done = bf16[8,2,2]{1,2,0:T(2,128)(2,1)S(1)} async-done(((bf16[8,2,2]{1,2,0:T(2,128)(2,1)}), bf16[8,2,2]{1,2,0:T(2,128)(2,1)S(1)}, u32[]{:S(2)}, u32[]{:S(2)}) %all-to-all-start) | async-done | bytes 96 | tf_op jit(solution)/shard_map/all_to_all | solution.py:78
  26.4 3.6 %all-to-all-start.1 = ((bf16[16,32,1024]{2,1,0:T(8,128)(2,1)}), bf16[16,32,1024]{2,1,0:T(8,128)(2,1)S(1)}, u32[]{:S(2)}, u32[]{:S(2)}) async-start(bf16[16,32,1024]{2,1,0:T(8,128)(2,1)} %get-tuple-element.127), calls=%async_computation.1 | async-start | bytes 2097152 | tf_op jit(solution)/shard_map/all_to_all | solution.py:77
  31.1 5.1 %all_gather.9 = bf16[1024,2]{0,1:T(2,128)(2,1)S(1)} all-gather(bf16[256,2]{0,1:T(2,128)(2,1)S(1)} %copy-done.15), channel_id=1, replica_groups=mesh['dp'=8,'mp'=4] {'mp'}, dimensions={0}, use_global_device_ids=true | all-gather | bytes 5120 | tf_op jit(solution)/shard_map/all_gather | solution.py:49
  36.8 18.0 %all-to-all-done.1 = bf16[16,32,1024]{2,1,0:T(8,128)(2,1)S(1)} async-done(((bf16[16,32,1024]{2,1,0:T(8,128)(2,1)}), bf16[16,32,1024]{2,1,0:T(8,128)(2,1)S(1)}, u32[]{:S(2)}, u32[]{:S(2)}) %all-to-all-start.1) | async-done | bytes 1048608 | tf_op jit(solution)/shard_map/all_to_all | solution.py:77
  54.7 3.6 %all-to-all-start.2 = ((bf16[16,32,1024]{2,1,0:T(8,128)(2,1)}), bf16[16,32,1024]{2,1,0:T(8,128)(2,1)S(1)}, u32[]{:S(2)}, u32[]{:S(2)}) async-start(bf16[16,32,1024]{2,1,0:T(8,128)(2,1)} %get-tuple-element.126), calls=%async_computation.2 | async-start | bytes 2097152 | tf_op jit(solution)/shard_map/all_to_all | solution.py:76
  61.9 2.0 gather_fusion.4
  63.9 20.2 %all-to-all-done.2 = bf16[16,32,1024]{2,1,0:T(8,128)(2,1)S(1)} async-done(((bf16[16,32,1024]{2,1,0:T(8,128)(2,1)}), bf16[16,32,1024]{2,1,0:T(8,128)(2,1)S(1)}, u32[]{:S(2)}, u32[]{:S(2)}) %all-to-all-start.2) | async-done | bytes 1048608 | tf_op jit(solution)/shard_map/all_to_all | solution.py:76
  84.1 2.0 gather_fusion.6
  86.1 3.9 %bitcast_select_fusion.1 = (bf16[2,512,1024]{2,1,0:T(8,128)(2,1)S(1)}, bf16[2,512,1024]{2,1,0:T(8,128)(2,1)}) fusion(pred[2,512]{1,0:T(4,128)(4,1)S(1)} %broadcast_in_dim.180, bf16[2,512,1024]{2,1,0:T(8,128)(2,1)} %bitcast.193, bf16[2,512,1024]{2,1,0:T(8,128)(2,1)} %bitcast.192), kind=kLoop, calls=%fused_computation.78 | loop fusion | flops 2097152 | bytes 8389632 | tf_op jit(solution)/shard_map/jit(_where)/select_n | solution.py:108
  93.2 1.6 broadcast.573.clone.1
  94.9 33.0 %while.18 = (s32[]{:T(128)}, bf16[2,512,1024]{2,1,0:T(8,128)(2,1)}, bf16[2,512,1024]{2,1,0:T(8,128)(2,1)}, bf16[2,512,512]{2,1,0:T(8,128)(2,1)}, bf16[2,512,512]...) while((s32[]{:T(128)}, bf16[2,512,1024]{2,1,0:T(8,128)(2,1)}, ...), condition=%wide.region_16.17_spmd, body=%wide.region_11.16_spmd.sunk | while | flops 1650198016 | bytes 108078112 | solution.py:127
  99.0 3.7 %fusion.83 = (bf16[2,512,512]{2,1,0:T(8,128)(2,1)}, f32[512,512]{1,0:T(8,128)S(1)}, f32[512,512]{1,0:T(8,128)S(1)}) fusion(bf16[2,512,512]{2,1,0:T(8,128)(2,1)} %get-tuple-element.262, s32[]{:T(128)} %get-tuple-element.259, bf16[1024,2,512]{2,0,1:T(8,128)(2,1)S(1)} %copy-done.16, s32[]{:T(128)S(6)} %select_n.256, f32[1024]{0:T(1024)S(1)} %bitcast.195, ...), kind=kOutput, calls=%fused_computation.60.clone.1 | convolution fusion | flops 556531712 | bytes 4727812 | tf_op jit(solution)/shard_map/while/body/eval_jaxpr/dot_general | solution.py:19
  115.5 3.7 %fusion.83 = (bf16[2,512,512]{2,1,0:T(8,128)(2,1)}, f32[512,512]{1,0:T(8,128)S(1)}, f32[512,512]{1,0:T(8,128)S(1)}) fusion(bf16[2,512,512]{2,1,0:T(8,128)(2,1)} %get-tuple-element.262, s32[]{:T(128)} %get-tuple-element.259, bf16[1024,2,512]{2,0,1:T(8,128)(2,1)S(1)} %copy-done.16, s32[]{:T(128)S(6)} %select_n.256, f32[1024]{0:T(1024)S(1)} %bitcast.195, ...), kind=kOutput, calls=%fused_computation.60.clone.1 | convolution fusion | flops 556531712 | bytes 4727812 | tf_op jit(solution)/shard_map/while/body/eval_jaxpr/dot_general | solution.py:19
  127.8 2.3 convolution_bitcast_fusion.1
  134.5 5.6 %add_multiply_fusion = f32[1024,2,2,512]{3,2,0,1:T(2,128)S(1)} fusion(f32[1024,2,512]{2,0,1:T(8,128)S(1)} %get-tuple-element.135, f32[1024,2,512]{2,0,1:T(8,128)S(1)} %get-tuple-element.134, f32[2]{0:T(128)S(1)} %get-tuple-element.136, f32[2]{0:T(128)S(1)} %get-tuple-element.137), kind=kLoop, calls=%fused_computation.74 | loop fusion | flops 8388608 | bytes 16777232 | tf_op jit(solution)/shard_map/mul | solution.py:158
  140.2 5.9 %copy.23 = f32[1024,2,2,512]{3,2,1,0:T(2,128)} copy(f32[1024,2,2,512]{3,2,0,1:T(2,128)S(1)} %add_multiply_fusion) | data formatting | bytes 16777216
  146.0 11.8 %reshape.529 = f32[1024,2048]{1,0:T(8,128)} reshape(f32[1024,2,2,512]{3,2,1,0:T(2,128)} %copy.23) | data formatting | bytes 16777216
  161.1 3.6 %all-to-all-start.3 = ((bf16[16,32,1024]{2,1,0:T(8,128)(2,1)}), bf16[16,32,1024]{2,1,0:T(8,128)(2,1)S(1)}, u32[]{:S(2)}, u32[]{:S(2)}) async-start(bf16[16,32,1024]{2,1,0:T(8,128)(2,1)} %broadcast_select_fusion.4), calls=%async_computation.3 | async-start | bytes 2097152 | tf_op jit(solution)/shard_map/all_to_all | solution.py:164
  164.8 25.9 %all-to-all-done.3 = bf16[16,32,1024]{2,1,0:T(8,128)(2,1)S(1)} async-done(((bf16[16,32,1024]{2,1,0:T(8,128)(2,1)}), bf16[16,32,1024]{2,1,0:T(8,128)(2,1)S(1)}, u32[]{:S(2)}, u32[]{:S(2)}) %all-to-all-start.3) | async-done | bytes 1048608 | tf_op jit(solution)/shard_map/all_to_all | solution.py:164
  192.3 36.5 %reduce-scatter.5.cloned.1.call-done = f32[256,2048]{1,0:T(8,128)} async-done(((f32[1024,2048]{1,0:T(8,128)}), f32[256,2048]{1,0:T(8,128)}) %reduce-scatter.5.cloned.1.call-update) | async-done | bytes 2097168
  228.8 1.8 reshape.530
  230.5 1.7 slice_bitcast_fusion
  (161 shorter events, 45.5 us)
Async XLA Ops:
  7.2 12.9 %copy-start = (bf16[16,32,1024]{2,1,0:T(8,128)(2,1)S(1)}, bf16[16,32,1024]{2,1,0:T(8,128)(2,1)}, u32[]{:S(2)}) copy-start(bf16[16,32,1024]{2,1,0:T(8,128)(2,1)} %param.11) | copy-start | bytes 3145732
  7.2 4.0 %copy-start.2 = (s32[16]{0:T(128)S(1)}, s32[16]{0:T(128)}, u32[]{:S(2)}) copy-start(s32[16]{0:T(128)} %param.13) | copy-start | bytes 196
  7.2 82.9 %all-gather.3.cloned.1.call-start = ((), (), s32[]{:S(2)}) async-start(), calls=%async_computation.5 | async-start | bytes 2621440 | tf_op jit(solution)/shard_map/all_gather | solution.py:50
  9.2 11.5 %copy-start.13 = (bf16[16,32,1024]{2,1,0:T(8,128)(2,1)S(1)}, bf16[16,32,1024]{2,1,0:T(8,128)(2,1)}, u32[]{:S(2)}) copy-start(bf16[16,32,1024]{2,1,0:T(8,128)(2,1)} %param.10) | copy-start | bytes 3145732
  12.8 13.7 %all-to-all-start = ((bf16[8,2,2]{1,2,0:T(2,128)(2,1)}), bf16[8,2,2]{1,2,0:T(2,128)(2,1)S(1)}, u32[]{:S(2)}, u32[]{:S(2)}) async-start(bf16[8,2,2]{1,2,0:T(2,128)(2,1)} %copy.19), calls=%async_computation | async-start | bytes 8192 | tf_op jit(solution)/shard_map/all_to_all | solution.py:78
  22.8 7.2 %copy-start.14 = (bf16[256,2,512]{2,1,0:T(2,128)(2,1)S(1)}, bf16[256,2,512]{2,1,0:T(2,128)(2,1)}, u32[]{:S(2)}) copy-start(bf16[256,2,512]{2,1,0:T(2,128)(2,1)} %param.17) | copy-start | bytes 1572868
  22.8 8.2 %copy-start.15 = (bf16[256,2]{0,1:T(2,128)(2,1)S(1)}, bf16[256,2]{0,1:T(2,128)(2,1)}, u32[]{:S(2)}) copy-start(bf16[256,2]{0,1:T(2,128)(2,1)} %param.15) | copy-start | bytes 3076
  26.4 28.3 %all-to-all-start.1 = ((bf16[16,32,1024]{2,1,0:T(8,128)(2,1)}), bf16[16,32,1024]{2,1,0:T(8,128)(2,1)S(1)}, u32[]{:S(2)}, u32[]{:S(2)}) async-start(bf16[16,32,1024]{2,1,0:T(8,128)(2,1)} %get-tuple-element.127), calls=%async_computation.1 | async-start | bytes 2097152 | tf_op jit(solution)/shard_map/all_to_all | solution.py:77
  30.0 60.0 %all-gather.5.cloned.1.call-start = ((), (), s32[]{:S(2)}) async-start(), calls=%async_computation.6 | async-start | bytes 2621440 | tf_op jit(solution)/shard_map/all_gather | solution.py:51
  54.7 29.4 %all-to-all-start.2 = ((bf16[16,32,1024]{2,1,0:T(8,128)(2,1)}), bf16[16,32,1024]{2,1,0:T(8,128)(2,1)S(1)}, u32[]{:S(2)}, u32[]{:S(2)}) async-start(bf16[16,32,1024]{2,1,0:T(8,128)(2,1)} %get-tuple-element.126), calls=%async_computation.2 | async-start | bytes 2097152 | tf_op jit(solution)/shard_map/all_to_all | solution.py:76
  58.3 170.5 %reduce-scatter.5.cloned.1.call-start = ((), (), s32[]{:S(2)}) async-start(), calls=%async_computation.7 | async-start | bytes 10485760
  99.0 3.7 %copy-start.3 = (bf16[2,512,1024]{2,1,0:T(8,128)(2,1)S(1)}, bf16[2,512,1024]{2,1,0:T(8,128)(2,1)}, u32[]{:S(2)}) copy-start(bf16[2,512,1024]{2,1,0:T(8,128)(2,1)} %get-tuple-element.282) | copy-start | bytes 6291460 | tf_op jit(solution)/shard_map/while
  99.0 3.7 %copy-start.17 = (bf16[1024,2,512]{2,0,1:T(8,128)(2,1)S(1)}, bf16[1024,2,512]{2,0,1:T(8,128)(2,1)}, u32[]{:S(2)}) copy-start(bf16[1024,2,512]{2,0,1:T(8,128)(2,1)} %get-tuple-element.287) | copy-start | bytes 6291460 | tf_op jit(solution)/shard_map/while
  99.0 3.7 %copy-start.19 = (bf16[2,512,512]{2,1,0:T(8,128)(2,1)S(1)}, bf16[2,512,512]{2,1,0:T(8,128)(2,1)}, u32[]{:S(2)}) copy-start(bf16[2,512,512]{2,1,0:T(8,128)(2,1)} %get-tuple-element.263) | copy-start | bytes 3145732 | tf_op jit(solution)/shard_map/while
  103.7 2.1 copy-start.4
  103.7 2.7 %copy-start.7 = (bf16[2,512,1024]{2,1,0:T(8,128)(2,1)S(1)}, bf16[2,512,1024]{2,1,0:T(8,128)(2,1)}, u32[]{:S(2)}) copy-start(bf16[2,512,1024]{2,1,0:T(8,128)(2,1)} %get-tuple-element.261) | copy-start | bytes 6291460 | tf_op jit(solution)/shard_map/while
  115.5 3.7 %copy-start.3 = (bf16[2,512,1024]{2,1,0:T(8,128)(2,1)S(1)}, bf16[2,512,1024]{2,1,0:T(8,128)(2,1)}, u32[]{:S(2)}) copy-start(bf16[2,512,1024]{2,1,0:T(8,128)(2,1)} %get-tuple-element.282) | copy-start | bytes 6291460 | tf_op jit(solution)/shard_map/while
  115.5 3.7 %copy-start.17 = (bf16[1024,2,512]{2,0,1:T(8,128)(2,1)S(1)}, bf16[1024,2,512]{2,0,1:T(8,128)(2,1)}, u32[]{:S(2)}) copy-start(bf16[1024,2,512]{2,0,1:T(8,128)(2,1)} %get-tuple-element.287) | copy-start | bytes 6291460 | tf_op jit(solution)/shard_map/while
  115.5 3.7 %copy-start.19 = (bf16[2,512,512]{2,1,0:T(8,128)(2,1)S(1)}, bf16[2,512,512]{2,1,0:T(8,128)(2,1)}, u32[]{:S(2)}) copy-start(bf16[2,512,512]{2,1,0:T(8,128)(2,1)} %get-tuple-element.263) | copy-start | bytes 3145732 | tf_op jit(solution)/shard_map/while
  120.2 2.7 %copy-start.7 = (bf16[2,512,1024]{2,1,0:T(8,128)(2,1)S(1)}, bf16[2,512,1024]{2,1,0:T(8,128)(2,1)}, u32[]{:S(2)}) copy-start(bf16[2,512,1024]{2,1,0:T(8,128)(2,1)} %get-tuple-element.261) | copy-start | bytes 6291460 | tf_op jit(solution)/shard_map/while
  127.8 2.3 copy-start.9
  127.8 2.3 copy-start.21
  161.1 29.6 %all-to-all-start.3 = ((bf16[16,32,1024]{2,1,0:T(8,128)(2,1)}), bf16[16,32,1024]{2,1,0:T(8,128)(2,1)S(1)}, u32[]{:S(2)}, u32[]{:S(2)}) async-start(bf16[16,32,1024]{2,1,0:T(8,128)(2,1)} %broadcast_select_fusion.4), calls=%async_computation.3 | async-start | bytes 2097152 | tf_op jit(solution)/shard_map/all_to_all | solution.py:164
  190.7 41.5 %copy-start.1 = (bf16[16,32,1024]{2,1,0:T(8,128)(2,1)S(1)}, bf16[16,32,1024]{2,1,0:T(8,128)(2,1)}, u32[]{:S(2)}) copy-start(bf16[16,32,1024]{2,1,0:T(8,128)(2,1)} %param.11) | copy-start | bytes 3145732
  (16 other events, 25.8 us)
Sparse Core Ops, SparseCore 0:
  10.2 25.2 all-gather.2
  37.6 22.6 all-gather.4
  158.0 70.7 reduce-scatter.4
where the time goes:
time: 240 us; the launch traced here: 239 us
  waiting for transfers between devices  104 us (43%)
  local copies, waits for them, and re-layouts  56.2 us (23%)
  other arithmetic  21.2 us (9%)
  starting transfers between devices  18.1 us (8%)
  matrix products  15.8 us (7%)
  between operations  14 us (6%)
  blocking collectives  5.06 us (2%)
  loops' own time  4.12 us (2%)
    unnamed x4, waiting for transfers between devices  36.5 us
    all_to_all x1, waiting for transfers between devices, shards(): lax.all_to_all(grad_recv, 'dp', split_axis=0, concat_axis=0, tiled=True)  25.9 us
    unnamed x27, local copies, waits for them, and re-layouts  25 us
    all_to_all x1, waiting for transfers between devices, shards(): lax.all_to_all(send_x, 'dp', split_axis=0, concat_axis=0, tiled=True)  20.2 us
    all_to_all x1, waiting for transfers between devices, shards(): lax.all_to_all(send_dy, 'dp', split_axis=0, concat_axis=0, tiled=True)  18 us
    while x44, local copies, waits for them, and re-layouts  12 us
    dot_general x2, matrix products, adapter_backward(): inner = jnp.dot(normed, down_cols, preferred_element_type=jnp.float32)  7.31 us
    all_to_all x1, starting transfers between devices, shards(): lax.all_to_all(slot_meta, 'dp', split_axis=0, concat_axis=0, tiled=True)  7.28 us
  transfers between devices with their start and end apart: 7, of which 5 were waited for; matrix products, arithmetic and copies ran while one was open for 9% of the time, Pallas kernels for 0%

commit v1 on v0

v1 whole, which is shorter than its diff:
```python
import functools
import math

import jax
import jax.numpy as jnp
from jax import lax
from jax.experimental import pallas as pl
from jax.experimental.pallas import tpu as pltpu
from jax.sharding import PartitionSpec as P

SLAB = 16
LANES = 128
VMEM_LIMIT = 48 * 1024 * 1024


def pack_kernel(
    dims, lang_ref, count_ref, slot_ref, mp_ref, x_hbm, dy_hbm, out_ref, dest_ref, dy_buf, source_ref, taken_ref, sems
):
    dp_size, capacity, lang_local, full = dims
    block_count, block_rows, features = x_hbm.shape
    slots = dp_size * capacity
    halves = block_rows // SLAB

    def clear_owner(owner, carry):
        taken_ref[owner] = 0
        return carry

    def clear_slot(slot, carry):
        source_ref[slot] = -1
        return carry

    lax.fori_loop(0, dp_size, clear_owner, 0)
    if not full:
        lax.fori_loop(0, slots, clear_slot, 0)

    def place(block, carry):
        owner = slot_ref[lang_ref[block]] // lang_local
        rank = taken_ref[owner]
        taken_ref[owner] = rank + 1
        dest = owner * capacity + rank
        dest_ref[block] = dest
        source_ref[dest] = block
        return carry

    lax.fori_loop(0, block_count, place, 0, unroll=True)

    def copies(slot):
        peer, place_in = slot // capacity, slot % capacity
        block = source_ref[slot]
        block = block if full else jnp.maximum(block, 0)
        result = [pltpu.make_async_copy(dy_hbm.at[block], dy_buf.at[slot], sems.at[0, slot])]
        for half in range(halves):
            group = place_in * halves + half
            result.append(
                pltpu.make_async_copy(
                    x_hbm.at[block, pl.ds(half * SLAB, SLAB)],
                    out_ref.at[peer, :, pl.ds(group * features, features)],
                    sems.at[1 + half, slot],
                )
            )
        return result

    for slot in range(slots):
        if full:
            for copy in copies(slot):
                copy.start()
        else:

            @pl.when(source_ref[slot] >= 0)
            def _():
                for copy in copies(slot):
                    copy.start()

    row_start = mp_ref[0] * block_rows
    dy_groups = capacity * halves
    for slot in range(slots):
        peer, place_in = slot // capacity, slot % capacity

        def finish(slot=slot, peer=peer, place_in=place_in):
            for copy in copies(slot):
                copy.wait()
            block = source_ref[slot]
            live = count_ref[block] - row_start
            for half in range(halves):
                rows = lax.broadcasted_iota(jnp.int32, (SLAB, features), 0) + half * SLAB
                piece = dy_buf[slot, pl.ds(half * SLAB, SLAB), :].astype(jnp.float32)
                group = dy_groups + place_in * halves + half
                out_ref[peer, :, pl.ds(group * features, features)] = jnp.where(rows < live, piece, 0.0).astype(
                    out_ref.dtype
                )

        def blank(peer=peer, place_in=place_in):
            for half in range(halves):
                for base in (0, dy_groups):
                    group = base + place_in * halves + half
                    out_ref[peer, :, pl.ds(group * features, features)] = jnp.zeros((SLAB, features), out_ref.dtype)

        if full:
            finish()
        else:
            pl.when(source_ref[slot] >= 0)(finish)
            pl.when(source_ref[slot] < 0)(blank)

    lane = lax.broadcasted_iota(jnp.int32, (SLAB, LANES), 1)
    for peer in range(dp_size):
        tags = jnp.zeros((SLAB, LANES), jnp.int32)
        for place_in in range(capacity):
            block = source_ref[peer * capacity + place_in]
            safe = block if full else jnp.maximum(block, 0)
            local = slot_ref[lang_ref[safe]] % lang_local
            tags = jnp.where(lane // (LANES // capacity) == place_in, local, tags)
        out_ref[peer, :, pl.ds(2 * dy_groups * features, LANES)] = tags.astype(jnp.float32).astype(out_ref.dtype)


def load_all(dims, mp_ref, recv_hbm, weight_hbms, x_buf, dy_buf, tag_buf, down_buf, up_buf, gain_buf, sems):
    groups, features, shard_rows = dims
    copies = []
    for group in range(groups):
        for base, buf in ((0, x_buf), (groups, dy_buf)):
            copies.append(
                (recv_hbm.at[:, :, pl.ds((base + group) * features, features)], buf.at[:, group])
            )
    copies.append((recv_hbm.at[:, :, pl.ds(2 * groups * features, LANES)], tag_buf))
    for offset, weight in enumerate(weight_hbms):
        rows = pl.ds(pl.multiple_of((mp_ref[0] ^ offset) * shard_rows, shard_rows), shard_rows)
        copies.append((weight.at[pl.ds(0, shard_rows)], down_buf.at[rows]))
        if up_buf is not None:
            copies.append((weight.at[pl.ds(shard_rows, shard_rows)], up_buf.at[rows]))
        copies.append((weight.at[pl.ds(2 * shard_rows, SLAB)], gain_buf.at[offset]))
    started = [pltpu.make_async_copy(src, dst, sems.at[n]) for n, (src, dst) in enumerate(copies)]
    for copy in started:
        copy.start()
    for copy in started:
        copy.wait()


def gain_rows(gain_buf):
    total = gain_buf[0].astype(jnp.float32)
    for offset in range(1, gain_buf.shape[0]):
        total = total + gain_buf[offset].astype(jnp.float32)
    return total[0:1, :], total[1:2, :]


def main_kernel(
    dims,
    mp_ref,
    recv_hbm,
    *refs,
):
    capacity, tile, mp_size, scale = dims
    weight_hbms = refs[:mp_size]
    (tg_ref, send_ref, keep_ref) = refs[mp_size : mp_size + 3]
    (x_buf, dy_buf, tag_buf, down_buf, up_buf, gain_buf, id_buf, normed_buf, act_buf, inner_buf, sems) = refs[
        mp_size + 3 :
    ]
    dp_size, groups, _, features = x_buf.shape
    width = down_buf.shape[1]
    half_width = width // 2
    rows = dp_size * groups * SLAB
    shard = features // mp_size
    load_all(
        (groups, features, shard), mp_ref, recv_hbm, weight_hbms, x_buf, dy_buf, tag_buf, down_buf, up_buf, gain_buf, sems
    )
    per_block = groups // capacity
    for peer in range(dp_size):
        for group in range(groups):
            place_in = group // per_block
            column = place_in * (LANES // capacity)
            tag = tag_buf[peer, :, column : column + 1].astype(jnp.float32)
            start = (peer * groups + group) * SLAB
            id_buf[pl.ds(start, SLAB), :] = jnp.broadcast_to(tag, (SLAB, LANES))
    gain_a, gain_b = gain_rows(gain_buf)
    peers_tile = tile // (groups * SLAB)

    def one_tile(step, carry):
        first = pl.multiple_of(step * tile, tile)
        peers = pl.ds(step * peers_tile, peers_tile)
        values = x_buf[peers].reshape(tile, features).astype(jnp.float32)
        masked = dy_buf[peers].reshape(tile, features)
        tags = id_buf[pl.ds(first, tile), :]
        second = tags[:, :1] > 0.5
        row_mean = jnp.mean(values, axis=-1, keepdims=True)
        centered = values - row_mean
        inv_std = lax.rsqrt(jnp.mean(centered * centered, axis=-1, keepdims=True) + 1e-05)
        unit = centered * inv_std
        gain = jnp.where(second, gain_b, gain_a)
        normed = (unit * gain).astype(jnp.bfloat16)
        normed_buf[pl.ds(first, tile), :] = normed
        inner_both = jnp.dot(normed, down_buf[...], preferred_element_type=jnp.float32)
        inner = jnp.where(second, inner_both[:, half_width:], inner_both[:, :half_width])
        bell = 0.5 * (1.0 + lax.erf(inner * (1.0 / math.sqrt(2.0))))
        act = inner * bell
        slope = bell + inner * jnp.exp(-0.5 * inner * inner) * (1.0 / math.sqrt(2.0 * math.pi))
        grad_act_both = jnp.dot(masked, up_buf[...], preferred_element_type=jnp.float32)
        grad_act = jnp.where(second, grad_act_both[:, half_width:], grad_act_both[:, :half_width])
        grad_inner = grad_act * slope
        act_buf[pl.ds(first, tile), :] = jnp.concatenate(
            [jnp.where(second, 0.0, act), jnp.where(second, act, 0.0)], axis=1
        ).astype(jnp.bfloat16)
        spread = jnp.concatenate(
            [jnp.where(second, 0.0, grad_inner), jnp.where(second, grad_inner, 0.0)], axis=1
        ).astype(jnp.bfloat16)
        inner_buf[pl.ds(first, tile), :] = spread
        grad_normed = lax.dot_general(
            spread, down_buf[...], (((1,), (1,)), ((), ())), preferred_element_type=jnp.float32
        )
        scaled = grad_normed * gain
        token_grad = masked.astype(jnp.float32) + inv_std * (
            scaled
            - jnp.mean(scaled, axis=-1, keepdims=True)
            - unit * jnp.mean(scaled * unit, axis=-1, keepdims=True)
        )
        tg_ref[pl.ds(first, tile), :] = token_grad.astype(jnp.bfloat16)
        return carry

    lax.fori_loop(0, rows // tile, one_tile, 0)

    for offset in range(mp_size):
        lanes = pl.ds(pl.multiple_of((mp_ref[0] ^ offset) * shard, shard), shard)
        out = send_ref if offset % 2 else keep_ref
        masked = dy_buf[:, :, :, lanes].reshape(rows, shard)
        up_part = lax.dot_general(
            masked, act_buf[...], (((0,), (0,)), ((), ())), preferred_element_type=jnp.float32
        )
        out[offset // 2, pl.ds(0, shard), :] = (up_part * scale).astype(jnp.bfloat16)
        down_part = lax.dot_general(
            normed_buf[:, lanes], inner_buf[...], (((0,), (0,)), ((), ())), preferred_element_type=jnp.float32
        )
        out[offset // 2, pl.ds(shard, shard), :] = (down_part * scale).astype(jnp.bfloat16)


def unpack_kernel(dest_ref, back_hbm, out_hbm, sems):
    block_count = out_hbm.shape[0]
    copies = [
        pltpu.make_async_copy(back_hbm.at[dest_ref[block]], out_hbm.at[block], sems.at[block])
        for block in range(block_count)
    ]
    for copy in copies:
        copy.start()
    for copy in copies:
        copy.wait()


def shards(tokens, cotangent, block_lang, counts, slot_of, ln_gain, w_down, w_up):
    block_count, block_rows, features = tokens.shape
    dp_size = lax.axis_size("dp")
    mp_size = lax.axis_size("mp")
    lang_local, bottleneck = w_down.shape[1:]
    shard = w_down.shape[0]
    width = lang_local * bottleneck
    capacity = (block_count + dp_size - 1) // dp_size
    slots = dp_size * capacity
    halves = block_rows // SLAB
    groups = capacity * halves
    packed_lanes = 2 * groups * features + LANES
    mp_index = lax.axis_index("mp").astype(jnp.int32)[None]
    smem = pl.BlockSpec(memory_space=pltpu.SMEM)
    vmem = pl.BlockSpec(memory_space=pltpu.VMEM)
    anywhere = pl.BlockSpec(memory_space=pl.ANY)
    params = pltpu.CompilerParams(vmem_limit_bytes=VMEM_LIMIT)

    send, dest = pl.pallas_call(
        functools.partial(pack_kernel, (dp_size, capacity, lang_local, slots == block_count)),
        out_shape=(
            jax.ShapeDtypeStruct((dp_size, SLAB, packed_lanes), jnp.bfloat16),
            jax.ShapeDtypeStruct((block_count,), jnp.int32),
        ),
        in_specs=[smem, smem, smem, smem, anywhere, anywhere],
        out_specs=(vmem, smem),
        scratch_shapes=[
            pltpu.VMEM((slots, block_rows, features), jnp.bfloat16),
            pltpu.SMEM((slots,), jnp.int32),
            pltpu.SMEM((dp_size,), jnp.int32),
            pltpu.SemaphoreType.DMA((1 + halves, slots)),
        ],
        compiler_params=params,
        name="pack",
    )(block_lang, counts, slot_of, mp_index, tokens, cotangent)
    recv = lax.all_to_all(send, "dp", split_axis=0, concat_axis=0, tiled=True)

    gain_part = lax.dynamic_update_slice(
        jnp.zeros((SLAB, features), jnp.bfloat16), ln_gain.T, (0, mp_index[0] * shard)
    )
    own = jnp.concatenate([w_down.reshape(shard, width), w_up.reshape(shard, width), gain_part], axis=0)

    def swap(array, bit):
        return lax.ppermute(array, "mp", [(i, i ^ bit) for i in range(mp_size)])

    across = swap(own, 2)
    weights = [own, swap(own, 1), across, swap(across, 1)]

    rows = slots * block_rows
    tile = min(128, rows)
    bf = jnp.bfloat16
    token_part, send_grad, keep_grad = pl.pallas_call(
        functools.partial(main_kernel, (capacity, tile, mp_size, 1.0 / (block_rows * mp_size))),
        out_shape=(
            jax.ShapeDtypeStruct((rows, features), bf),
            jax.ShapeDtypeStruct((mp_size // 2, 2 * shard, width), bf),
            jax.ShapeDtypeStruct((mp_size // 2, 2 * shard, width), bf),
        ),
        in_specs=[smem, anywhere] + [anywhere] * mp_size,
        out_specs=(vmem, vmem, vmem),
        scratch_shapes=[
            pltpu.VMEM((dp_size, groups, SLAB, features), bf),
            pltpu.VMEM((dp_size, groups, SLAB, features), bf),
            pltpu.VMEM((dp_size, SLAB, LANES), bf),
            pltpu.VMEM((features, width), bf),
            pltpu.VMEM((features, width), bf),
            pltpu.VMEM((mp_size, SLAB, features), bf),
            pltpu.VMEM((rows, LANES), jnp.float32),
            pltpu.VMEM((rows, features), bf),
            pltpu.VMEM((rows, width), bf),
            pltpu.VMEM((rows, width), bf),
            pltpu.SemaphoreType.DMA((2 * groups + 1 + 3 * mp_size,)),
        ],
        compiler_params=params,
        name="adapter",
    )(mp_index, recv, *weights)

    back = lax.all_to_all(
        token_part.reshape(slots, block_rows, features), "dp", split_axis=0, concat_axis=0, tiled=True
    )
    near = swap(send_grad, 1)
    pair = keep_grad.astype(jnp.float32) + near.astype(jnp.float32)
    far = swap(pair[1].astype(bf), 2)
    total = (pair[0] + far.astype(jnp.float32)).astype(bf)
    grad_up = total[:shard].reshape(shard, lang_local, bottleneck)
    grad_down = total[shard:].reshape(shard, lang_local, bottleneck)
    token_grad = pl.pallas_call(
        unpack_kernel,
        out_shape=jax.ShapeDtypeStruct(tokens.shape, bf),
        in_specs=[smem, anywhere],
        out_specs=anywhere,
        scratch_shapes=[pltpu.SemaphoreType.DMA((block_count,))],
        name="unpack",
    )(dest, back)
    return (token_grad, grad_down, grad_up)


def solution(mesh):
    placed = (
        P("dp", "mp", None),
        P("dp", "mp", None),
        P("dp"),
        P("dp"),
        P(),
        P("mp", "dp"),
        P("mp", "dp", None),
        P("mp", "dp", None),
    )
    return jax.shard_map(
        shards,
        mesh=mesh,
        in_specs=placed,
        out_specs=(P("dp", "mp", None), P("mp", "dp", None), P("mp", "dp", None)),
        check_vma=False,
    )
```

time: 240 us -> 152 us (0.63)
  Pallas kernels: 0 us -> 51.9 us
  local copies, waits for them, and re-layouts: 56.2 us -> 14.3 us
  waiting for transfers between devices: 104 us -> 66 us
  other arithmetic: 21.2 us -> 4.49 us
  matrix products: 15.8 us -> 0 us
  between operations: 14 us -> 0.79 us
  blocking collectives: 5.06 us -> 0 us
  loops' own time: 4.12 us -> 0 us
  starting transfers between devices: 18.1 us -> 14.3 us
    pallas_call x0 -> x3, Pallas kernels: none -> 51.9 us  [the longest x1 33.7 us: shards(): pl.pallas_call(unpack_kernel, out_shape=jax.ShapeDtypeStruct(tokens.shape...]
    unnamed x4 -> x0, waiting for transfers between devices: 36.5 us -> none
    all_to_all x4 -> x2, waiting for transfers between devices: 67.7 us -> 38.7 us  [the longest x1 19.6 us: shards(): lax.all_to_all(token_part.reshape(slots, block_rows, features), 'dp', spl...]
    ppermute x0 -> x5, waiting for transfers between devices: none -> 27.3 us  [swap(): return lax.ppermute(array, 'mp', [(i, i ^ bit) for i in range(mp_size)])]
    dot_general x10 -> x0, matrix products: 15.8 us -> none  [the longest x2 7.31 us: adapter_backward(): inner = jnp.dot(normed, down_cols, preferred_element_type=jnp.float32)]
    unnamed x27 -> x32, local copies, waits for them, and re-layouts: 25 us -> 11.7 us
    while x44 -> x0, local copies, waits for them, and re-layouts: 12 us -> none
    gather x10 -> x0, local copies, waits for them, and re-layouts: 9.57 us -> none  [the longest x1 2.03 us: shards(): buf_x = jnp.where(buf_has[:, None, None], recv_x[buf_source], bf_zero)]
  transfers between devices with their start and end apart: 7 -> 7, of which waited for: 5 -> 5; matrix products, arithmetic and copies ran while one was open for 9% -> 2% of each run, Pallas kernels for 0% -> 22%
where the time goes in v1:
time: 152 us
  waiting for transfers between devices  66 us (43%)
  Pallas kernels  51.9 us (34%)
  local copies, waits for them, and re-layouts  14.3 us (9%)
  starting transfers between devices  14.3 us (9%)
  other arithmetic  4.49 us (3%)
    pallas_call x1, Pallas kernels, shards(): pl.pallas_call(unpack_kernel, out_shape=jax.ShapeDtypeStruct(tokens.shape...  33.7 us
    ppermute x5, waiting for transfers between devices, swap(): return lax.ppermute(array, 'mp', [(i, i ^ bit) for i in range(mp_size)])  27.3 us
    all_to_all x1, waiting for transfers between devices, shards(): lax.all_to_all(token_part.reshape(slots, block_rows, features), 'dp', spl...  19.6 us
    all_to_all x1, waiting for transfers between devices, shards(): recv = lax.all_to_all(send, 'dp', split_axis=0, concat_axis=0, tiled=True)  19.2 us
    pallas_call x1, Pallas kernels, shards(): pl.pallas_call(functools.partial(main_kernel, (capacity, tile, mp_size, 1...  13.3 us
    unnamed x32, local copies, waits for them, and re-layouts  11.7 us
    all_to_all x1, starting transfers between devices, shards(): recv = lax.all_to_all(send, 'dp', split_axis=0, concat_axis=0, tiled=True)  7.41 us
    pallas_call x1, Pallas kernels, shards(): pl.pallas_call(functools.partial(pack_kernel, (dp_size, capacity, lang_lo...  4.93 us
  transfers between devices with their start and end apart: 7, of which 5 were waited for; matrix products, arithmetic and copies ran while one was open for 2% of the time, Pallas kernels for 22%

profile of v1, /device:TPU:0, one launch (start us, length us, event | category | flops | bytes accessed | tf_op | source)
XLA Modules:
  0.0 151.8 jit_solution(3857969743523278649)
XLA Ops:
  0.6 1.2 copy-done.2
  1.9 1.2 copy-done.3
  3.1 0.7 copy-done.5
  5.1 4.9 %pack.1 = (bf16[8,16,8320]{2,1,0:T(8,128)(2,1)}, s32[16]{0:T(128)S(1)}) custom-call(s32[16]{0:T(128)S(1)} %copy-done.5, s32[16]{0:T(128)S(1)} %copy-done.6, s32[16]{0:T(128)S(1)} %copy-done.7, s32[1]{0:T(128)} %bitcast.mp_ref, bf16[16,32,1024]{2,1,0:T(8,128)(2,1)S(1)} %copy-done.2, bf16[16,32,1024]{2,1,0:T(8,128)(2,1)S(1)} %copy-done.3), custom_call_target="tpu_custom_call" | custom-call | tf_op jit(solution)/shard_map/pack/pallas_call | solution.py:262
  10.5 7.4 %all-to-all-start = ((bf16[8,16,8320]{2,1,0:T(8,128)(2,1)}), bf16[8,16,8320]{2,1,0:T(8,128)(2,1)}, u32[]{:S(2)}, u32[]{:S(2)}) async-start(bf16[8,16,8320]{2,1,0:T(8,128)(2,1)} %get-tuple-element.9), calls=%async_computation | async-start | bytes 4259840 | tf_op jit(solution)/shard_map/all_to_all | solution.py:279
  18.7 1.6 %collective-permute-start.1 = (bf16[528,1024]{1,0:T(8,128)(2,1)S(1)}, bf16[528,1024]{1,0:T(8,128)(2,1)S(1)}, u32[]{:S(2)}, u32[]{:S(2)}) collective-permute-start(bf16[528,1024]{1,0:T(8,128)(2,1)S(1)} %pad_maximum_fusion.refs_0_), channel_id=1, source_target_pairs={{0,2},{1,3},{2,0},{3,1},{4,6},{5,7},{6,4},{7,5},{8,10},{9,11},{10,... | collective-permute-start | bytes 3244040 | tf_op jit(solution)/shard_map/ppermute | solution.py:287
  20.2 23.8 %collective-permute-done.1.refs_2_ = bf16[528,1024]{1,0:T(8,128)(2,1)S(1)} collective-permute-done((bf16[528,1024]{1,0:T(8,128)(2,1)S(1)}, bf16[528,1024]{1,0:T(8,128)(2,1)S(1)}, u32[]{:S(2)}, u32[]{:S(2)}) %collective-permute-start.1) | collective-permute-done | bytes 1081376 | tf_op jit(solution)/shard_map/ppermute | solution.py:287
  44.1 2.7 %collective-permute-done.2.refs_3_ = bf16[528,1024]{1,0:T(8,128)(2,1)S(1)} collective-permute-done((bf16[528,1024]{1,0:T(8,128)(2,1)S(1)}, bf16[528,1024]{1,0:T(8,128)(2,1)S(1)}, u32[]{:S(2)}, u32[]{:S(2)}) %collective-permute-start.2) | collective-permute-done | bytes 1081376 | tf_op jit(solution)/shard_map/ppermute | solution.py:287
  46.8 1.0 copy-done
  47.8 19.2 %all-to-all-done.recv_hbm = bf16[8,16,8320]{2,1,0:T(8,128)(2,1)} async-done(((bf16[8,16,8320]{2,1,0:T(8,128)(2,1)}), bf16[8,16,8320]{2,1,0:T(8,128)(2,1)}, u32[]{:S(2)}, u32[]{:S(2)}) %all-to-all-start) | async-done | bytes 2129952 | tf_op jit(solution)/shard_map/all_to_all | solution.py:279
  67.0 1.2 copy-done.1
  68.2 13.3 %adapter.1 = (bf16[512,1024]{1,0:T(8,128)(2,1)S(1)}, bf16[2,512,1024]{2,1,0:T(8,128)(2,1)}, bf16[2,512,1024]{2,1,0:T(8,128)(2,1)}) custom-call(s32[1]{0:T(128)} %bitcast.mp_ref, bf16[8,16,8320]{2,1,0:T(8,128)(2,1)} %all-to-all-done.recv_hbm, bf16[528,1024]{1,0:T(8,128)(2,1)S(1)} %pad_maximum_fusion.refs_0_, ...), custom_call_target="tpu_custom_call" | custom-call | tf_op jit(solution)/shard_map/adapter/pallas_call | solution.py:295
  81.6 1.0 copy-done.4
  82.5 3.8 %all-to-all-start.1 = ((bf16[16,32,1024]{2,1,0:T(8,128)(2,1)}), bf16[16,32,1024]{2,1,0:T(8,128)(2,1)S(1)}, u32[]{:S(2)}, u32[]{:S(2)}) async-start(bf16[16,32,1024]{2,1,0:T(8,128)(2,1)} %bitcast.16), calls=%async_computation.1 | async-start | bytes 2097152 | tf_op jit(solution)/shard_map/all_to_all | solution.py:321
  86.3 0.7 collective-permute-done.3
  87.0 2.5 %convert_add_fusion = f32[2,512,1024]{2,1,0:T(8,128)S(1)} fusion(bf16[2,512,1024]{2,1,0:T(8,128)(2,1)} %collective-permute-done.3, bf16[2,512,1024]{2,1,0:T(8,128)(2,1)S(1)} %copy-done.11), kind=kLoop, calls=%fused_computation | loop fusion | flops 3145728 | bytes 8388608 | tf_op jit(solution)/shard_map/add | solution.py:325
  89.5 1.9 %copy-done.9 = f32[2,512,1024]{2,1,0:T(8,128)} copy-done((f32[2,512,1024]{2,1,0:T(8,128)}, f32[2,512,1024]{2,1,0:T(8,128)S(1)}, u32[]{:S(2)}) %copy-start.9) | copy-done | bytes 4194328
  91.6 1.5 %collective-permute-start.4 = (bf16[512,1024]{1,0:T(8,128)(2,1)S(1)}, bf16[512,1024]{1,0:T(8,128)(2,1)S(1)}, u32[]{:S(2)}, u32[]{:S(2)}) collective-permute-start(bf16[512,1024]{1,0:T(8,128)(2,1)S(1)} %fusion.2), channel_id=1, source_target_pairs={{0,2},{1,3},{2,0},{3,1},{4,6},{5,7},{6,4},{7,5},{8,10},{9,11},{10,... | collective-permute-start | bytes 3145736 | tf_op jit(solution)/shard_map/ppermute | solution.py:287
  93.2 19.6 %all-to-all-done.1.back_hbm = bf16[16,32,1024]{2,1,0:T(8,128)(2,1)S(1)} async-done(((bf16[16,32,1024]{2,1,0:T(8,128)(2,1)}), bf16[16,32,1024]{2,1,0:T(8,128)(2,1)S(1)}, u32[]{:S(2)}, u32[]{:S(2)}) %all-to-all-start.1) | async-done | bytes 1048608 | tf_op jit(solution)/shard_map/all_to_all | solution.py:321
  112.7 1.0 copy-done.10
  113.7 33.7 %unpack.1 = bf16[16,32,1024]{2,1,0:T(8,128)(2,1)} custom-call(s32[16]{0:T(128)} %copy-done.8, bf16[16,32,1024]{2,1,0:T(8,128)(2,1)} %copy-done.10), custom_call_target="tpu_custom_call" | custom-call | tf_op jit(solution)/shard_map/unpack/pallas_call | solution.py:330
  147.4 1.9 %fusion.1 = bf16[512,1024]{1,0:T(8,128)(2,1)S(1)} fusion(f32[2,512,1024]{2,1,0:T(8,128)} %copy-done.9, bf16[512,1024]{1,0:T(8,128)(2,1)S(1)} %collective-permute-done.4), kind=kLoop, calls=%fused_computation.4 | loop fusion | flops 1572864 | bytes 4194304 | tf_op jit(solution)/shard_map/convert_element_type | solution.py:327
  149.5 1.2 reshape.26
  150.6 1.2 reshape.25
  (34 shorter events, 2.8 us)
Async XLA Ops:
  0.6 1.2 copy-start.2
  1.9 1.2 copy-start.3
  3.1 0.7 copy-start.5
  3.7 0.7 copy-start.6
  4.4 0.7 copy-start.7
  10.0 0.5 copy-start.8
  10.5 7.4 %copy-start.12 = (bf16[256,2,512]{2,1,0:T(2,128)(2,1)S(1)}, bf16[256,2,512]{2,1,0:T(2,128)(2,1)}, u32[]{:S(2)}) copy-start(bf16[256,2,512]{2,1,0:T(2,128)(2,1)} %param.14) | copy-start | bytes 1572868
  10.5 7.5 %copy-start.13 = (bf16[256,2,512]{2,1,0:T(2,128)(2,1)S(1)}, bf16[256,2,512]{2,1,0:T(2,128)(2,1)}, u32[]{:S(2)}) copy-start(bf16[256,2,512]{2,1,0:T(2,128)(2,1)} %param.15) | copy-start | bytes 1572868
  10.5 56.5 %all-to-all-start = ((bf16[8,16,8320]{2,1,0:T(8,128)(2,1)}), bf16[8,16,8320]{2,1,0:T(8,128)(2,1)}, u32[]{:S(2)}, u32[]{:S(2)}) async-start(bf16[8,16,8320]{2,1,0:T(8,128)(2,1)} %get-tuple-element.9), calls=%async_computation | async-start | bytes 4259840 | tf_op jit(solution)/shard_map/all_to_all | solution.py:279
  17.9 0.7 copy-start.14
  18.7 25.4 %collective-permute-start.1 = (bf16[528,1024]{1,0:T(8,128)(2,1)S(1)}, bf16[528,1024]{1,0:T(8,128)(2,1)S(1)}, u32[]{:S(2)}, u32[]{:S(2)}) collective-permute-start(bf16[528,1024]{1,0:T(8,128)(2,1)S(1)} %pad_maximum_fusion.refs_0_), channel_id=1, source_target_pairs={{0,2},{1,3},{2,0},{3,1},{4,6},{5,7},{6,4},{7,5},{8,10},{9,11},{10,... | collective-permute-start | bytes 3244040 | tf_op jit(solution)/shard_map/ppermute | solution.py:287
  20.2 23.8 %collective-permute-start = (bf16[528,1024]{1,0:T(8,128)(2,1)S(1)}, bf16[528,1024]{1,0:T(8,128)(2,1)S(1)}, u32[]{:S(2)}, u32[]{:S(2)}) collective-permute-start(bf16[528,1024]{1,0:T(8,128)(2,1)S(1)} %pad_maximum_fusion.refs_0_), channel_id=1, source_target_pairs={{0,1},{1,0},{2,3},{3,2},{4,5},{5,4},{6,7},{7,6},{8,9},{9,8},{10,11... | collective-permute-start | bytes 3244040 | tf_op jit(solution)/shard_map/ppermute | solution.py:287
  44.1 2.7 %collective-permute-start.2 = (bf16[528,1024]{1,0:T(8,128)(2,1)S(1)}, bf16[528,1024]{1,0:T(8,128)(2,1)S(1)}, u32[]{:S(2)}, u32[]{:S(2)}) collective-permute-start(bf16[528,1024]{1,0:T(8,128)(2,1)S(1)} %collective-permute-done.1.refs_2_), channel_id=1, source_target_pairs={{0,1},{1,0},{2,3},{3,2},{4,5},{5,4},{6,7},{7,6},{8,9},{9,8},{10,11... | collective-permute-start | bytes 3244040 | tf_op jit(solution)/shard_map/ppermute | solution.py:287
  46.8 1.0 copy-start
  67.0 1.2 copy-start.1
  81.6 1.0 copy-start.4
  82.5 4.5 %copy-start.11 = (bf16[2,512,1024]{2,1,0:T(8,128)(2,1)S(1)}, bf16[2,512,1024]{2,1,0:T(8,128)(2,1)}, u32[]{:S(2)}) copy-start(bf16[2,512,1024]{2,1,0:T(8,128)(2,1)} %get-tuple-element.11) | copy-start | bytes 6291460
  82.5 4.5 %collective-permute-start.3 = (bf16[2,512,1024]{2,1,0:T(8,128)(2,1)}, bf16[2,512,1024]{2,1,0:T(8,128)(2,1)}, u32[]{:S(2)}, u32[]{:S(2)}) collective-permute-start(bf16[2,512,1024]{2,1,0:T(8,128)(2,1)} %get-tuple-element.12), channel_id=1, source_target_pairs={{0,1},{1,0},{2,3},{3,2},{4,5},{5,4},{6,7},{7,6},{8,9},{9,8},{10,11... | collective-permute-start | bytes 6291464 | tf_op jit(solution)/shard_map/ppermute | solution.py:287
  82.5 30.2 %all-to-all-start.1 = ((bf16[16,32,1024]{2,1,0:T(8,128)(2,1)}), bf16[16,32,1024]{2,1,0:T(8,128)(2,1)S(1)}, u32[]{:S(2)}, u32[]{:S(2)}) async-start(bf16[16,32,1024]{2,1,0:T(8,128)(2,1)} %bitcast.16), calls=%async_computation.1 | async-start | bytes 2097152 | tf_op jit(solution)/shard_map/all_to_all | solution.py:321
  89.5 1.9 %copy-start.9 = (f32[2,512,1024]{2,1,0:T(8,128)}, f32[2,512,1024]{2,1,0:T(8,128)S(1)}, u32[]{:S(2)}) copy-start(f32[2,512,1024]{2,1,0:T(8,128)S(1)} %convert_add_fusion) | copy-start | bytes 12582916
  91.6 55.8 %collective-permute-start.4 = (bf16[512,1024]{1,0:T(8,128)(2,1)S(1)}, bf16[512,1024]{1,0:T(8,128)(2,1)S(1)}, u32[]{:S(2)}, u32[]{:S(2)}) collective-permute-start(bf16[512,1024]{1,0:T(8,128)(2,1)S(1)} %fusion.2), channel_id=1, source_target_pairs={{0,2},{1,3},{2,0},{3,1},{4,6},{5,7},{6,4},{7,5},{8,10},{9,11},{10,... | collective-permute-start | bytes 3145736 | tf_op jit(solution)/shard_map/ppermute | solution.py:287
  112.7 1.0 copy-start.10

commit v2 on v0

v2 whole, which is shorter than its diff:
```python
import functools
import math

import jax
import jax.numpy as jnp
from jax import lax
from jax.experimental import pallas as pl
from jax.experimental.pallas import tpu as pltpu
from jax.sharding import PartitionSpec as P

SLAB = 16
LANES = 128
MIB = 1024 * 1024
ANYWHERE = pl.BlockSpec(memory_space=pl.ANY)
VMEM = pl.BlockSpec(memory_space=pltpu.VMEM)
SMEM = pl.BlockSpec(memory_space=pltpu.SMEM)


def params(mib):
    return pltpu.CompilerParams(vmem_limit_bytes=min(mib, 60) * MIB)


def start_all(copies):
    for copy in copies:
        copy.start()


def wait_all(copies):
    for copy in copies:
        copy.wait()


def payload_kernel(after_ref, down_ref, up_ref, gain_ref, out_ref):
    shard = down_ref.shape[0]
    for n, ref in enumerate((down_ref, up_ref)):
        values = ref[...]
        out_ref[pl.ds(n * shard, shard), :] = jnp.concatenate(
            [values[:, local, :] for local in range(values.shape[1])], axis=1
        )
    tail = pl.ds(2 * shard, SLAB)
    out_ref[tail, :] = jnp.zeros((SLAB, out_ref.shape[1]), out_ref.dtype)
    lanes = pl.ds(pl.multiple_of(lax.axis_index("mp") * shard, shard), shard)
    gains = gain_ref[...].astype(jnp.float32)
    rows = [gains, jnp.zeros((SLAB - gains.shape[0], shard), jnp.float32)]
    out_ref[tail, lanes] = jnp.concatenate(rows, axis=0).astype(out_ref.dtype)


def pack_kernel(dims, lang_hbm, count_hbm, slot_hbm, x_hbm, dy_hbm, out_hbm, source_ref, *scratch):
    dp_size, capacity, lang_local, full = dims
    block_count, block_rows, features = x_hbm.shape
    slots = dp_size * capacity
    halves = block_rows // SLAB
    packed, x_buf, dy_buf, lang_ref, count_ref, slot_ref, taken_ref, sems, out_sems = scratch
    loads = [
        pltpu.make_async_copy(src, dst, sems.at[n])
        for n, (src, dst) in enumerate(
            (
                (lang_hbm, lang_ref),
                (count_hbm, count_ref),
                (slot_hbm, slot_ref),
                (x_hbm, x_buf),
                (dy_hbm, dy_buf),
            )
        )
    ]
    start_all(loads)

    def clear_owner(owner, carry):
        taken_ref[owner] = 0
        return carry

    def clear_slot(slot, carry):
        source_ref[slot] = -1
        return carry

    lax.fori_loop(0, dp_size, clear_owner, 0, unroll=dp_size <= 8)
    if not full:
        lax.fori_loop(0, slots, clear_slot, 0)
    wait_all(loads[:3])

    def place(block, carry):
        owner = slot_ref[lang_ref[block]] // lang_local
        rank = taken_ref[owner]
        taken_ref[owner] = rank + 1
        source_ref[owner * capacity + rank] = block
        return carry

    lax.fori_loop(0, block_count, place, 0, unroll=True)
    wait_all(loads[3:])
    row_start = lax.axis_index("mp") * block_rows
    dy_groups = capacity * halves
    lane = lax.broadcasted_iota(jnp.int32, (SLAB, LANES), 1)

    def lanes_of(group):
        return pl.ds(group * features, features)

    def fill(peer, place_in):
        block = source_ref[peer * capacity + place_in]
        live = count_ref[block] - row_start
        for half in range(halves):
            here = pl.ds(half * SLAB, SLAB)
            group = place_in * halves + half
            packed[peer, :, lanes_of(group)] = x_buf[block, here, :]
            rows = lax.broadcasted_iota(jnp.int32, (SLAB, features), 0) + half * SLAB
            piece = dy_buf[block, here, :].astype(jnp.float32)
            packed[peer, :, lanes_of(dy_groups + group)] = jnp.where(rows < live, piece, 0.0).astype(jnp.bfloat16)

    def blank(peer, place_in):
        for half in range(halves):
            for base in (0, dy_groups):
                group = base + place_in * halves + half
                packed[peer, :, lanes_of(group)] = jnp.zeros((SLAB, features), jnp.bfloat16)

    def one_peer(peer, carry):
        tags = jnp.zeros((SLAB, LANES), jnp.int32)
        for place_in in range(capacity):
            block = source_ref[peer * capacity + place_in]
            if full:
                fill(peer, place_in)
            else:
                pl.when(block >= 0)(functools.partial(fill, peer, place_in))
                pl.when(block < 0)(functools.partial(blank, peer, place_in))
                block = jnp.maximum(block, 0)
            local = slot_ref[lang_ref[block]] % lang_local
            tags = jnp.where(lane // (LANES // capacity) == place_in, local, tags)
        packed[peer, :, pl.ds(2 * dy_groups * features, LANES)] = tags.astype(jnp.float32).astype(jnp.bfloat16)
        pltpu.make_async_copy(packed.at[peer], out_hbm.at[peer], out_sems.at[peer]).start()
        return carry

    def wait_peer(peer, carry):
        pltpu.make_async_copy(packed.at[peer], out_hbm.at[peer], out_sems.at[peer]).wait()
        return carry

    lax.fori_loop(0, dp_size, one_peer, 0, unroll=dp_size <= 8)
    lax.fori_loop(0, dp_size, wait_peer, 0, unroll=dp_size <= 8)


def spread(values, second):
    return jnp.concatenate([jnp.where(second, 0.0, values), jnp.where(second, values, 0.0)], axis=1).astype(jnp.bfloat16)


def pick(values, second):
    half = values.shape[1] // 2
    return jnp.where(second, values[:, half:], values[:, :half])


def wide(column):
    return jnp.broadcast_to(column, (column.shape[0], LANES))


def gains_of(gain_ref, second):
    return jnp.where(second, gain_ref[1:2, :], gain_ref[0:1, :])


def normalize(values, second, gain_ref):
    values = values.astype(jnp.float32)
    row_mean = jnp.mean(values, axis=-1, keepdims=True)
    centered = values - row_mean
    inv_std = lax.rsqrt(jnp.mean(centered * centered, axis=-1, keepdims=True) + 1e-05)
    normed = (centered * inv_std * gains_of(gain_ref, second)).astype(jnp.bfloat16)
    return row_mean, inv_std, normed


def middle(masked, inner, second, up_ref):
    bell = 0.5 * (1.0 + lax.erf(inner * (1.0 / math.sqrt(2.0))))
    slope = bell + inner * jnp.exp(-0.5 * inner * inner) * (1.0 / math.sqrt(2.0 * math.pi))
    grad_act = pick(jnp.dot(masked, up_ref[...], preferred_element_type=jnp.float32), second)
    return spread(inner * bell, second), spread(grad_act * slope, second)


def backward(values, masked, row_mean, inv_std, second, grad_inner, gain_ref, down_ref):
    grad_normed = lax.dot_general(
        grad_inner, down_ref[...], (((1,), (1,)), ((), ())), preferred_element_type=jnp.float32
    )
    unit = (values.astype(jnp.float32) - row_mean) * inv_std
    scaled = grad_normed * gains_of(gain_ref, second)
    token_grad = masked.astype(jnp.float32) + inv_std * (
        scaled - jnp.mean(scaled, axis=-1, keepdims=True) - unit * jnp.mean(scaled * unit, axis=-1, keepdims=True)
    )
    return token_grad.astype(jnp.bfloat16)


def weight_grad_kernel(dims, recv_hbm, own_hbm, across_hbm, both_hbm, *refs):
    capacity, mp_size, tile, scale = dims
    part_refs, (x_buf, dy_buf, inner_buf, stats_buf, id_buf, down_ref, gain_ref) = refs[:4], refs[4:11]
    raw, up_ref, gain_buf, normed_buf, act_buf, sems, weight_sems = refs[11:]
    chunks, _, lanes = raw.shape
    rows, features = x_buf.shape
    groups = rows // (chunks * SLAB)
    shard = features // mp_size
    size = own_hbm.shape[0]
    split = groups * features

    def recv_copy(n, start, count):
        return pltpu.make_async_copy(
            recv_hbm.at[:, :, pl.ds(start, count)], raw.at[:, :, pl.ds(start, count)], sems.at[n]
        )

    first = [recv_copy(0, 0, split), recv_copy(1, 2 * split, LANES)]
    then, later = [], [recv_copy(2, split, split)]
    for offset, weight in enumerate(
        (own_hbm, both_hbm.at[pl.ds(0, size)], across_hbm, both_hbm.at[pl.ds(size, size)])
    ):
        here = pl.ds(pl.multiple_of((lax.axis_index("mp") ^ offset) * shard, shard), shard)
        for n, (group, src, dst) in enumerate(
            (
                (then, weight.at[pl.ds(0, shard)], down_ref.at[here]),
                (first, weight.at[pl.ds(2 * shard, SLAB)], gain_buf.at[offset]),
                (later, weight.at[pl.ds(shard, shard)], up_ref.at[here]),
            )
        ):
            group.append(pltpu.make_async_copy(src, dst, weight_sems.at[n, offset]))
    start_all(first)
    start_all(then)
    start_all(later)
    wait_all(first)
    gain = gain_buf[0].astype(jnp.float32)
    for offset in range(1, mp_size):
        gain = gain + gain_buf[offset].astype(jnp.float32)
    gain_ref[...] = gain
    tile_chunks = tile // (groups * SLAB)
    per_block = groups // capacity

    def rows_of(step, base):
        return jnp.concatenate(
            [
                raw[step * tile_chunks + chunk, :, pl.ds((base + group) * features, features)]
                for chunk in range(tile_chunks)
                for group in range(groups)
            ],
            axis=0,
        )

    def ids_of(step):
        pieces = []
        for chunk in range(tile_chunks):
            tags = raw[step * tile_chunks + chunk, :, pl.ds(2 * split, LANES)].astype(jnp.float32)
            for group in range(groups):
                column = (group // per_block) * (LANES // capacity)
                pieces.append(wide(tags[:, column : column + 1]))
        return jnp.concatenate(pieces, axis=0)

    whole = rows == tile
    if not whole:
        wait_all(then + later)

    def one_tile(step, carry):
        here = pl.ds(pl.multiple_of(step * tile, tile), tile)
        ids = ids_of(step)
        id_buf[here, :] = ids
        second = ids[:, :1] > 0.5
        values = rows_of(step, 0)
        x_buf[here, :] = values
        row_mean, inv_std, normed = normalize(values, second, gain_ref)
        normed_buf[here, :] = normed
        stats_buf[here, :] = jnp.concatenate([wide(row_mean), wide(inv_std)], axis=1)
        if whole:
            wait_all(then)
        inner = pick(jnp.dot(normed_buf[here, :], down_ref[...], preferred_element_type=jnp.float32), second)
        if whole:
            wait_all(later)
        dy_buf[here, :] = rows_of(step, groups)
        act, grad_inner = middle(dy_buf[here, :], inner, second, up_ref)
        act_buf[here, :] = act
        inner_buf[here, :] = grad_inner
        return carry

    if whole:
        one_tile(0, 0)
    else:
        lax.fori_loop(0, rows // tile, one_tile, 0)
    for kind, (left, right) in enumerate(((dy_buf, act_buf), (normed_buf, inner_buf))):
        for offset in range(mp_size):
            here = pl.ds(pl.multiple_of((lax.axis_index("mp") ^ offset) * shard, shard), shard)
            part = lax.dot_general(
                left[:, here], right[...], (((0,), (0,)), ((), ())), preferred_element_type=jnp.float32
            )
            part_refs[2 * kind + offset % 2][offset // 2] = (part * scale).astype(jnp.bfloat16)


def token_grad_kernel(tile, x_ref, dy_ref, inner_ref, stats_ref, id_ref, down_ref, gain_ref, out_hbm, grad_buf, sems):
    steps = grad_buf.shape[0] // tile

    def copy(step):
        here = pl.ds(pl.multiple_of(step * tile, tile), tile)
        return pltpu.make_async_copy(grad_buf.at[here], out_hbm.at[here], sems.at[step])

    def one_tile(step, carry):
        here = pl.ds(pl.multiple_of(step * tile, tile), tile)
        stats = stats_ref[here, :]
        grad_buf[here, :] = backward(
            x_ref[here, :],
            dy_ref[here, :],
            stats[:, :1],
            stats[:, LANES : LANES + 1],
            id_ref[here, :][:, :1] > 0.5,
            inner_ref[here, :],
            gain_ref,
            down_ref,
        )
        copy(step).start()
        return carry

    def finish(step, carry):
        copy(step).wait()
        return carry

    lax.fori_loop(0, steps, one_tile, 0, unroll=steps <= 2)
    lax.fori_loop(0, steps, finish, 0, unroll=steps <= 2)


def add_kernel(keep_ref, near_ref, *refs):
    out_ref = refs[-1]
    total = keep_ref[1].astype(jnp.float32) + near_ref[1].astype(jnp.float32)
    out_ref[...] = total.astype(out_ref.dtype)


def finish_grad(keep_ref, near_ref, far_ref, out_ref):
    total = keep_ref[0].astype(jnp.float32) + near_ref[0].astype(jnp.float32) + far_ref[...].astype(jnp.float32)
    out_ref[...] = total.reshape(out_ref.shape).astype(out_ref.dtype)


def tail_kernel(full, source_ref, back_hbm, keep_hbm, near_hbm, far_hbm, out_hbm, grad_ref, buf, *scratch):
    sums, (sum_sems, in_sems, out_sems) = scratch[:3], scratch[3:]
    slots = back_hbm.shape[0]
    terms = [
        pltpu.make_async_copy(src, dst, sum_sems.at[n])
        for n, (src, dst) in enumerate(zip((keep_hbm.at[0], near_hbm.at[0], far_hbm), sums))
    ]

    def load(slot):
        return pltpu.make_async_copy(back_hbm.at[slot], buf.at[slot], in_sems.at[slot])

    def store(slot, do):
        block = source_ref[slot]
        copy = pltpu.make_async_copy(
            buf.at[slot], out_hbm.at[block if full else jnp.maximum(block, 0)], out_sems.at[slot]
        )
        if full:
            getattr(copy, do)()
        else:
            pl.when(block >= 0)(getattr(copy, do))

    start_all([load(slot) for slot in range(slots)])
    start_all(terms)
    for slot in range(slots):
        load(slot).wait()
        store(slot, "start")
    wait_all(terms)
    total = sums[0][...].astype(jnp.float32) + sums[1][...].astype(jnp.float32) + sums[2][...].astype(jnp.float32)
    grad_ref[...] = total.reshape(grad_ref.shape).astype(grad_ref.dtype)
    for slot in range(slots):
        store(slot, "wait")


def shards(tokens, cotangent, block_lang, counts, slot_of, ln_gain, w_down, w_up):
    block_count, block_rows, features = tokens.shape
    dp_size = lax.axis_size("dp")
    mp_size = lax.axis_size("mp")
    lang_local, bottleneck = w_down.shape[1:]
    shard = w_down.shape[0]
    width = lang_local * bottleneck
    capacity = (block_count + dp_size - 1) // dp_size
    slots = dp_size * capacity
    full = slots == block_count
    halves = block_rows // SLAB
    groups = capacity * halves
    lanes = 2 * groups * features + LANES
    rows = slots * block_rows
    tile = min(512, rows)
    resident = rows <= tile
    bf = jnp.bfloat16

    def shape(*extent, kind=bf):
        return jax.ShapeDtypeStruct(extent, kind)

    def vmem_shape(*extent, kind=bf):
        return pltpu.VMEM(extent, kind) if resident else shape(*extent, kind=kind)

    def in_vmem(*arrays):
        return [pltpu.with_memory_space_constraint(array, pltpu.VMEM) if resident else array for array in arrays]

    def in_hbm(*arrays):
        return [pltpu.with_memory_space_constraint(array, pltpu.HBM) for array in arrays]

    def swap(array, bit):
        return lax.ppermute(array, "mp", [(i, i ^ bit) for i in range(mp_size)])

    def exchange(array):
        return lax.all_to_all(array, "dp", split_axis=0, concat_axis=0, tiled=True)

    packed, source = pl.pallas_call(
        functools.partial(pack_kernel, (dp_size, capacity, lang_local, full)),
        out_shape=(pltpu.HBM((dp_size, SLAB, lanes), bf), shape(slots, kind=jnp.int32)),
        in_specs=[ANYWHERE] * 5,
        out_specs=(ANYWHERE, SMEM),
        scratch_shapes=[
            pltpu.VMEM((dp_size, SLAB, lanes), bf),
            pltpu.VMEM(tokens.shape, bf),
            pltpu.VMEM(cotangent.shape, bf),
            pltpu.SMEM(block_lang.shape, jnp.int32),
            pltpu.SMEM(counts.shape, jnp.int32),
            pltpu.SMEM(slot_of.shape, jnp.int32),
            pltpu.SMEM((dp_size,), jnp.int32),
            pltpu.SemaphoreType.DMA((5,)),
            pltpu.SemaphoreType.DMA((dp_size,)),
        ],
        compiler_params=params(8 + slots // 4),
        name="pack",
    )(*in_hbm(block_lang, counts, slot_of, tokens, cotangent))
    recv = exchange(packed)

    own = pl.pallas_call(
        payload_kernel,
        out_shape=shape(2 * shard + SLAB, width),
        in_specs=[SMEM] + [VMEM] * 3,
        out_specs=VMEM,
        compiler_params=params(8),
        name="payload",
    )(source, w_down, w_up, ln_gain.T)
    across = swap(own, 2)
    both = swap(jnp.concatenate([own, across], axis=0), 1)
    part = vmem_shape(mp_size // 2, shard, width)
    up_keep, up_send, down_keep, down_send, *kept = pl.pallas_call(
        functools.partial(weight_grad_kernel, (capacity, mp_size, tile, 1.0 / (block_rows * mp_size))),
        out_shape=(
            part,
            part,
            part,
            part,
            vmem_shape(rows, features),
            vmem_shape(rows, features),
            vmem_shape(rows, width),
            vmem_shape(rows, 2 * LANES, kind=jnp.float32),
            vmem_shape(rows, LANES, kind=jnp.float32),
            vmem_shape(features, width),
            vmem_shape(SLAB, features, kind=jnp.float32),
        ),
        in_specs=[ANYWHERE] * 4,
        out_specs=(VMEM,) * 11,
        scratch_shapes=[
            pltpu.VMEM((dp_size, SLAB, lanes), bf),
            pltpu.VMEM((features, width), bf),
            pltpu.VMEM((mp_size, SLAB, features), bf),
            pltpu.VMEM((rows, features), bf),
            pltpu.VMEM((rows, width), bf),
            pltpu.SemaphoreType.DMA((3,)),
            pltpu.SemaphoreType.DMA((3, mp_size)),
        ],
        compiler_params=params(14 + rows // 48),
        name="weight_grads",
    )(*in_hbm(recv, own, across, both))

    tile = min(256, rows)
    token_part = pl.pallas_call(
        functools.partial(token_grad_kernel, tile),
        out_shape=pltpu.HBM((rows, features), bf),
        in_specs=[VMEM] * 7,
        out_specs=ANYWHERE,
        scratch_shapes=[pltpu.VMEM((rows, features), bf), pltpu.SemaphoreType.DMA((rows // tile,))],
        compiler_params=params(4 + rows // 64),
        name="token_grads",
    )(*in_vmem(*kept))

    def reduce_core(keep, send, name, *through):
        near = swap(send, 1)
        *through, partial_sum = pl.pallas_call(
            add_kernel,
            out_shape=(*[pltpu.HBM(array.shape, array.dtype) for array in through], vmem_shape(shard, width)),
            in_specs=[VMEM] * 2 + [ANYWHERE] * len(through),
            out_specs=(*[ANYWHERE] * len(through), VMEM),
            input_output_aliases={2 + n: n for n in range(len(through))},
            compiler_params=params(4),
            name=name + "_add",
        )(*in_vmem(keep, near), *in_hbm(*through))
        return near, partial_sum, *through

    up_near, up_sum, token_part = reduce_core(up_keep, up_send, "up", token_part)
    down_near, down_sum = reduce_core(down_keep, down_send, "down")
    up_far, down_far = swap(up_sum, 2), swap(down_sum, 2)
    back = exchange(token_part.reshape(slots, block_rows, features))
    grad_shape = shape(shard, lang_local, bottleneck)
    grad_up = pl.pallas_call(
        finish_grad,
        out_shape=grad_shape,
        in_specs=[VMEM] * 3,
        out_specs=VMEM,
        compiler_params=params(8),
        name="up_finish",
    )(*in_hbm(up_keep, up_near, up_far))
    token_grad, grad_down = pl.pallas_call(
        functools.partial(tail_kernel, full),
        out_shape=(shape(*tokens.shape), grad_shape),
        in_specs=[SMEM] + [ANYWHERE] * 4,
        out_specs=(ANYWHERE, VMEM),
        scratch_shapes=[
            pltpu.VMEM((slots, block_rows, features), bf),
            pltpu.VMEM((shard, width), bf),
            pltpu.VMEM((shard, width), bf),
            pltpu.VMEM((shard, width), bf),
            pltpu.SemaphoreType.DMA((3,)),
            pltpu.SemaphoreType.DMA((slots,)),
            pltpu.SemaphoreType.DMA((slots,)),
        ],
        compiler_params=params(8 + slots // 8),
        name="tail",
    )(source, *in_hbm(back, down_keep, down_near, down_far))
    return (token_grad, grad_down, grad_up)


def solution(mesh):
    placed = (
        P("dp", "mp", None),
        P("dp", "mp", None),
        P("dp"),
        P("dp"),
        P(),
        P("mp", "dp"),
        P("mp", "dp", None),
        P("mp", "dp", None),
    )
    return jax.shard_map(
        shards,
        mesh=mesh,
        in_specs=placed,
        out_specs=(P("dp", "mp", None), P("mp", "dp", None), P("mp", "dp", None)),
        check_vma=False,
    )
```

time: 240 us -> 109 us (0.45)
  local copies, waits for them, and re-layouts: 56.2 us -> 2.74 us
  waiting for transfers between devices: 104 us -> 63 us
  Pallas kernels: 0 us -> 24.7 us
  other arithmetic: 21.2 us -> 0.18 us
  matrix products: 15.8 us -> 0 us
  between operations: 14 us -> 0.81 us
  blocking collectives: 5.06 us -> 0 us
  loops' own time: 4.12 us -> 0 us
    all_to_all x4 -> x2, waiting for transfers between devices: 67.7 us -> 16.6 us  [exchange(): return lax.all_to_all(array, 'dp', split_axis=0, concat_axis=0, tiled=True)]
    ppermute x0 -> x6, waiting for transfers between devices: none -> 46.5 us  [swap(): return lax.ppermute(array, 'mp', [(i, i ^ bit) for i in range(mp_size)])]
    unnamed x4 -> x0, waiting for transfers between devices: 36.5 us -> none
    pallas_call x0 -> x8, Pallas kernels: none -> 24.7 us  [the longest x1 8.27 us: shards(): pl.pallas_call(functools.partial(weight_grad_kernel, (capacity, mp_size,...]
    unnamed x27 -> x24, local copies, waits for them, and re-layouts: 25 us -> 2.74 us
    dot_general x10 -> x0, matrix products: 15.8 us -> none  [the longest x2 7.31 us: adapter_backward(): inner = jnp.dot(normed, down_cols, preferred_element_type=jnp.float32)]
    while x44 -> x0, local copies, waits for them, and re-layouts: 12 us -> none
    gather x10 -> x0, local copies, waits for them, and re-layouts: 9.57 us -> none  [the longest x1 2.03 us: shards(): buf_x = jnp.where(buf_has[:, None, None], recv_x[buf_source], bf_zero)]
  transfers between devices with their start and end apart: 7 -> 8, of which waited for: 5 -> 7; matrix products, arithmetic and copies ran while one was open for 9% -> 0% of each run, Pallas kernels for 0% -> 8%
where the time goes in v2:
time: 109 us; the launch traced here: 108 us
  waiting for transfers between devices  63 us (58%)
  Pallas kernels  24.7 us (23%)
  starting transfers between devices  16.9 us (16%)
  local copies, waits for them, and re-layouts  2.74 us (3%)
    ppermute x6, waiting for transfers between devices, swap(): return lax.ppermute(array, 'mp', [(i, i ^ bit) for i in range(mp_size)])  46.5 us
    all_to_all x2, waiting for transfers between devices, exchange(): return lax.all_to_all(array, 'dp', split_axis=0, concat_axis=0, tiled=True)  16.6 us
    all_to_all x2, starting transfers between devices, exchange(): return lax.all_to_all(array, 'dp', split_axis=0, concat_axis=0, tiled=True)  11.7 us
    pallas_call x1, Pallas kernels, shards(): pl.pallas_call(functools.partial(weight_grad_kernel, (capacity, mp_size,...  8.27 us
    ppermute x6, starting transfers between devices, swap(): return lax.ppermute(array, 'mp', [(i, i ^ bit) for i in range(mp_size)])  5.23 us
    pallas_call x1, Pallas kernels, shards(): pl.pallas_call(functools.partial(tail_kernel, full), out_shape=(shape(*to...  4.2 us
    pallas_call x1, Pallas kernels, shards(): pl.pallas_call(functools.partial(pack_kernel, (dp_size, capacity, lang_lo...  3.67 us
    pallas_call x1, Pallas kernels, shards(): pl.pallas_call(finish_grad, out_shape=grad_shape, in_specs=[VMEM] * 3, ou...  3.14 us
  transfers between devices with their start and end apart: 8, of which 7 were waited for; matrix products, arithmetic and copies ran while one was open for 0% of the time, Pallas kernels for 8%

profile of v2, /device:TPU:0, one launch (start us, length us, event | category | flops | bytes accessed | tf_op | source)
XLA Modules:
  0.0 108.4 jit_solution(15349933502879942457)
XLA Ops:
  0.6 3.7 %pack.1 = (bf16[8,16,8320]{2,1,0:T(8,128)(2,1)}, s32[16]{0:T(128)S(1)}) custom-call(s32[16]{0:T(128)} %lang_hbm.1, s32[16]{0:T(128)} %count_hbm.1, s32[16]{0:T(128)} %slot_hbm.1, bf16[16,32,1024]{2,1,0:T(8,128)(2,1)} %x_hbm.1, bf16[16,32,1024]{2,1,0:T(8,128)(2,1)} %dy_hbm.1), custom_call_target="tpu_custom_call" | custom-call | tf_op jit(solution)/shard_map/pack/pallas_call | solution.py:392
  4.3 7.4 %all-to-all-start = ((bf16[8,16,8320]{2,1,0:T(8,128)(2,1)}), bf16[8,16,8320]{2,1,0:T(8,128)(2,1)}, u32[]{:S(2)}, u32[]{:S(2)}) async-start(bf16[8,16,8320]{2,1,0:T(8,128)(2,1)} %get-tuple-element.21), calls=%async_computation | async-start | bytes 4259840 | tf_op jit(solution)/shard_map/all_to_all | solution.py:390
  11.8 2.3 %payload.1.own_hbm = bf16[528,1024]{1,0:T(8,128)(2,1)S(1)} custom-call(s32[16]{0:T(128)S(1)} %get-tuple-element.20.after_ref.source_ref, bf16[256,2,512]{2,1,0:T(2,128)(2,1)S(1)} %copy-done.5, bf16[256,2,512]{2,1,0:T(2,128)(2,1)S(1)} %copy-done.6, bf16[2,256]{1,0:T(2,128)(2,1)S(1)} %bitcast.2), custom_call_target="tpu_custom_call" | custom-call | tf_op jit(solution)/shard_map/payload/pallas_call | solution.py:413
  14.2 1.6 %collective-permute-start = (bf16[528,1024]{1,0:T(8,128)(2,1)S(1)}, bf16[528,1024]{1,0:T(8,128)(2,1)S(1)}, u32[]{:S(2)}, u32[]{:S(2)}) collective-permute-start(bf16[528,1024]{1,0:T(8,128)(2,1)S(1)} %payload.1.own_hbm), channel_id=1, source_target_pairs={{0,2},{1,3},{2,0},{3,1},{4,6},{5,7},{6,4},{7,5},{8,10},{9,11},{10,... | collective-permute-start | bytes 3244040 | tf_op jit(solution)/shard_map/ppermute | solution.py:387
  15.7 23.8 %collective-permute-done.across_hbm = bf16[528,1024]{1,0:T(8,128)(2,1)S(1)} collective-permute-done((bf16[528,1024]{1,0:T(8,128)(2,1)S(1)}, bf16[528,1024]{1,0:T(8,128)(2,1)S(1)}, u32[]{:S(2)}, u32[]{:S(2)}) %collective-permute-start) | collective-permute-done | bytes 1081376 | tf_op jit(solution)/shard_map/ppermute | solution.py:387
  39.6 0.2 pad_maximum_fusion
  39.7 0.9 copy-done.9
  40.6 4.4 %collective-permute-done.1.both_hbm = bf16[1056,1024]{1,0:T(8,128)(2,1)} collective-permute-done((bf16[1056,1024]{1,0:T(8,128)(2,1)S(1)}, bf16[1056,1024]{1,0:T(8,128)(2,1)}, u32[]{:S(2)}, u32[]{:S(2)}) %collective-permute-start.1) | collective-permute-done | bytes 2162720 | tf_op jit(solution)/shard_map/ppermute | solution.py:387
  45.0 15.8 %all-to-all-done.recv_hbm = bf16[8,16,8320]{2,1,0:T(8,128)(2,1)} async-done(((bf16[8,16,8320]{2,1,0:T(8,128)(2,1)}), bf16[8,16,8320]{2,1,0:T(8,128)(2,1)}, u32[]{:S(2)}, u32[]{:S(2)}) %all-to-all-start) | async-done | bytes 2129952 | tf_op jit(solution)/shard_map/all_to_all | solution.py:390
  60.8 8.3 %weight_grads.1 = (bf16[2,256,1024]{2,1,0:T(8,128)(2,1)S(1)}, bf16[2,256,1024]{2,1,0:T(8,128)(2,1)S(1)}, bf16[2,256,1024]{2,1,0:T(8,128)(2,1)S(1)}, bf16[2,256,1...) custom-call(bf16[8,16,8320]{2,1,0:T(8,128)(2,1)} %all-to-all-done.re, ...), custom_call_target="tpu_custom_call" | custom-call | tf_op jit(solution)/shard_map/weight_grads/pallas_call | solution.py:424
  69.2 2.8 %token_grads.1.refs_0_ = bf16[512,1024]{1,0:T(8,128)(2,1)} custom-call(bf16[512,1024]{1,0:T(8,128)(2,1)S(1)} %get-tuple-element.24.x_ref, bf16[512,1024]{1,0:T(8,128)(2,1)S(1)} %get-tuple-element.25.dy_ref, bf16[512,1024]{1,0:T(8,128)(2,1)S(1)} %get-tuple-element.26.inner_ref, f32[512,256]{1,0:T(8,128)S(1)} %get-tuple-element.27.stats_ref, ...), custom_call_target="tpu_custom_call" | custom-call | tf_op jit(solution)/shard_map/token_grads/pallas_call | solution.py:455
  72.1 0.1 up_add.1
  72.2 0.9 copy-done.8
  73.2 4.2 %all-to-all-start.1 = ((bf16[16,32,1024]{2,1,0:T(8,128)(2,1)}), bf16[16,32,1024]{2,1,0:T(8,128)(2,1)}, u32[]{:S(2)}, u32[]{:S(2)}) async-start(bf16[16,32,1024]{2,1,0:T(8,128)(2,1)} %bitcast.3), calls=%async_computation.1 | async-start | bytes 2097152 | tf_op jit(solution)/shard_map/all_to_all | solution.py:390
  77.5 0.6 collective-permute-start.3
  78.0 1.5 %collective-permute-start.5 = (bf16[256,1024]{1,0:T(8,128)(2,1)}, bf16[256,1024]{1,0:T(8,128)(2,1)S(1)}, u32[]{:S(2)}, u32[]{:S(2)}) collective-permute-start(bf16[256,1024]{1,0:T(8,128)(2,1)} %copy-done.8), channel_id=1, source_target_pairs={{0,2},{1,3},{2,0},{3,1},{4,6},{5,7},{6,4},{7,5},{8,10},{9,11},{10,... | collective-permute-start | bytes 1572872 | tf_op jit(solution)/shard_map/ppermute | solution.py:387
  79.5 0.8 collective-permute-done.3.near_ref.near_hbm
  80.4 1.6 %collective-permute-start.4 = (bf16[256,1024]{1,0:T(8,128)(2,1)S(1)}, bf16[256,1024]{1,0:T(8,128)(2,1)S(1)}, u32[]{:S(2)}, u32[]{:S(2)}) collective-permute-start(bf16[256,1024]{1,0:T(8,128)(2,1)S(1)} %down_add.1), channel_id=1, source_target_pairs={{0,2},{1,3},{2,0},{3,1},{4,6},{5,7},{6,4},{7,5},{8,10},{9,11},{10,... | collective-permute-start | bytes 1572872 | tf_op jit(solution)/shard_map/ppermute | solution.py:387
  82.0 11.0 %collective-permute-done.5.far_ref = bf16[256,1024]{1,0:T(8,128)(2,1)S(1)} collective-permute-done((bf16[256,1024]{1,0:T(8,128)(2,1)}, bf16[256,1024]{1,0:T(8,128)(2,1)S(1)}, u32[]{:S(2)}, u32[]{:S(2)}) %collective-permute-start.5) | collective-permute-done | bytes 524320 | tf_op jit(solution)/shard_map/ppermute | solution.py:387
  93.0 0.8 copy-done.11
  93.8 3.1 %up_finish.1 = bf16[256,2,512]{2,1,0:T(2,128)(2,1)} custom-call(bf16[2,256,1024]{2,1,0:T(8,128)(2,1)} %copy-done.1, bf16[2,256,1024]{2,1,0:T(8,128)(2,1)} %copy-done.2, bf16[256,1024]{1,0:T(8,128)(2,1)} %copy-done.11), custom_call_target="tpu_custom_call" | custom-call | tf_op jit(solution)/shard_map/up_finish/pallas_call | solution.py:483
  97.0 6.4 %collective-permute-done.4.far_hbm = bf16[256,1024]{1,0:T(8,128)(2,1)S(1)} collective-permute-done((bf16[256,1024]{1,0:T(8,128)(2,1)S(1)}, bf16[256,1024]{1,0:T(8,128)(2,1)S(1)}, u32[]{:S(2)}, u32[]{:S(2)}) %collective-permute-start.4) | collective-permute-done | bytes 524320 | tf_op jit(solution)/shard_map/ppermute | solution.py:387
  103.4 0.8 all-to-all-done.1.back_hbm
  104.2 4.2 %tail.1 = (bf16[16,32,1024]{2,1,0:T(8,128)(2,1)}, bf16[256,2,512]{2,1,0:T(2,128)(2,1)}) custom-call(s32[16]{0:T(128)S(1)} %get-tuple-element.20.after_ref.source_ref, bf16[16,32,1024]{2,1,0:T(8,128)(2,1)} %all-to-all-done.1.back_hbm, bf16[2,256,1024]{2,1,0:T(8,128)(2,1)} %copy-done.3, bf16[2,256,1024]{2,1,0:T(8,128)(2,1)} %copy-done.4, ...), custom_call_target="tpu_custom_call" | custom-call | tf_op jit(solution)/shard_map/tail/pallas_call | solution.py:491
  (25 shorter events, 0.3 us)
Async XLA Ops:
  4.3 7.5 %copy-start.5 = (bf16[256,2,512]{2,1,0:T(2,128)(2,1)S(1)}, bf16[256,2,512]{2,1,0:T(2,128)(2,1)}, u32[]{:S(2)}) copy-start(bf16[256,2,512]{2,1,0:T(2,128)(2,1)} %down_ref.1) | copy-start | bytes 1572868
  4.3 7.5 %copy-start.6 = (bf16[256,2,512]{2,1,0:T(2,128)(2,1)S(1)}, bf16[256,2,512]{2,1,0:T(2,128)(2,1)}, u32[]{:S(2)}) copy-start(bf16[256,2,512]{2,1,0:T(2,128)(2,1)} %up_ref.1) | copy-start | bytes 1572868
  4.3 7.5 %copy-start.7 = (bf16[256,2]{0,1:T(2,128)(2,1)S(1)}, bf16[256,2]{0,1:T(2,128)(2,1)}, u32[]{:S(2)}) copy-start(bf16[256,2]{0,1:T(2,128)(2,1)} %param.13) | copy-start | bytes 3076
  4.3 56.5 %all-to-all-start = ((bf16[8,16,8320]{2,1,0:T(8,128)(2,1)}), bf16[8,16,8320]{2,1,0:T(8,128)(2,1)}, u32[]{:S(2)}, u32[]{:S(2)}) async-start(bf16[8,16,8320]{2,1,0:T(8,128)(2,1)} %get-tuple-element.21), calls=%async_computation | async-start | bytes 4259840 | tf_op jit(solution)/shard_map/all_to_all | solution.py:390
  14.2 25.6 %copy-start = (bf16[528,1024]{1,0:T(8,128)(2,1)}, bf16[528,1024]{1,0:T(8,128)(2,1)S(1)}, u32[]{:S(2)}) copy-start(bf16[528,1024]{1,0:T(8,128)(2,1)S(1)} %payload.1.own_hbm) | copy-start | bytes 3244036
  14.2 25.4 %collective-permute-start = (bf16[528,1024]{1,0:T(8,128)(2,1)S(1)}, bf16[528,1024]{1,0:T(8,128)(2,1)S(1)}, u32[]{:S(2)}, u32[]{:S(2)}) collective-permute-start(bf16[528,1024]{1,0:T(8,128)(2,1)S(1)} %payload.1.own_hbm), channel_id=1, source_target_pairs={{0,2},{1,3},{2,0},{3,1},{4,6},{5,7},{6,4},{7,5},{8,10},{9,11},{10,... | collective-permute-start | bytes 3244040 | tf_op jit(solution)/shard_map/ppermute | solution.py:387
  39.5 1.1 %copy-start.9 = (bf16[528,1024]{1,0:T(8,128)(2,1)}, bf16[528,1024]{1,0:T(8,128)(2,1)S(1)}, u32[]{:S(2)}) copy-start(bf16[528,1024]{1,0:T(8,128)(2,1)S(1)} %collective-permute-done.across_hbm) | copy-start | bytes 3244036
  40.6 4.4 %collective-permute-start.1 = (bf16[1056,1024]{1,0:T(8,128)(2,1)S(1)}, bf16[1056,1024]{1,0:T(8,128)(2,1)}, u32[]{:S(2)}, u32[]{:S(2)}) collective-permute-start(bf16[1056,1024]{1,0:T(8,128)(2,1)S(1)} %pad_maximum_fusion), channel_id=1, source_target_pairs={{0,1},{1,0},{2,3},{3,2},{4,5},{5,4},{6,7},{7,6},{8,9},{9,8},{10,11... | collective-permute-start | bytes 6488072 | tf_op jit(solution)/shard_map/ppermute | solution.py:387
  69.1 3.0 %copy-start.1 = (bf16[2,256,1024]{2,1,0:T(8,128)(2,1)}, bf16[2,256,1024]{2,1,0:T(8,128)(2,1)S(1)}, u32[]{:S(2)}) copy-start(bf16[2,256,1024]{2,1,0:T(8,128)(2,1)S(1)} %get-tuple-element.22.keep_ref) | copy-start | bytes 3145732
  69.1 11.2 %copy-start.3 = (bf16[2,256,1024]{2,1,0:T(8,128)(2,1)}, bf16[2,256,1024]{2,1,0:T(8,128)(2,1)S(1)}, u32[]{:S(2)}) copy-start(bf16[2,256,1024]{2,1,0:T(8,128)(2,1)S(1)} %get-tuple-element.32.keep_ref.keep_hbm) | copy-start | bytes 3145732
  69.1 2.9 %collective-permute-start.2 = (bf16[2,256,1024]{2,1,0:T(8,128)(2,1)S(1)}, bf16[2,256,1024]{2,1,0:T(8,128)(2,1)S(1)}, u32[]{:S(2)}, u32[]{:S(2)}) collective-permute-start(bf16[2,256,1024]{2,1,0:T(8,128)(2,1)S(1)} %get-tuple-element.23), channel_id=1, source_target_pairs={{0,1},{1,0},{2,3},{3,2},{4,5},{5,4},{6,7},{7,6},{8,9},{9,8},{10,11... | collective-permute-start | bytes 3145736 | tf_op jit(solution)/shard_map/ppermute | solution.py:387
  72.0 1.2 %copy-start.2 = (bf16[2,256,1024]{2,1,0:T(8,128)(2,1)}, bf16[2,256,1024]{2,1,0:T(8,128)(2,1)S(1)}, u32[]{:S(2)}) copy-start(bf16[2,256,1024]{2,1,0:T(8,128)(2,1)S(1)} %collective-permute-done.2.near_ref) | copy-start | bytes 3145732
  72.2 0.9 copy-start.8
  73.2 30.9 %all-to-all-start.1 = ((bf16[16,32,1024]{2,1,0:T(8,128)(2,1)}), bf16[16,32,1024]{2,1,0:T(8,128)(2,1)}, u32[]{:S(2)}, u32[]{:S(2)}) async-start(bf16[16,32,1024]{2,1,0:T(8,128)(2,1)} %bitcast.3), calls=%async_computation.1 | async-start | bytes 2097152 | tf_op jit(solution)/shard_map/all_to_all | solution.py:390
  77.5 2.8 %collective-permute-start.3 = (bf16[2,256,1024]{2,1,0:T(8,128)(2,1)S(1)}, bf16[2,256,1024]{2,1,0:T(8,128)(2,1)S(1)}, u32[]{:S(2)}, u32[]{:S(2)}) collective-permute-start(bf16[2,256,1024]{2,1,0:T(8,128)(2,1)S(1)} %get-tuple-element.33), channel_id=1, source_target_pairs={{0,1},{1,0},{2,3},{3,2},{4,5},{5,4},{6,7},{7,6},{8,9},{9,8},{10,11... | collective-permute-start | bytes 3145736 | tf_op jit(solution)/shard_map/ppermute | solution.py:387
  78.0 15.0 %collective-permute-start.5 = (bf16[256,1024]{1,0:T(8,128)(2,1)}, bf16[256,1024]{1,0:T(8,128)(2,1)S(1)}, u32[]{:S(2)}, u32[]{:S(2)}) collective-permute-start(bf16[256,1024]{1,0:T(8,128)(2,1)} %copy-done.8), channel_id=1, source_target_pairs={{0,2},{1,3},{2,0},{3,1},{4,6},{5,7},{6,4},{7,5},{8,10},{9,11},{10,... | collective-permute-start | bytes 1572872 | tf_op jit(solution)/shard_map/ppermute | solution.py:387
  80.3 16.6 %copy-start.4 = (bf16[2,256,1024]{2,1,0:T(8,128)(2,1)}, bf16[2,256,1024]{2,1,0:T(8,128)(2,1)S(1)}, u32[]{:S(2)}) copy-start(bf16[2,256,1024]{2,1,0:T(8,128)(2,1)S(1)} %collective-permute-done.3.near_ref.near_hbm) | copy-start | bytes 3145732
  80.4 22.9 %collective-permute-start.4 = (bf16[256,1024]{1,0:T(8,128)(2,1)S(1)}, bf16[256,1024]{1,0:T(8,128)(2,1)S(1)}, u32[]{:S(2)}, u32[]{:S(2)}) collective-permute-start(bf16[256,1024]{1,0:T(8,128)(2,1)S(1)} %down_add.1), channel_id=1, source_target_pairs={{0,2},{1,3},{2,0},{3,1},{4,6},{5,7},{6,4},{7,5},{8,10},{9,11},{10,... | collective-permute-start | bytes 1572872 | tf_op jit(solution)/shard_map/ppermute | solution.py:387
  93.0 0.8 copy-start.11
  103.4 0.8 copy-start.10

commit v3 on v2

v3 whole, which is shorter than its diff:
```python
import functools
import math

import jax
import jax.numpy as jnp
from jax import lax
from jax.experimental import pallas as pl
from jax.experimental.pallas import tpu as pltpu
from jax.sharding import PartitionSpec as P

SLAB = 16
LANES = 128
MIB = 1024 * 1024
OFFSETS = (0, 4, 1, 5, 2, 6, 3, 7)
ANYWHERE = pl.BlockSpec(memory_space=pl.ANY)
VMEM = pl.BlockSpec(memory_space=pltpu.VMEM)
SMEM = pl.BlockSpec(memory_space=pltpu.SMEM)


def params(mib):
    return pltpu.CompilerParams(vmem_limit_bytes=min(mib, 60) * MIB)


def start_all(copies):
    for copy in copies:
        copy.start()


def wait_all(copies):
    for copy in copies:
        copy.wait()


def pair_kernel(after_ref, own_hbm, core_hbm, out_ref, sems):
    size = own_hbm.shape[0]
    copies = [
        pltpu.make_async_copy(src, out_ref.at[pl.ds(n * size, size)], sems.at[n])
        for n, src in enumerate((own_hbm, core_hbm))
    ]
    start_all(copies)
    wait_all(copies)


def pack_kernel(dims, lang_hbm, count_hbm, slot_hbm, x_hbm, dy_hbm, *refs):
    dp_size, capacity, lang_local, full, direct = dims
    chunks, (source_ref, *scratch) = (refs[:dp_size], refs[dp_size:]) if direct else (None, refs[1:])
    block_count, block_rows, features = x_hbm.shape
    slots = dp_size * capacity
    halves = block_rows // SLAB
    x_buf, dy_buf, lang_ref, count_ref, slot_ref, taken_ref, sems, *scratch = scratch
    if not direct:
        out_hbm, (packed, out_sem) = refs[0], scratch
    loads = [
        pltpu.make_async_copy(src, dst, sems.at[n])
        for n, (src, dst) in enumerate(
            (
                (lang_hbm, lang_ref),
                (count_hbm, count_ref),
                (slot_hbm, slot_ref),
                (x_hbm, x_buf),
                (dy_hbm, dy_buf),
            )
        )
    ]
    start_all(loads)

    def clear_owner(owner, carry):
        taken_ref[owner] = 0
        return carry

    def clear_slot(slot, carry):
        source_ref[slot] = -1
        return carry

    lax.fori_loop(0, dp_size, clear_owner, 0, unroll=dp_size <= 8)
    if not full:
        lax.fori_loop(0, slots, clear_slot, 0)
    wait_all(loads[:3])

    def place(block, carry):
        owner = slot_ref[lang_ref[block]] // lang_local
        rank = taken_ref[owner]
        taken_ref[owner] = rank + 1
        source_ref[owner * capacity + rank] = block
        return carry

    lax.fori_loop(0, block_count, place, 0, unroll=True)
    wait_all(loads[3:])
    row_start = lax.axis_index("mp") * block_rows
    dy_groups = capacity * halves
    lane = lax.broadcasted_iota(jnp.int32, (SLAB, LANES), 1)

    def lanes_of(group):
        return pl.ds(group * features, features)

    def fill(out, block, place_in):
        live = count_ref[block] - row_start
        for half in range(halves):
            here = pl.ds(half * SLAB, SLAB)
            group = place_in * halves + half
            out[:, lanes_of(group)] = x_buf[block, here, :]
            rows = lax.broadcasted_iota(jnp.int32, (SLAB, features), 0) + half * SLAB
            piece = dy_buf[block, here, :].astype(jnp.float32)
            out[:, lanes_of(dy_groups + group)] = jnp.where(rows < live, piece, 0.0).astype(jnp.bfloat16)

    def blank(out, place_in):
        for half in range(halves):
            for base in (0, dy_groups):
                group = base + place_in * halves + half
                out[:, lanes_of(group)] = jnp.zeros((SLAB, features), jnp.bfloat16)

    def one_peer(out, peer):
        tags = jnp.zeros((SLAB, LANES), jnp.int32)
        for place_in in range(capacity):
            block = source_ref[peer * capacity + place_in]
            if full:
                fill(out, block, place_in)
            else:
                pl.when(block >= 0)(functools.partial(fill, out, block, place_in))
                pl.when(block < 0)(functools.partial(blank, out, place_in))
                block = jnp.maximum(block, 0)
            local = slot_ref[lang_ref[block]] % lang_local
            tags = jnp.where(lane // (LANES // capacity) == place_in, local, tags)
        out[:, pl.ds(2 * dy_groups * features, LANES)] = tags.astype(jnp.float32).astype(jnp.bfloat16)

    if direct:
        for offset, out in zip(direct, chunks):
            one_peer(out, lax.axis_index("dp") ^ offset)
    else:

        def send_peer(peer, carry):
            one_peer(packed.at[peer], peer)
            pltpu.make_async_copy(packed.at[peer], out_hbm.at[peer], out_sem).start()
            return carry

        lax.fori_loop(0, dp_size, send_peer, 0)
        pltpu.make_async_copy(packed, out_hbm, out_sem).wait()


def spread(values, second):
    return jnp.concatenate([jnp.where(second, 0.0, values), jnp.where(second, values, 0.0)], axis=1).astype(jnp.bfloat16)


def pick(values, second):
    half = values.shape[1] // 2
    return jnp.where(second, values[:, half:], values[:, :half])


def wide(column):
    return jnp.broadcast_to(column, (column.shape[0], LANES))


def gains_of(gain_ref, second):
    return jnp.where(second, gain_ref[1:2, :], gain_ref[0:1, :])


def normalize(values, second, gain_ref):
    values = values.astype(jnp.float32)
    row_mean = jnp.mean(values, axis=-1, keepdims=True)
    centered = values - row_mean
    inv_std = lax.rsqrt(jnp.mean(centered * centered, axis=-1, keepdims=True) + 1e-05)
    normed = (centered * inv_std * gains_of(gain_ref, second)).astype(jnp.bfloat16)
    return row_mean, inv_std, normed


def middle(masked, inner, second, up_ref):
    bell = 0.5 * (1.0 + lax.erf(inner * (1.0 / math.sqrt(2.0))))
    slope = bell + inner * jnp.exp(-0.5 * inner * inner) * (1.0 / math.sqrt(2.0 * math.pi))
    grad_act = pick(jnp.dot(masked, up_ref[...], preferred_element_type=jnp.float32), second)
    return spread(inner * bell, second), spread(grad_act * slope, second)


def backward(values, masked, row_mean, inv_std, second, grad_inner, gain_ref, down_ref):
    grad_normed = lax.dot_general(
        grad_inner, down_ref[...], (((1,), (1,)), ((), ())), preferred_element_type=jnp.float32
    )
    unit = (values.astype(jnp.float32) - row_mean) * inv_std
    scaled = grad_normed * gains_of(gain_ref, second)
    token_grad = masked.astype(jnp.float32) + inv_std * (
        scaled - jnp.mean(scaled, axis=-1, keepdims=True) - unit * jnp.mean(scaled * unit, axis=-1, keepdims=True)
    )
    return token_grad.astype(jnp.bfloat16)


def weight_grad_kernel(dims, *refs):
    capacity, mp_size, tile, scale, direct = dims
    source_count = len(direct) or 1
    sources, (pair_hbm, far_hbm), refs = refs[:source_count], refs[source_count:][:2], refs[source_count + 2 :]
    part_refs, (x_buf, dy_buf, inner_buf, stats_buf, id_buf, down_ref, gain_ref) = refs[:4], refs[4:11]
    up_ref, gain_buf, normed_buf, act_buf, sems, weight_sems, *scratch = refs[11:]
    rows, features = x_buf.shape
    shard = features // mp_size
    first, then, later = [], [], []
    if direct:
        raw = sources
        chunks = len(direct)
    else:
        (raw,) = scratch
        chunks = raw.shape[0]
    groups = rows // (chunks * SLAB)
    split = groups * features
    if not direct:
        first.append(pltpu.make_async_copy(sources[0], raw, sems))
    size = pair_hbm.shape[0] // 2
    for offset in range(mp_size):
        weight, start = (pair_hbm, far_hbm)[offset // 2], offset % 2 * size
        here = pl.ds(pl.multiple_of((lax.axis_index("mp") ^ offset) * shard, shard), shard)
        for n, (group, src, dst) in enumerate(
            (
                (first, weight.at[pl.ds(start + 2 * shard, SLAB)], gain_buf.at[offset]),
                (then, weight.at[pl.ds(start, shard)], down_ref.at[here]),
                (later, weight.at[pl.ds(start + shard, shard)], up_ref.at[here]),
            )
        ):
            group.append(pltpu.make_async_copy(src, dst, weight_sems.at[n, offset]))
    start_all(first)
    start_all(then)
    start_all(later)
    wait_all(first)
    gain = gain_buf[0].astype(jnp.float32)
    for offset in range(1, mp_size):
        gain = gain + gain_buf[offset].astype(jnp.float32)
    gain_ref[...] = gain
    tile_chunks = tile // (groups * SLAB)
    per_block = groups // capacity

    def chunk_of(step, chunk):
        return raw[chunk] if direct else raw.at[step * tile_chunks + chunk]

    def rows_of(step, base):
        return jnp.concatenate(
            [
                chunk_of(step, chunk)[:, pl.ds((base + group) * features, features)]
                for chunk in range(tile_chunks)
                for group in range(groups)
            ],
            axis=0,
        )

    def ids_of(step):
        pieces = []
        for chunk in range(tile_chunks):
            tags = chunk_of(step, chunk)[:, pl.ds(2 * split, LANES)].astype(jnp.float32)
            for group in range(groups):
                column = (group // per_block) * (LANES // capacity)
                pieces.append(wide(tags[:, column : column + 1]))
        return jnp.concatenate(pieces, axis=0)

    whole = rows == tile
    if not whole:
        wait_all(then + later)

    def one_tile(step, carry):
        here = pl.ds(pl.multiple_of(step * tile, tile), tile)
        ids = ids_of(step)
        id_buf[here, :] = ids
        second = ids[:, :1] > 0.5
        values = rows_of(step, 0)
        x_buf[here, :] = values
        row_mean, inv_std, normed = normalize(values, second, gain_ref)
        normed_buf[here, :] = normed
        stats_buf[here, :] = jnp.concatenate([wide(row_mean), wide(inv_std)], axis=1)
        if whole:
            wait_all(then)
        inner = pick(jnp.dot(normed_buf[here, :], down_ref[...], preferred_element_type=jnp.float32), second)
        if whole:
            wait_all(later)
        dy_buf[here, :] = rows_of(step, groups)
        act, grad_inner = middle(dy_buf[here, :], inner, second, up_ref)
        act_buf[here, :] = act
        inner_buf[here, :] = grad_inner
        return carry

    if whole:
        one_tile(0, 0)
    else:
        lax.fori_loop(0, rows // tile, one_tile, 0)
    for kind, (left, right) in enumerate(((dy_buf, act_buf), (normed_buf, inner_buf))):
        for offset in range(mp_size):
            here = pl.ds(pl.multiple_of((lax.axis_index("mp") ^ offset) * shard, shard), shard)
            part = lax.dot_general(
                left[:, here], right[...], (((0,), (0,)), ((), ())), preferred_element_type=jnp.float32
            )
            part_refs[2 * kind + offset % 2][offset // 2] = (part * scale).astype(jnp.bfloat16)


def token_grad_kernel(tile, chunk_rows, direct, x_ref, dy_ref, inner_ref, stats_ref, id_ref, down_ref, gain_ref, *refs):
    rows = x_ref.shape[0]

    def part(here):
        stats = stats_ref[here, :]
        return backward(
            x_ref[here, :],
            dy_ref[here, :],
            stats[:, :1],
            stats[:, LANES : LANES + 1],
            id_ref[here, :][:, :1] > 0.5,
            inner_ref[here, :],
            gain_ref,
            down_ref,
        )

    if direct:
        for step in range(rows // tile):
            token_grad = part(pl.ds(step * tile, tile))
            for n in range(tile // chunk_rows):
                refs[step * (tile // chunk_rows) + n][...] = token_grad[n * chunk_rows : (n + 1) * chunk_rows]
        return
    out_hbm, grad_buf, sem = refs

    def one_tile(step, carry):
        here = pl.ds(pl.multiple_of(step * tile, tile), tile)
        grad_buf[here, :] = part(here)
        pltpu.make_async_copy(grad_buf.at[here], out_hbm.at[here], sem).start()
        return carry

    lax.fori_loop(0, rows // tile, one_tile, 0)
    pltpu.make_async_copy(grad_buf, out_hbm, sem).wait()


def up_add_kernel(keep_ref, near_ref, *refs):
    sum_ref = refs[-1]
    sum_ref[...] = (keep_ref[1].astype(jnp.float32) + near_ref[1].astype(jnp.float32)).astype(sum_ref.dtype)


def down_add_kernel(keep_ref, near_ref, sum_ref, own_ref):
    total = keep_ref[...].astype(jnp.float32) + near_ref[...].astype(jnp.float32)
    sum_ref[...] = total[1].reshape(sum_ref.shape).astype(sum_ref.dtype)
    own_ref[...] = total[0].reshape(own_ref.shape)


def finish_grad(keep_ref, near_ref, far_ref, out_ref):
    total = keep_ref[0].astype(jnp.float32) + near_ref[0].astype(jnp.float32) + far_ref[...].astype(jnp.float32)
    out_ref[...] = total.reshape(out_ref.shape).astype(out_ref.dtype)


def tail_kernel(dims, source_ref, own_hbm, far_ref, *refs):
    capacity, full, direct = dims
    back_count = len(direct) or 1
    backs, (out_hbm, grad_hbm, own, grad, sems, out_sems, *buf) = refs[:back_count], refs[back_count:]
    slots = out_sems.shape[0]
    block_rows = out_hbm.shape[1]
    half = slots // 2
    term = pltpu.make_async_copy(own_hbm, own, sems.at[0])
    term.start()

    def store(slot, piece):
        if full:
            return pltpu.make_async_copy(piece, out_hbm.at[source_ref[slot]], out_sems.at[0])
        return pltpu.make_async_copy(piece, out_hbm.at[jnp.maximum(source_ref[slot], 0)], out_sems.at[slot])

    if direct:
        for offset, back in zip(direct, backs):
            for place_in in range(capacity):
                slot = (lax.axis_index("dp") ^ offset) * capacity + place_in
                store(slot, back.at[pl.ds(place_in * block_rows, block_rows)]).start()
    else:
        (buf,) = buf
        loads = [
            pltpu.make_async_copy(backs[0].at[pl.ds(n * half, half)], buf.at[pl.ds(n * half, half)], sems.at[1 + n])
            for n in range(2)
        ]
        start_all(loads)
        for n, load in enumerate(loads):
            load.wait()
            for slot in range(n * half, (n + 1) * half):
                if full:
                    store(slot, buf.at[slot]).start()
                else:
                    pl.when(source_ref[slot] >= 0)(store(slot, buf.at[slot]).start)
    term.wait()
    grad[...] = (own[...] + far_ref[...].astype(jnp.float32)).astype(grad.dtype)
    write = pltpu.make_async_copy(grad, grad_hbm, sems.at[3])
    write.start()
    if full:
        pltpu.make_async_copy(out_hbm, out_hbm, out_sems.at[0]).wait()
    else:
        for slot in range(slots):
            pl.when(source_ref[slot] >= 0)(store(slot, buf.at[slot]).wait)
    write.wait()


def shards(tokens, cotangent, block_lang, counts, slot_of, ln_gain, w_down, w_up):
    block_count, block_rows, features = tokens.shape
    dp_size = lax.axis_size("dp")
    mp_size = lax.axis_size("mp")
    lang_local, bottleneck = w_down.shape[1:]
    shard = w_down.shape[0]
    width = lang_local * bottleneck
    capacity = (block_count + dp_size - 1) // dp_size
    slots = dp_size * capacity
    full = slots == block_count
    halves = block_rows // SLAB
    groups = capacity * halves
    lanes = 2 * groups * features + LANES
    rows = slots * block_rows
    tile = min(512, rows)
    resident = rows <= tile
    bf = jnp.bfloat16

    def shape(*extent, kind=bf):
        return jax.ShapeDtypeStruct(extent, kind)

    def vmem_shape(*extent, kind=bf):
        return pltpu.VMEM(extent, kind) if resident else shape(*extent, kind=kind)

    def in_vmem(*arrays):
        return [pltpu.with_memory_space_constraint(array, pltpu.VMEM) if resident else array for array in arrays]

    def in_hbm(*arrays):
        return [pltpu.with_memory_space_constraint(array, pltpu.HBM) for array in arrays]

    def swap(array, bit):
        return lax.ppermute(array, "mp", [(i, i ^ bit) for i in range(mp_size)])

    def exchange(array):
        return lax.all_to_all(array, "dp", split_axis=0, concat_axis=0, tiled=True)

    def swap_all(chunks):
        return [
            lax.ppermute(chunk, "dp", [(i, i ^ offset) for i in range(dp_size)]) if offset else chunk
            for offset, chunk in zip(OFFSETS, chunks)
        ]

    direct = OFFSETS if resident and dp_size == len(OFFSETS) else ()
    chunk_shape = [vmem_shape(SLAB, lanes)] * dp_size if direct else [pltpu.HBM((dp_size, SLAB, lanes), bf)]
    staging = [] if direct else [pltpu.VMEM((dp_size, SLAB, lanes), bf), pltpu.SemaphoreType.DMA(())]
    *packed, source = pl.pallas_call(
        functools.partial(pack_kernel, (dp_size, capacity, lang_local, full, direct)),
        out_shape=(*chunk_shape, shape(slots, kind=jnp.int32)),
        in_specs=[ANYWHERE] * 5,
        out_specs=(*([VMEM] * dp_size if direct else [ANYWHERE]), SMEM),
        scratch_shapes=[
            pltpu.VMEM(tokens.shape, bf),
            pltpu.VMEM(cotangent.shape, bf),
            pltpu.SMEM(block_lang.shape, jnp.int32),
            pltpu.SMEM(counts.shape, jnp.int32),
            pltpu.SMEM(slot_of.shape, jnp.int32),
            pltpu.SMEM((dp_size,), jnp.int32),
            pltpu.SemaphoreType.DMA((5,)),
            *staging,
        ],
        compiler_params=params(8 + slots // 4),
        name="pack",
    )(*in_hbm(block_lang, counts, slot_of, tokens, cotangent))

    gain_part = lax.dynamic_update_slice(
        jnp.zeros((SLAB, features), bf), ln_gain.T, (0, lax.axis_index("mp").astype(jnp.int32) * shard)
    )
    own = jnp.concatenate([w_down.reshape(shard, width), w_up.reshape(shard, width), gain_part], axis=0)
    core = swap(own, 1)
    pair = pl.pallas_call(
        pair_kernel,
        out_shape=vmem_shape(2 * own.shape[0], width),
        in_specs=[SMEM] + [ANYWHERE] * 2,
        out_specs=VMEM if resident else ANYWHERE,
        scratch_shapes=[pltpu.SemaphoreType.DMA((2,))],
        compiler_params=params(2 if resident else 8),
        name="pair",
    )(source, own, core)
    pair_far = swap(pair, 2)

    if direct:
        recv = swap_all(packed)
    else:
        recv = [exchange(packed[0])]
    inputs = in_vmem(*recv, pair, pair_far) if direct else in_hbm(*recv, pair, pair_far)

    part = vmem_shape(mp_size // 2, shard, width)
    up_keep, up_send, down_keep, down_send, *kept = pl.pallas_call(
        functools.partial(weight_grad_kernel, (capacity, mp_size, tile, 1.0 / (block_rows * mp_size), direct)),
        out_shape=(
            part,
            part,
            part,
            part,
            vmem_shape(rows, features),
            vmem_shape(rows, features),
            vmem_shape(rows, width),
            vmem_shape(rows, 2 * LANES, kind=jnp.float32),
            vmem_shape(rows, LANES, kind=jnp.float32),
            vmem_shape(features, width),
            vmem_shape(SLAB, features, kind=jnp.float32),
        ),
        in_specs=[VMEM if direct else ANYWHERE] * len(recv) + [ANYWHERE] * 2,
        out_specs=(VMEM,) * 11,
        scratch_shapes=[
            pltpu.VMEM((features, width), bf),
            pltpu.VMEM((mp_size, SLAB, features), bf),
            pltpu.VMEM((rows, features), bf),
            pltpu.VMEM((rows, width), bf),
            pltpu.SemaphoreType.DMA(()),
            pltpu.SemaphoreType.DMA((3, mp_size)),
            *staging[:1],
        ],
        compiler_params=params(14 + rows // 48),
        name="weight_grads",
    )(*inputs)

    tile = min(256, rows)
    chunk_rows = capacity * block_rows
    token_parts = pl.pallas_call(
        functools.partial(token_grad_kernel, tile, chunk_rows, direct),
        out_shape=[vmem_shape(chunk_rows, features)] * dp_size if direct else [pltpu.HBM((rows, features), bf)],
        in_specs=[VMEM] * 7,
        out_specs=[VMEM] * dp_size if direct else [ANYWHERE],
        scratch_shapes=[] if direct else [pltpu.VMEM((rows, features), bf), pltpu.SemaphoreType.DMA(())],
        compiler_params=params(4 + rows // 64),
        name="token_grads",
    )(*in_vmem(*kept))

    up_near, down_near = swap(up_send, 1), swap(down_send, 1)
    after = in_vmem(token_parts[0]) if direct else in_hbm(token_parts[0])
    *through, up_sum = pl.pallas_call(
        up_add_kernel,
        out_shape=(*[pltpu.HBM(array.shape, array.dtype) for array in after if not direct], vmem_shape(shard, width)),
        in_specs=[VMEM] * 2 + [ANYWHERE],
        out_specs=(*[ANYWHERE for _ in after if not direct], VMEM),
        input_output_aliases={} if direct else {2: 0},
        compiler_params=params(4),
        name="up_add",
    )(*in_vmem(up_keep, up_near), *after)
    down_sum, down_own = pl.pallas_call(
        down_add_kernel,
        out_shape=(
            vmem_shape(shard, lang_local, bottleneck),
            shape(shard, lang_local, bottleneck, kind=jnp.float32),
        ),
        in_specs=[VMEM] * 2,
        out_specs=(VMEM,) * 2,
        compiler_params=params(12),
        name="down_add",
    )(*in_vmem(down_keep, down_near))
    up_far, down_far = swap(up_sum, 2), swap(down_sum, 2)
    if direct:
        backs = in_vmem(*swap_all(token_parts))
    else:
        backs = in_hbm(exchange(through[0].reshape(slots, block_rows, features)))
    grad_shape = shape(shard, lang_local, bottleneck)
    grad_up = pl.pallas_call(
        finish_grad,
        out_shape=grad_shape,
        in_specs=[VMEM] * 3,
        out_specs=VMEM,
        compiler_params=params(8),
        name="up_finish",
    )(*in_hbm(up_keep, up_near, up_far))
    token_grad, grad_down = pl.pallas_call(
        functools.partial(tail_kernel, (capacity, full, direct)),
        out_shape=(shape(*tokens.shape), grad_shape),
        in_specs=[SMEM, ANYWHERE, VMEM] + [VMEM if direct else ANYWHERE] * len(backs),
        out_specs=(ANYWHERE, ANYWHERE),
        scratch_shapes=[
            pltpu.VMEM(grad_shape.shape, jnp.float32),
            pltpu.VMEM(grad_shape.shape, bf),
            pltpu.SemaphoreType.DMA((4,)),
            pltpu.SemaphoreType.DMA((slots,)),
            *([] if direct else [pltpu.VMEM((slots, block_rows, features), bf)]),
        ],
        compiler_params=params(8 + slots // 8),
        name="tail",
    )(source, *in_hbm(down_own), *in_vmem(down_far), *backs)
    return (token_grad, grad_down, grad_up)


def solution(mesh):
    placed = (
        P("dp", "mp", None),
        P("dp", "mp", None),
        P("dp"),
        P("dp"),
        P(),
        P("mp", "dp"),
        P("mp", "dp", None),
        P("mp", "dp", None),
    )
    return jax.shard_map(
        shards,
        mesh=mesh,
        in_specs=placed,
        out_specs=(P("dp", "mp", None), P("mp", "dp", None), P("mp", "dp", None)),
        check_vma=False,
    )
```

time: 109 us -> 103 us (0.945)
  waiting for transfers between devices: 63 us -> 49.8 us
  starting transfers between devices: 16.9 us -> 29.9 us
  Pallas kernels: 24.7 us -> 19.3 us
    ppermute x0 -> x14, waiting for transfers between devices: none -> 46.5 us  [swap_all(): lax.ppermute(chunk, 'dp', [(i, i ^ offset) for i in range(dp_size)])]
    ppermute x6, waiting for transfers between devices: 46.5 us -> 3.33 us  [swap(): return lax.ppermute(array, 'mp', [(i, i ^ bit) for i in range(mp_size)])]
    ppermute x0 -> x14, starting transfers between devices: none -> 22.7 us  [swap_all(): lax.ppermute(chunk, 'dp', [(i, i ^ offset) for i in range(dp_size)])]
    all_to_all x2 -> x0, waiting for transfers between devices: 16.6 us -> none  [exchange(): return lax.all_to_all(array, 'dp', split_axis=0, concat_axis=0, tiled=True)]
    all_to_all x2 -> x0, starting transfers between devices: 11.7 us -> none  [exchange(): return lax.all_to_all(array, 'dp', split_axis=0, concat_axis=0, tiled=True)]
    pallas_call x5, Pallas kernels: 9.63 us -> 7.29 us  [the longest x1 3.57 us: shards(): pl.pallas_call(functools.partial(tail_kernel, (capacity, full, direct)),...]
    ppermute x6, starting transfers between devices: 5.23 us -> 7.2 us  [swap(): return lax.ppermute(array, 'mp', [(i, i ^ bit) for i in range(mp_size)])]
    pallas_call x1, Pallas kernels: 8.27 us -> 6.56 us  [shards(): pl.pallas_call(functools.partial(weight_grad_kernel, (capacity, mp_size,...]
  transfers between devices with their start and end apart: 8 -> 20, of which waited for: 7 -> 9; matrix products, arithmetic and copies ran while one was open for 0% -> 0% of each run, Pallas kernels for 8% -> 8%
where the time goes in v3:
time: 103 us
  waiting for transfers between devices  49.8 us (48%)
  starting transfers between devices  29.9 us (29%)
  Pallas kernels  19.3 us (19%)
  local copies, waits for them, and re-layouts  2.94 us (3%)
    ppermute x14, waiting for transfers between devices, swap_all(): lax.ppermute(chunk, 'dp', [(i, i ^ offset) for i in range(dp_size)])  46.5 us
    ppermute x14, starting transfers between devices, swap_all(): lax.ppermute(chunk, 'dp', [(i, i ^ offset) for i in range(dp_size)])  22.7 us
    ppermute x6, starting transfers between devices, swap(): return lax.ppermute(array, 'mp', [(i, i ^ bit) for i in range(mp_size)])  7.2 us
    pallas_call x1, Pallas kernels, shards(): pl.pallas_call(functools.partial(weight_grad_kernel, (capacity, mp_size,...  6.56 us
    pallas_call x1, Pallas kernels, shards(): pl.pallas_call(functools.partial(tail_kernel, (capacity, full, direct)),...  3.57 us
    ppermute x6, waiting for transfers between devices, swap(): return lax.ppermute(array, 'mp', [(i, i ^ bit) for i in range(mp_size)])  3.33 us
    pallas_call x1, Pallas kernels, shards(): pl.pallas_call(finish_grad, out_shape=grad_shape, in_specs=[VMEM] * 3, ou...  3.14 us
    pallas_call x1, Pallas kernels, shards(): pl.pallas_call(functools.partial(pack_kernel, (dp_size, capacity, lang_lo...  2.31 us
  transfers between devices with their start and end apart: 20, of which 9 were waited for; matrix products, arithmetic and copies ran while one was open for 0% of the time, Pallas kernels for 8%

profile of v3, /device:TPU:0, one launch (start us, length us, event | category | flops | bytes accessed | tf_op | source)
XLA Modules:
  0.0 102.7 jit_solution(13282760454668249045)
XLA Ops:
  4.2 2.3 %pack.1 = (bf16[16,8320]{1,0:T(8,128)(2,1)S(1)}, bf16[16,8320]{1,0:T(8,128)(2,1)S(1)}, bf16[16,8320]{1,0:T(8,128)(2,1)S(1)}, bf16[16,8320]{1,0:T(8,128)(2,1)S(1)...) custom-call(s32[16]{0:T(128)} %lang_hbm.1, ...), custom_call_target="tpu_custom_call" | custom-call | tf_op jit(solution)/shard_map/pack/pallas_call | solution.py:428
  7.3 2.9 %collective-permute-start.8 = (bf16[1056,1024]{1,0:T(8,128)(2,1)S(1)}, bf16[1056,1024]{1,0:T(8,128)(2,1)S(1)}, u32[]{:S(2)}, u32[]{:S(2)}) collective-permute-start(bf16[1056,1024]{1,0:T(8,128)(2,1)S(1)} %pair.1.refs_8_), channel_id=1, source_target_pairs={{0,2},{1,3},{2,0},{3,1},{4,6},{5,7},{6,4},{7,5},{8,10},{9,11},{10,... | collective-permute-start | bytes 6488072 | tf_op jit(solution)/shard_map/ppermute | solution.py:414
  10.2 2.6 %collective-permute-start = (bf16[16,8320]{1,0:T(8,128)(2,1)S(1)}, bf16[16,8320]{1,0:T(8,128)(2,1)S(1)}, u32[]{:S(2)}, u32[]{:S(2)}) collective-permute-start(bf16[16,8320]{1,0:T(8,128)(2,1)S(1)} %get-tuple-element.37), channel_id=1, source_target_pairs={{0,16},{4,20},{8,24},{12,28},{16,0},{20,4},{24,8},{28,12},{1,17},{... | collective-permute-start | bytes 798728 | tf_op jit(solution)/shard_map/ppermute | solution.py:421
  12.8 1.5 %collective-permute-start.1 = (bf16[16,8320]{1,0:T(8,128)(2,1)S(1)}, bf16[16,8320]{1,0:T(8,128)(2,1)S(1)}, u32[]{:S(2)}, u32[]{:S(2)}) collective-permute-start(bf16[16,8320]{1,0:T(8,128)(2,1)S(1)} %get-tuple-element.38), channel_id=1, source_target_pairs={{0,4},{4,0},{8,12},{12,8},{16,20},{20,16},{24,28},{28,24},{1,5},{5... | collective-permute-start | bytes 798728 | tf_op jit(solution)/shard_map/ppermute | solution.py:421
  14.6 1.6 %collective-permute-start.3 = (bf16[16,8320]{1,0:T(8,128)(2,1)S(1)}, bf16[16,8320]{1,0:T(8,128)(2,1)S(1)}, u32[]{:S(2)}, u32[]{:S(2)}) collective-permute-start(bf16[16,8320]{1,0:T(8,128)(2,1)S(1)} %get-tuple-element.40), channel_id=1, source_target_pairs={{0,8},{4,12},{8,0},{12,4},{16,24},{20,28},{24,16},{28,20},{1,9},{5... | collective-permute-start | bytes 798728 | tf_op jit(solution)/shard_map/ppermute | solution.py:421
  16.2 15.6 %collective-permute-done.refs_1_ = bf16[16,8320]{1,0:T(8,128)(2,1)S(1)} collective-permute-done((bf16[16,8320]{1,0:T(8,128)(2,1)S(1)}, bf16[16,8320]{1,0:T(8,128)(2,1)S(1)}, u32[]{:S(2)}, u32[]{:S(2)}) %collective-permute-start) | collective-permute-done | bytes 266272 | tf_op jit(solution)/shard_map/ppermute | solution.py:421
  31.8 2.5 %collective-permute-start.4 = (bf16[16,8320]{1,0:T(8,128)(2,1)S(1)}, bf16[16,8320]{1,0:T(8,128)(2,1)S(1)}, u32[]{:S(2)}, u32[]{:S(2)}) collective-permute-start(bf16[16,8320]{1,0:T(8,128)(2,1)S(1)} %get-tuple-element.41), channel_id=1, source_target_pairs={{0,24},{4,28},{8,16},{12,20},{16,8},{20,12},{24,0},{28,4},{1,25},{... | collective-permute-start | bytes 798728 | tf_op jit(solution)/shard_map/ppermute | solution.py:421
  34.3 9.9 %collective-permute-done.2.refs_3_ = bf16[16,8320]{1,0:T(8,128)(2,1)S(1)} collective-permute-done((bf16[16,8320]{1,0:T(8,128)(2,1)S(1)}, bf16[16,8320]{1,0:T(8,128)(2,1)S(1)}, u32[]{:S(2)}, u32[]{:S(2)}) %collective-permute-start.2) | collective-permute-done | bytes 266272 | tf_op jit(solution)/shard_map/ppermute | solution.py:421
  44.2 2.4 %collective-permute-start.6 = (bf16[16,8320]{1,0:T(8,128)(2,1)S(1)}, bf16[16,8320]{1,0:T(8,128)(2,1)S(1)}, u32[]{:S(2)}, u32[]{:S(2)}) collective-permute-start(bf16[16,8320]{1,0:T(8,128)(2,1)S(1)} %get-tuple-element.43), channel_id=1, source_target_pairs={{0,28},{4,24},{8,20},{12,16},{16,12},{20,8},{24,4},{28,0},{1,29},{... | collective-permute-start | bytes 798728 | tf_op jit(solution)/shard_map/ppermute | solution.py:421
  46.6 7.8 %collective-permute-done.5.refs_6_ = bf16[16,8320]{1,0:T(8,128)(2,1)S(1)} collective-permute-done((bf16[16,8320]{1,0:T(8,128)(2,1)S(1)}, bf16[16,8320]{1,0:T(8,128)(2,1)S(1)}, u32[]{:S(2)}, u32[]{:S(2)}) %collective-permute-start.5) | collective-permute-done | bytes 266272 | tf_op jit(solution)/shard_map/ppermute | solution.py:421
  54.5 3.1 %collective-permute-done.8.refs_9_ = bf16[1056,1024]{1,0:T(8,128)(2,1)S(1)} collective-permute-done((bf16[1056,1024]{1,0:T(8,128)(2,1)S(1)}, bf16[1056,1024]{1,0:T(8,128)(2,1)S(1)}, u32[]{:S(2)}, u32[]{:S(2)}) %collective-permute-start.8) | collective-permute-done | bytes 2162720 | tf_op jit(solution)/shard_map/ppermute | solution.py:414
  57.6 6.6 %weight_grads.1 = (bf16[2,256,1024]{2,1,0:T(8,128)(2,1)S(1)}, bf16[2,256,1024]{2,1,0:T(8,128)(2,1)S(1)}, bf16[2,256,1024]{2,1,0:T(8,128)(2,1)S(1)}, bf16[2,256,1...) custom-call(bf16[16,8320]{1,0:T(8,128)(2,1)S(1)} %get-tuple-element., ...), custom_call_target="tpu_custom_call" | custom-call | tf_op jit(solution)/shard_map/weight_grads/pallas_call | solution.py:470
  64.7 1.9 %token_grads.1 = (bf16[64,1024]{1,0:T(8,128)(2,1)S(1)}, bf16[64,1024]{1,0:T(8,128)(2,1)S(1)}, bf16[64,1024]{1,0:T(8,128)(2,1)S(1)}, bf16[64,1024]{1,0:T(8,128)(2...) custom-call(bf16[512,1024]{1,0:T(8,128)(2,1)S(1)} %get-tuple-element, ...), custom_call_target="tpu_custom_call" | custom-call | tf_op jit(solution)/shard_map/token_grads/pallas_call | solution.py:502
  67.0 1.8 %collective-permute-start.19 = (bf16[256,1024]{1,0:T(8,128)(2,1)S(1)}, bf16[256,1024]{1,0:T(8,128)(2,1)S(1)}, u32[]{:S(2)}, u32[]{:S(2)}) collective-permute-start(bf16[256,1024]{1,0:T(8,128)(2,1)S(1)} %up_add.1), channel_id=1, source_target_pairs={{0,2},{1,3},{2,0},{3,1},{4,6},{5,7},{6,4},{7,5},{8,10},{9,11},{10,... | collective-permute-start | bytes 1572872 | tf_op jit(solution)/shard_map/ppermute | solution.py:414
  69.7 1.4 %collective-permute-start.10 = (bf16[256,2,512]{2,1,0:T(2,128)(2,1)S(1)}, bf16[256,2,512]{2,1,0:T(2,128)(2,1)S(1)}, u32[]{:S(2)}, u32[]{:S(2)}) collective-permute-start(bf16[256,2,512]{2,1,0:T(2,128)(2,1)S(1)} %get-tuple-element.47), channel_id=1, source_target_pairs={{0,2},{1,3},{2,0},{3,1},{4,6},{5,7},{6,4},{7,5},{8,10},{9,11},{10,... | collective-permute-start | bytes 1572872 | tf_op jit(solution)/shard_map/ppermute | solution.py:414
  71.1 4.2 %collective-permute-start.11 = (bf16[64,1024]{1,0:T(8,128)(2,1)S(1)}, bf16[64,1024]{1,0:T(8,128)(2,1)S(1)}, u32[]{:S(2)}, u32[]{:S(2)}) collective-permute-start(bf16[64,1024]{1,0:T(8,128)(2,1)S(1)} %get-tuple-element.56), channel_id=1, source_target_pairs={{0,16},{4,20},{8,24},{12,28},{16,0},{20,4},{24,8},{28,12},{1,17},{... | collective-permute-start | bytes 393224 | tf_op jit(solution)/shard_map/ppermute | solution.py:421
  76.8 7.6 %collective-permute-done.11.refs_1_ = bf16[64,1024]{1,0:T(8,128)(2,1)S(1)} collective-permute-done((bf16[64,1024]{1,0:T(8,128)(2,1)S(1)}, bf16[64,1024]{1,0:T(8,128)(2,1)S(1)}, u32[]{:S(2)}, u32[]{:S(2)}) %collective-permute-start.11) | collective-permute-done | bytes 131104 | tf_op jit(solution)/shard_map/ppermute | solution.py:421
  84.8 2.8 %collective-permute-start.15 = (bf16[64,1024]{1,0:T(8,128)(2,1)S(1)}, bf16[64,1024]{1,0:T(8,128)(2,1)S(1)}, u32[]{:S(2)}, u32[]{:S(2)}) collective-permute-start(bf16[64,1024]{1,0:T(8,128)(2,1)S(1)} %get-tuple-element.60), channel_id=1, source_target_pairs={{0,24},{4,28},{8,16},{12,20},{16,8},{20,12},{24,0},{28,4},{1,25},{... | collective-permute-start | bytes 393224 | tf_op jit(solution)/shard_map/ppermute | solution.py:421
  87.6 1.4 %collective-permute-start.16 = (bf16[64,1024]{1,0:T(8,128)(2,1)S(1)}, bf16[64,1024]{1,0:T(8,128)(2,1)S(1)}, u32[]{:S(2)}, u32[]{:S(2)}) collective-permute-start(bf16[64,1024]{1,0:T(8,128)(2,1)S(1)} %get-tuple-element.61), channel_id=1, source_target_pairs={{0,12},{4,8},{8,4},{12,0},{16,28},{20,24},{24,20},{28,16},{1,13},{... | collective-permute-start | bytes 393224 | tf_op jit(solution)/shard_map/ppermute | solution.py:421
  89.0 1.6 %collective-permute-start.17 = (bf16[64,1024]{1,0:T(8,128)(2,1)S(1)}, bf16[64,1024]{1,0:T(8,128)(2,1)S(1)}, u32[]{:S(2)}, u32[]{:S(2)}) collective-permute-start(bf16[64,1024]{1,0:T(8,128)(2,1)S(1)} %get-tuple-element.62), channel_id=1, source_target_pairs={{0,28},{4,24},{8,20},{12,16},{16,12},{20,8},{24,4},{28,0},{1,29},{... | collective-permute-start | bytes 393224 | tf_op jit(solution)/shard_map/ppermute | solution.py:421
  90.6 3.1 %up_finish.1 = bf16[256,2,512]{2,1,0:T(2,128)(2,1)} custom-call(bf16[2,256,1024]{2,1,0:T(8,128)(2,1)} %copy-done, bf16[2,256,1024]{2,1,0:T(8,128)(2,1)} %copy-done.1, bf16[256,1024]{1,0:T(8,128)(2,1)} %copy-done.3), custom_call_target="tpu_custom_call" | custom-call | tf_op jit(solution)/shard_map/up_finish/pallas_call | solution.py:540
  94.8 1.4 %collective-permute-done.16.refs_6_ = bf16[64,1024]{1,0:T(8,128)(2,1)S(1)} collective-permute-done((bf16[64,1024]{1,0:T(8,128)(2,1)S(1)}, bf16[64,1024]{1,0:T(8,128)(2,1)S(1)}, u32[]{:S(2)}, u32[]{:S(2)}) %collective-permute-start.16) | collective-permute-done | bytes 131104 | tf_op jit(solution)/shard_map/ppermute | solution.py:421
  96.2 3.0 %collective-permute-done.17.refs_7_ = bf16[64,1024]{1,0:T(8,128)(2,1)S(1)} collective-permute-done((bf16[64,1024]{1,0:T(8,128)(2,1)S(1)}, bf16[64,1024]{1,0:T(8,128)(2,1)S(1)}, u32[]{:S(2)}, u32[]{:S(2)}) %collective-permute-start.17) | collective-permute-done | bytes 131104 | tf_op jit(solution)/shard_map/ppermute | solution.py:421
  99.2 3.6 %tail.1 = (bf16[16,32,1024]{2,1,0:T(8,128)(2,1)}, bf16[256,2,512]{2,1,0:T(2,128)(2,1)}) custom-call(s32[16]{0:T(128)S(1)} %get-tuple-element.35.after_ref.source_ref, f32[256,2,512]{2,1,0:T(2,128)} %copy-done.2, bf16[256,2,512]{2,1,0:T(2,128)(2,1)S(1)} %collective-permute-done.10.far_ref, bf16[64,1024]{1,0:T(8,128)(2,1)S(1)} %get-tuple-element.55.refs_0_, ...), custom_call_target="tpu_custom_call" | custom-call | tf_op jit(solution)/shard_map/tail/pallas_call | solution.py:548
  (37 shorter events, 9.3 us)
Async XLA Ops:
  3.6 2.9 %collective-permute-start.7 = (bf16[528,1024]{1,0:T(8,128)(2,1)S(1)}, bf16[528,1024]{1,0:T(8,128)(2,1)S(1)}, u32[]{:S(2)}, u32[]{:S(2)}) collective-permute-start(bf16[528,1024]{1,0:T(8,128)(2,1)S(1)} %pad_maximum_fusion.own_hbm), channel_id=1, source_target_pairs={{0,1},{1,0},{2,3},{3,2},{4,5},{5,4},{6,7},{7,6},{8,9},{9,8},{10,11... | collective-permute-start | bytes 3244040 | tf_op jit(solution)/shard_map/ppermute | solution.py:414
  7.3 50.3 %collective-permute-start.8 = (bf16[1056,1024]{1,0:T(8,128)(2,1)S(1)}, bf16[1056,1024]{1,0:T(8,128)(2,1)S(1)}, u32[]{:S(2)}, u32[]{:S(2)}) collective-permute-start(bf16[1056,1024]{1,0:T(8,128)(2,1)S(1)} %pair.1.refs_8_), channel_id=1, source_target_pairs={{0,2},{1,3},{2,0},{3,1},{4,6},{5,7},{6,4},{7,5},{8,10},{9,11},{10,... | collective-permute-start | bytes 6488072 | tf_op jit(solution)/shard_map/ppermute | solution.py:414
  10.2 21.6 %collective-permute-start = (bf16[16,8320]{1,0:T(8,128)(2,1)S(1)}, bf16[16,8320]{1,0:T(8,128)(2,1)S(1)}, u32[]{:S(2)}, u32[]{:S(2)}) collective-permute-start(bf16[16,8320]{1,0:T(8,128)(2,1)S(1)} %get-tuple-element.37), channel_id=1, source_target_pairs={{0,16},{4,20},{8,24},{12,28},{16,0},{20,4},{24,8},{28,12},{1,17},{... | collective-permute-start | bytes 798728 | tf_op jit(solution)/shard_map/ppermute | solution.py:421
  12.8 21.5 %collective-permute-start.1 = (bf16[16,8320]{1,0:T(8,128)(2,1)S(1)}, bf16[16,8320]{1,0:T(8,128)(2,1)S(1)}, u32[]{:S(2)}, u32[]{:S(2)}) collective-permute-start(bf16[16,8320]{1,0:T(8,128)(2,1)S(1)} %get-tuple-element.38), channel_id=1, source_target_pairs={{0,4},{4,0},{8,12},{12,8},{16,20},{20,16},{24,28},{28,24},{1,5},{5... | collective-permute-start | bytes 798728 | tf_op jit(solution)/shard_map/ppermute | solution.py:421
  14.3 29.9 %collective-permute-start.2 = (bf16[16,8320]{1,0:T(8,128)(2,1)S(1)}, bf16[16,8320]{1,0:T(8,128)(2,1)S(1)}, u32[]{:S(2)}, u32[]{:S(2)}) collective-permute-start(bf16[16,8320]{1,0:T(8,128)(2,1)S(1)} %get-tuple-element.39), channel_id=1, source_target_pairs={{0,20},{4,16},{8,28},{12,24},{16,4},{20,0},{24,12},{28,8},{1,21},{... | collective-permute-start | bytes 798728 | tf_op jit(solution)/shard_map/ppermute | solution.py:421
  14.6 32.0 %collective-permute-start.3 = (bf16[16,8320]{1,0:T(8,128)(2,1)S(1)}, bf16[16,8320]{1,0:T(8,128)(2,1)S(1)}, u32[]{:S(2)}, u32[]{:S(2)}) collective-permute-start(bf16[16,8320]{1,0:T(8,128)(2,1)S(1)} %get-tuple-element.40), channel_id=1, source_target_pairs={{0,8},{4,12},{8,0},{12,4},{16,24},{20,28},{24,16},{28,20},{1,9},{5... | collective-permute-start | bytes 798728 | tf_op jit(solution)/shard_map/ppermute | solution.py:421
  31.8 14.8 %collective-permute-start.4 = (bf16[16,8320]{1,0:T(8,128)(2,1)S(1)}, bf16[16,8320]{1,0:T(8,128)(2,1)S(1)}, u32[]{:S(2)}, u32[]{:S(2)}) collective-permute-start(bf16[16,8320]{1,0:T(8,128)(2,1)S(1)} %get-tuple-element.41), channel_id=1, source_target_pairs={{0,24},{4,28},{8,16},{12,20},{16,8},{20,12},{24,0},{28,4},{1,25},{... | collective-permute-start | bytes 798728 | tf_op jit(solution)/shard_map/ppermute | solution.py:421
  34.3 20.2 %collective-permute-start.5 = (bf16[16,8320]{1,0:T(8,128)(2,1)S(1)}, bf16[16,8320]{1,0:T(8,128)(2,1)S(1)}, u32[]{:S(2)}, u32[]{:S(2)}) collective-permute-start(bf16[16,8320]{1,0:T(8,128)(2,1)S(1)} %get-tuple-element.42), channel_id=1, source_target_pairs={{0,12},{4,8},{8,4},{12,0},{16,28},{20,24},{24,20},{28,16},{1,13},{... | collective-permute-start | bytes 798728 | tf_op jit(solution)/shard_map/ppermute | solution.py:421
  44.2 10.3 %collective-permute-start.6 = (bf16[16,8320]{1,0:T(8,128)(2,1)S(1)}, bf16[16,8320]{1,0:T(8,128)(2,1)S(1)}, u32[]{:S(2)}, u32[]{:S(2)}) collective-permute-start(bf16[16,8320]{1,0:T(8,128)(2,1)S(1)} %get-tuple-element.43), channel_id=1, source_target_pairs={{0,28},{4,24},{8,20},{12,16},{16,12},{20,8},{24,4},{28,0},{1,29},{... | collective-permute-start | bytes 798728 | tf_op jit(solution)/shard_map/ppermute | solution.py:421
  64.1 2.7 %copy-start = (bf16[2,256,1024]{2,1,0:T(8,128)(2,1)}, bf16[2,256,1024]{2,1,0:T(8,128)(2,1)S(1)}, u32[]{:S(2)}) copy-start(bf16[2,256,1024]{2,1,0:T(8,128)(2,1)S(1)} %get-tuple-element.65.keep_ref) | copy-start | bytes 3145732
  64.1 2.7 %collective-permute-start.18 = (bf16[2,256,1024]{2,1,0:T(8,128)(2,1)S(1)}, bf16[2,256,1024]{2,1,0:T(8,128)(2,1)S(1)}, u32[]{:S(2)}, u32[]{:S(2)}) collective-permute-start(bf16[2,256,1024]{2,1,0:T(8,128)(2,1)S(1)} %get-tuple-element.66), channel_id=1, source_target_pairs={{0,1},{1,0},{2,3},{3,2},{4,5},{5,4},{6,7},{7,6},{8,9},{9,8},{10,11... | collective-permute-start | bytes 3145736 | tf_op jit(solution)/shard_map/ppermute | solution.py:414
  64.2 4.6 %collective-permute-start.9 = (bf16[2,256,1024]{2,1,0:T(8,128)(2,1)S(1)}, bf16[2,256,1024]{2,1,0:T(8,128)(2,1)S(1)}, u32[]{:S(2)}, u32[]{:S(2)}) collective-permute-start(bf16[2,256,1024]{2,1,0:T(8,128)(2,1)S(1)} %get-tuple-element.45), channel_id=1, source_target_pairs={{0,1},{1,0},{2,3},{3,2},{4,5},{5,4},{6,7},{7,6},{8,9},{9,8},{10,11... | collective-permute-start | bytes 3145736 | tf_op jit(solution)/shard_map/ppermute | solution.py:414
  66.9 2.8 %copy-start.1 = (bf16[2,256,1024]{2,1,0:T(8,128)(2,1)}, bf16[2,256,1024]{2,1,0:T(8,128)(2,1)S(1)}, u32[]{:S(2)}) copy-start(bf16[2,256,1024]{2,1,0:T(8,128)(2,1)S(1)} %collective-permute-done.18.near_ref) | copy-start | bytes 3145732
  67.0 22.0 %collective-permute-start.19 = (bf16[256,1024]{1,0:T(8,128)(2,1)S(1)}, bf16[256,1024]{1,0:T(8,128)(2,1)S(1)}, u32[]{:S(2)}, u32[]{:S(2)}) collective-permute-start(bf16[256,1024]{1,0:T(8,128)(2,1)S(1)} %up_add.1), channel_id=1, source_target_pairs={{0,2},{1,3},{2,0},{3,1},{4,6},{5,7},{6,4},{7,5},{8,10},{9,11},{10,... | collective-permute-start | bytes 1572872 | tf_op jit(solution)/shard_map/ppermute | solution.py:414
  69.7 29.5 %copy-start.2 = (f32[256,2,512]{2,1,0:T(2,128)}, f32[256,2,512]{2,1,0:T(2,128)S(1)}, u32[]{:S(2)}) copy-start(f32[256,2,512]{2,1,0:T(2,128)S(1)} %get-tuple-element.46.own_hbm) | copy-start | bytes 3145732
  69.7 29.4 %collective-permute-start.10 = (bf16[256,2,512]{2,1,0:T(2,128)(2,1)S(1)}, bf16[256,2,512]{2,1,0:T(2,128)(2,1)S(1)}, u32[]{:S(2)}, u32[]{:S(2)}) collective-permute-start(bf16[256,2,512]{2,1,0:T(2,128)(2,1)S(1)} %get-tuple-element.47), channel_id=1, source_target_pairs={{0,2},{1,3},{2,0},{3,1},{4,6},{5,7},{6,4},{7,5},{8,10},{9,11},{10,... | collective-permute-start | bytes 1572872 | tf_op jit(solution)/shard_map/ppermute | solution.py:414
  71.1 13.3 %collective-permute-start.11 = (bf16[64,1024]{1,0:T(8,128)(2,1)S(1)}, bf16[64,1024]{1,0:T(8,128)(2,1)S(1)}, u32[]{:S(2)}, u32[]{:S(2)}) collective-permute-start(bf16[64,1024]{1,0:T(8,128)(2,1)S(1)} %get-tuple-element.56), channel_id=1, source_target_pairs={{0,16},{4,20},{8,24},{12,28},{16,0},{20,4},{24,8},{28,12},{1,17},{... | collective-permute-start | bytes 393224 | tf_op jit(solution)/shard_map/ppermute | solution.py:421
  75.3 9.5 %collective-permute-start.12 = (bf16[64,1024]{1,0:T(8,128)(2,1)S(1)}, bf16[64,1024]{1,0:T(8,128)(2,1)S(1)}, u32[]{:S(2)}, u32[]{:S(2)}) collective-permute-start(bf16[64,1024]{1,0:T(8,128)(2,1)S(1)} %get-tuple-element.57), channel_id=1, source_target_pairs={{0,4},{4,0},{8,12},{12,8},{16,20},{20,16},{24,28},{28,24},{1,5},{5... | collective-permute-start | bytes 393224 | tf_op jit(solution)/shard_map/ppermute | solution.py:421
  75.8 11.8 %collective-permute-start.13 = (bf16[64,1024]{1,0:T(8,128)(2,1)S(1)}, bf16[64,1024]{1,0:T(8,128)(2,1)S(1)}, u32[]{:S(2)}, u32[]{:S(2)}) collective-permute-start(bf16[64,1024]{1,0:T(8,128)(2,1)S(1)} %get-tuple-element.58), channel_id=1, source_target_pairs={{0,20},{4,16},{8,28},{12,24},{16,4},{20,0},{24,12},{28,8},{1,21},{... | collective-permute-start | bytes 393224 | tf_op jit(solution)/shard_map/ppermute | solution.py:421
  84.4 9.3 %collective-permute-start.14 = (bf16[64,1024]{1,0:T(8,128)(2,1)S(1)}, bf16[64,1024]{1,0:T(8,128)(2,1)S(1)}, u32[]{:S(2)}, u32[]{:S(2)}) collective-permute-start(bf16[64,1024]{1,0:T(8,128)(2,1)S(1)} %get-tuple-element.59), channel_id=1, source_target_pairs={{0,8},{4,12},{8,0},{12,4},{16,24},{20,28},{24,16},{28,20},{1,9},{5... | collective-permute-start | bytes 393224 | tf_op jit(solution)/shard_map/ppermute | solution.py:421
  84.8 10.0 %collective-permute-start.15 = (bf16[64,1024]{1,0:T(8,128)(2,1)S(1)}, bf16[64,1024]{1,0:T(8,128)(2,1)S(1)}, u32[]{:S(2)}, u32[]{:S(2)}) collective-permute-start(bf16[64,1024]{1,0:T(8,128)(2,1)S(1)} %get-tuple-element.60), channel_id=1, source_target_pairs={{0,24},{4,28},{8,16},{12,20},{16,8},{20,12},{24,0},{28,4},{1,25},{... | collective-permute-start | bytes 393224 | tf_op jit(solution)/shard_map/ppermute | solution.py:421
  87.6 8.6 %collective-permute-start.16 = (bf16[64,1024]{1,0:T(8,128)(2,1)S(1)}, bf16[64,1024]{1,0:T(8,128)(2,1)S(1)}, u32[]{:S(2)}, u32[]{:S(2)}) collective-permute-start(bf16[64,1024]{1,0:T(8,128)(2,1)S(1)} %get-tuple-element.61), channel_id=1, source_target_pairs={{0,12},{4,8},{8,4},{12,0},{16,28},{20,24},{24,20},{28,16},{1,13},{... | collective-permute-start | bytes 393224 | tf_op jit(solution)/shard_map/ppermute | solution.py:421
  89.0 1.6 %copy-start.3 = (bf16[256,1024]{1,0:T(8,128)(2,1)}, bf16[256,1024]{1,0:T(8,128)(2,1)S(1)}, u32[]{:S(2)}) copy-start(bf16[256,1024]{1,0:T(8,128)(2,1)S(1)} %collective-permute-done.19.far_ref) | copy-start | bytes 1572868
  89.0 10.2 %collective-permute-start.17 = (bf16[64,1024]{1,0:T(8,128)(2,1)S(1)}, bf16[64,1024]{1,0:T(8,128)(2,1)S(1)}, u32[]{:S(2)}, u32[]{:S(2)}) collective-permute-start(bf16[64,1024]{1,0:T(8,128)(2,1)S(1)} %get-tuple-element.62), channel_id=1, source_target_pairs={{0,28},{4,24},{8,20},{12,16},{16,12},{20,8},{24,4},{28,0},{1,29},{... | collective-permute-start | bytes 393224 | tf_op jit(solution)/shard_map/ppermute | solution.py:421

commit v4 on v3

--- a/solution.py
+++ b/solution.py
@@ -186,8 +186,8 @@
     capacity, mp_size, tile, scale, direct = dims
     source_count = len(direct) or 1
     sources, (pair_hbm, far_hbm), refs = refs[:source_count], refs[source_count:][:2], refs[source_count + 2 :]
-    part_refs, (x_buf, dy_buf, inner_buf, stats_buf, id_buf, down_ref, gain_ref) = refs[:4], refs[4:11]
-    up_ref, gain_buf, normed_buf, act_buf, sems, weight_sems, *scratch = refs[11:]
+    send_ref, x_buf, dy_buf, inner_buf, stats_buf, id_buf, down_ref, gain_ref, normed_buf, act_buf = refs[:10]
+    up_ref, gain_buf, sems, weight_sems, *scratch = refs[10:]
     rows, features = x_buf.shape
     shard = features // mp_size
     first, then, later = [], [], []
@@ -275,16 +275,24 @@
         one_tile(0, 0)
     else:
         lax.fori_loop(0, rows // tile, one_tile, 0)
-    for kind, (left, right) in enumerate(((dy_buf, act_buf), (normed_buf, inner_buf))):
-        for offset in range(mp_size):
-            here = pl.ds(pl.multiple_of((lax.axis_index("mp") ^ offset) * shard, shard), shard)
+    products(dy_buf, act_buf, normed_buf, inner_buf, send_ref, 1, scale)
+
+
+def products(dy_ref, act_ref, normed_ref, inner_ref, out_ref, first, scale):
+    half, _, shard, _ = out_ref.shape
+    for n in range(half):
+        here = pl.ds(pl.multiple_of((lax.axis_index("mp") ^ (2 * n + first)) * shard, shard), shard)
+        for kind, (left, right) in enumerate(((dy_ref, act_ref), (normed_ref, inner_ref))):
             part = lax.dot_general(
                 left[:, here], right[...], (((0,), (0,)), ((), ())), preferred_element_type=jnp.float32
             )
-            part_refs[2 * kind + offset % 2][offset // 2] = (part * scale).astype(jnp.bfloat16)
-
-
-def token_grad_kernel(tile, chunk_rows, direct, x_ref, dy_ref, inner_ref, stats_ref, id_ref, down_ref, gain_ref, *refs):
+            out_ref[n, kind] = (part * scale).astype(jnp.bfloat16)
+
+
+def token_grad_kernel(
+    dims, x_ref, dy_ref, inner_ref, stats_ref, id_ref, down_ref, gain_ref, normed_ref, act_ref, keep_ref, *refs
+):
+    tile, chunk_rows, direct, scale = dims
     rows = x_ref.shape[0]
 
     def part(here):
@@ -305,6 +313,7 @@
             token_grad = part(pl.ds(step * tile, tile))
             for n in range(tile // chunk_rows):
                 refs[step * (tile // chunk_rows) + n][...] = token_grad[n * chunk_rows : (n + 1) * chunk_rows]
+        products(dy_ref, act_ref, normed_ref, inner_ref, keep_ref, 0, scale)
         return
     out_hbm, grad_buf, sem = refs
 
@@ -315,34 +324,27 @@
         return carry
 
     lax.fori_loop(0, rows // tile, one_tile, 0)
+    products(dy_ref, act_ref, normed_ref, inner_ref, keep_ref, 0, scale)
     pltpu.make_async_copy(grad_buf, out_hbm, sem).wait()
 
 
-def up_add_kernel(keep_ref, near_ref, *refs):
-    sum_ref = refs[-1]
-    sum_ref[...] = (keep_ref[1].astype(jnp.float32) + near_ref[1].astype(jnp.float32)).astype(sum_ref.dtype)
-
-
-def down_add_kernel(keep_ref, near_ref, sum_ref, own_ref):
-    total = keep_ref[...].astype(jnp.float32) + near_ref[...].astype(jnp.float32)
-    sum_ref[...] = total[1].reshape(sum_ref.shape).astype(sum_ref.dtype)
-    own_ref[...] = total[0].reshape(own_ref.shape)
-
-
-def finish_grad(keep_ref, near_ref, far_ref, out_ref):
-    total = keep_ref[0].astype(jnp.float32) + near_ref[0].astype(jnp.float32) + far_ref[...].astype(jnp.float32)
-    out_ref[...] = total.reshape(out_ref.shape).astype(out_ref.dtype)
-
-
-def tail_kernel(dims, source_ref, own_hbm, far_ref, *refs):
+def add_kernel(place, keep_ref, near_ref, out_ref):
+    for kind in range(keep_ref.shape[1]):
+        total = keep_ref[place, kind].astype(jnp.float32) + near_ref[place, kind].astype(jnp.float32)
+        out_ref[kind] = total.reshape(out_ref.shape[1:]).astype(out_ref.dtype)
+
+
+def tail_kernel(dims, source_ref, own_ref, far_ref, *refs):
     capacity, full, direct = dims
     back_count = len(direct) or 1
-    backs, (out_hbm, grad_hbm, own, grad, sems, out_sems, *buf) = refs[:back_count], refs[back_count:]
+    backs, (out_hbm, *grad_hbms, grad, sems, out_sems), buf = (
+        refs[:back_count],
+        refs[back_count : back_count + 6],
+        refs[back_count + 6 :],
+    )
     slots = out_sems.shape[0]
     block_rows = out_hbm.shape[1]
     half = slots // 2
-    term = pltpu.make_async_copy(own_hbm, own, sems.at[0])
-    term.start()
 
     def store(slot, piece):
         if full:
@@ -357,7 +359,7 @@
     else:
         (buf,) = buf
         loads = [
-            pltpu.make_async_copy(backs[0].at[pl.ds(n * half, half)], buf.at[pl.ds(n * half, half)], sems.at[1 + n])
+            pltpu.make_async_copy(backs[0].at[pl.ds(n * half, half)], buf.at[pl.ds(n * half, half)], sems.at[n])
             for n in range(2)
         ]
         start_all(loads)
@@ -368,16 +370,17 @@
                     store(slot, buf.at[slot]).start()
                 else:
                     pl.when(source_ref[slot] >= 0)(store(slot, buf.at[slot]).start)
-    term.wait()
-    grad[...] = (own[...] + far_ref[...].astype(jnp.float32)).astype(grad.dtype)
-    write = pltpu.make_async_copy(grad, grad_hbm, sems.at[3])
-    write.start()
+    writes = []
+    for kind, grad_hbm in enumerate(grad_hbms):
+        grad[kind] = (own_ref[kind] + far_ref[kind].astype(jnp.float32)).astype(grad.dtype)
+        writes.append(pltpu.make_async_copy(grad.at[kind], grad_hbm, sems.at[2 + kind]))
+        writes[-1].start()
     if full:
         pltpu.make_async_copy(out_hbm, out_hbm, out_sems.at[0]).wait()
     else:
         for slot in range(slots):
             pl.when(source_ref[slot] >= 0)(store(slot, buf.at[slot]).wait)
-    write.wait()
+    wait_all(writes)
 
 
 def shards(tokens, cotangent, block_lang, counts, slot_of, ln_gain, w_down, w_up):
@@ -466,13 +469,11 @@
         recv = [exchange(packed[0])]
     inputs = in_vmem(*recv, pair, pair_far) if direct else in_hbm(*recv, pair, pair_far)
 
-    part = vmem_shape(mp_size // 2, shard, width)
-    up_keep, up_send, down_keep, down_send, *kept = pl.pallas_call(
-        functools.partial(weight_grad_kernel, (capacity, mp_size, tile, 1.0 / (block_rows * mp_size), direct)),
+    part = vmem_shape(mp_size // 2, 2, shard, width)
+    scale = 1.0 / (block_rows * mp_size)
+    send, *kept = pl.pallas_call(
+        functools.partial(weight_grad_kernel, (capacity, mp_size, tile, scale, direct)),
         out_shape=(
-            part,
-            part,
-            part,
             part,
             vmem_shape(rows, features),
             vmem_shape(rows, features),
@@ -481,14 +482,14 @@
             vmem_shape(rows, LANES, kind=jnp.float32),
             vmem_shape(features, width),
             vmem_shape(SLAB, features, kind=jnp.float32),
+            vmem_shape(rows, features),
+            vmem_shape(rows, width),
         ),
         in_specs=[VMEM if direct else ANYWHERE] * len(recv) + [ANYWHERE] * 2,
-        out_specs=(VMEM,) * 11,
+        out_specs=(VMEM,) * 10,
         scratch_shapes=[
             pltpu.VMEM((features, width), bf),
             pltpu.VMEM((mp_size, SLAB, features), bf),
-            pltpu.VMEM((rows, features), bf),
-            pltpu.VMEM((rows, width), bf),
             pltpu.SemaphoreType.DMA(()),
             pltpu.SemaphoreType.DMA((3, mp_size)),
             *staging[:1],
@@ -496,70 +497,54 @@
         compiler_params=params(14 + rows // 48),
         name="weight_grads",
     )(*inputs)
+    near = swap(send, 1)
 
     tile = min(256, rows)
     chunk_rows = capacity * block_rows
-    token_parts = pl.pallas_call(
-        functools.partial(token_grad_kernel, tile, chunk_rows, direct),
-        out_shape=[vmem_shape(chunk_rows, features)] * dp_size if direct else [pltpu.HBM((rows, features), bf)],
-        in_specs=[VMEM] * 7,
-        out_specs=[VMEM] * dp_size if direct else [ANYWHERE],
+    keep, *token_parts = pl.pallas_call(
+        functools.partial(token_grad_kernel, (tile, chunk_rows, direct, scale)),
+        out_shape=[
+            part,
+            *([vmem_shape(chunk_rows, features)] * dp_size if direct else [pltpu.HBM((rows, features), bf)]),
+        ],
+        in_specs=[VMEM] * 9,
+        out_specs=[VMEM] * (1 + dp_size) if direct else [VMEM, ANYWHERE],
         scratch_shapes=[] if direct else [pltpu.VMEM((rows, features), bf), pltpu.SemaphoreType.DMA(())],
-        compiler_params=params(4 + rows // 64),
+        compiler_params=params(12 + rows // 64),
         name="token_grads",
     )(*in_vmem(*kept))
 
-    up_near, down_near = swap(up_send, 1), swap(down_send, 1)
-    after = in_vmem(token_parts[0]) if direct else in_hbm(token_parts[0])
-    *through, up_sum = pl.pallas_call(
-        up_add_kernel,
-        out_shape=(*[pltpu.HBM(array.shape, array.dtype) for array in after if not direct], vmem_shape(shard, width)),
-        in_specs=[VMEM] * 2 + [ANYWHERE],
-        out_specs=(*[ANYWHERE for _ in after if not direct], VMEM),
-        input_output_aliases={} if direct else {2: 0},
-        compiler_params=params(4),
-        name="up_add",
-    )(*in_vmem(up_keep, up_near), *after)
-    down_sum, down_own = pl.pallas_call(
-        down_add_kernel,
-        out_shape=(
-            vmem_shape(shard, lang_local, bottleneck),
-            shape(shard, lang_local, bottleneck, kind=jnp.float32),
-        ),
-        in_specs=[VMEM] * 2,
-        out_specs=(VMEM,) * 2,
-        compiler_params=params(12),
-        name="down_add",
-    )(*in_vmem(down_keep, down_near))
-    up_far, down_far = swap(up_sum, 2), swap(down_sum, 2)
+    def add(place, kind, name):
+        return pl.pallas_call(
+            functools.partial(add_kernel, place),
+            out_shape=vmem_shape(2, shard, lang_local, bottleneck, kind=kind),
+            in_specs=[VMEM] * 2,
+            out_specs=VMEM,
+            compiler_params=params(14),
+            name=name,
+        )(*in_vmem(keep, near))
+
+    far = swap(add(1, bf, "far_add"), 2)
+    own_sum = add(0, jnp.float32, "own_add")
     if direct:
         backs = in_vmem(*swap_all(token_parts))
     else:
-        backs = in_hbm(exchange(through[0].reshape(slots, block_rows, features)))
+        backs = in_hbm(exchange(token_parts[0].reshape(slots, block_rows, features)))
     grad_shape = shape(shard, lang_local, bottleneck)
-    grad_up = pl.pallas_call(
-        finish_grad,
-        out_shape=grad_shape,
-        in_specs=[VMEM] * 3,
-        out_specs=VMEM,
-        compiler_params=params(8),
-        name="up_finish",
-    )(*in_hbm(up_keep, up_near, up_far))
-    token_grad, grad_down = pl.pallas_call(
+    token_grad, grad_up, grad_down = pl.pallas_call(
         functools.partial(tail_kernel, (capacity, full, direct)),
-        out_shape=(shape(*tokens.shape), grad_shape),
-        in_specs=[SMEM, ANYWHERE, VMEM] + [VMEM if direct else ANYWHERE] * len(backs),
-        out_specs=(ANYWHERE, ANYWHERE),
+        out_shape=(shape(*tokens.shape), grad_shape, grad_shape),
+        in_specs=[SMEM] + [VMEM] * 2 + [VMEM if direct else ANYWHERE] * len(backs),
+        out_specs=(ANYWHERE,) * 3,
         scratch_shapes=[
-            pltpu.VMEM(grad_shape.shape, jnp.float32),
-            pltpu.VMEM(grad_shape.shape, bf),
+            pltpu.VMEM((2, shard, lang_local, bottleneck), bf),
             pltpu.SemaphoreType.DMA((4,)),
             pltpu.SemaphoreType.DMA((slots,)),
             *([] if direct else [pltpu.VMEM((slots, block_rows, features), bf)]),
         ],
-        compiler_params=params(8 + slots // 8),
+        compiler_params=params(8 + slots // 4),
         name="tail",
-    )(source, *in_hbm(down_own), *in_vmem(down_far), *backs)
+    )(source, *in_vmem(own_sum, far), *backs)
     return (token_grad, grad_down, grad_up)
 
 

time: 103 us -> 97.9 us (0.950)
  Pallas kernels: 19.3 us -> 16 us
  waiting for transfers between devices: 49.8 us -> 47.8 us
    ppermute x14, waiting for transfers between devices: 46.5 us -> 43.7 us  [swap_all(): lax.ppermute(chunk, 'dp', [(i, i ^ offset) for i in range(dp_size)])]
    ppermute x14, starting transfers between devices: 22.7 us -> 25.4 us  [swap_all(): lax.ppermute(chunk, 'dp', [(i, i ^ offset) for i in range(dp_size)])]
    ppermute x6 -> x4, starting transfers between devices: 7.2 us -> 5.34 us  [swap(): return lax.ppermute(array, 'mp', [(i, i ^ bit) for i in range(mp_size)])]
    pallas_call x4 -> x3, Pallas kernels: 6.08 us -> 4.86 us  [the longest x1 3.09 us: shards(): pl.pallas_call(functools.partial(token_grad_kernel, (tile, chunk_rows, di...]
    pallas_call x1, Pallas kernels: 3.57 us -> 2.36 us  [shards(): pl.pallas_call(functools.partial(tail_kernel, (capacity, full, direct)),...]
    ppermute x6 -> x4, waiting for transfers between devices: 3.33 us -> 4.16 us  [swap(): return lax.ppermute(array, 'mp', [(i, i ^ bit) for i in range(mp_size)])]
    unnamed x10 -> x4, local copies, waits for them, and re-layouts: 2.23 us -> 2.22 us
  transfers between devices with their start and end apart: 20 -> 18, of which waited for: 9 -> 8; matrix products, arithmetic and copies ran while one was open for 0% -> 0% of each run, Pallas kernels for 8% -> 6%
where the time goes in v4:
time: 97.9 us; the launch traced here: 97.6 us
  waiting for transfers between devices  47.8 us (49%)
  starting transfers between devices  30.8 us (31%)
  Pallas kernels  16 us (16%)
  local copies, waits for them, and re-layouts  2.24 us (2%)
    ppermute x14, waiting for transfers between devices, swap_all(): lax.ppermute(chunk, 'dp', [(i, i ^ offset) for i in range(dp_size)])  43.7 us
    ppermute x14, starting transfers between devices, swap_all(): lax.ppermute(chunk, 'dp', [(i, i ^ offset) for i in range(dp_size)])  25.4 us
    pallas_call x1, Pallas kernels, shards(): pl.pallas_call(functools.partial(weight_grad_kernel, (capacity, mp_size,...  5.67 us
    ppermute x4, starting transfers between devices, swap(): return lax.ppermute(array, 'mp', [(i, i ^ bit) for i in range(mp_size)])  5.34 us
    ppermute x4, waiting for transfers between devices, swap(): return lax.ppermute(array, 'mp', [(i, i ^ bit) for i in range(mp_size)])  4.16 us
    pallas_call x1, Pallas kernels, shards(): pl.pallas_call(functools.partial(token_grad_kernel, (tile, chunk_rows, di...  3.09 us
    pallas_call x1, Pallas kernels, shards(): pl.pallas_call(functools.partial(tail_kernel, (capacity, full, direct)),...  2.36 us
    pallas_call x1, Pallas kernels, shards(): pl.pallas_call(functools.partial(pack_kernel, (dp_size, capacity, lang_lo...  2.31 us
  transfers between devices with their start and end apart: 18, of which 8 were waited for; matrix products, arithmetic and copies ran while one was open for 0% of the time, Pallas kernels for 6%

profile of v4, /device:TPU:0, one launch (start us, length us, event | category | flops | bytes accessed | tf_op | source)
XLA Modules:
  0.0 97.6 jit_solution(598187143795911920)
XLA Ops:
  0.6 1.1 %copy.11 = bf16[32,8,2,512]{3,1,2,0:T(8,128)(2,1)S(1)} copy(bf16[32,8,2,512]{3,2,1,0:T(2,128)(2,1)} %bitcast.8) | data formatting | bytes 1048576
  1.8 1.1 %copy.12 = bf16[32,8,2,512]{3,1,2,0:T(8,128)(2,1)S(1)} copy(bf16[32,8,2,512]{3,2,1,0:T(2,128)(2,1)} %bitcast.9) | data formatting | bytes 1048576
  3.5 2.3 %pack.1 = (bf16[16,8320]{1,0:T(8,128)(2,1)S(1)}, bf16[16,8320]{1,0:T(8,128)(2,1)S(1)}, bf16[16,8320]{1,0:T(8,128)(2,1)S(1)}, bf16[16,8320]{1,0:T(8,128)(2,1)S(1)...) custom-call(s32[16]{0:T(128)} %lang_hbm.1, ...), custom_call_target="tpu_custom_call" | custom-call | tf_op jit(solution)/shard_map/pack/pallas_call | solution.py:431
  6.6 2.9 %collective-permute-start.8 = (bf16[1056,1024]{1,0:T(8,128)(2,1)S(1)}, bf16[1056,1024]{1,0:T(8,128)(2,1)S(1)}, u32[]{:S(2)}, u32[]{:S(2)}) collective-permute-start(bf16[1056,1024]{1,0:T(8,128)(2,1)S(1)} %pair.1.refs_8_), channel_id=1, source_target_pairs={{0,2},{1,3},{2,0},{3,1},{4,6},{5,7},{6,4},{7,5},{8,10},{9,11},{10,... | collective-permute-start | bytes 6488072 | tf_op jit(solution)/shard_map/ppermute | solution.py:417
  9.6 2.6 %collective-permute-start = (bf16[16,8320]{1,0:T(8,128)(2,1)S(1)}, bf16[16,8320]{1,0:T(8,128)(2,1)S(1)}, u32[]{:S(2)}, u32[]{:S(2)}) collective-permute-start(bf16[16,8320]{1,0:T(8,128)(2,1)S(1)} %get-tuple-element.36), channel_id=1, source_target_pairs={{0,16},{4,20},{8,24},{12,28},{16,0},{20,4},{24,8},{28,12},{1,17},{... | collective-permute-start | bytes 798728 | tf_op jit(solution)/shard_map/ppermute | solution.py:424
  12.2 1.5 %collective-permute-start.1 = (bf16[16,8320]{1,0:T(8,128)(2,1)S(1)}, bf16[16,8320]{1,0:T(8,128)(2,1)S(1)}, u32[]{:S(2)}, u32[]{:S(2)}) collective-permute-start(bf16[16,8320]{1,0:T(8,128)(2,1)S(1)} %get-tuple-element.37), channel_id=1, source_target_pairs={{0,4},{4,0},{8,12},{12,8},{16,20},{20,16},{24,28},{28,24},{1,5},{5... | collective-permute-start | bytes 798728 | tf_op jit(solution)/shard_map/ppermute | solution.py:424
  14.0 1.6 %collective-permute-start.3 = (bf16[16,8320]{1,0:T(8,128)(2,1)S(1)}, bf16[16,8320]{1,0:T(8,128)(2,1)S(1)}, u32[]{:S(2)}, u32[]{:S(2)}) collective-permute-start(bf16[16,8320]{1,0:T(8,128)(2,1)S(1)} %get-tuple-element.39), channel_id=1, source_target_pairs={{0,8},{4,12},{8,0},{12,4},{16,24},{20,28},{24,16},{28,20},{1,9},{5... | collective-permute-start | bytes 798728 | tf_op jit(solution)/shard_map/ppermute | solution.py:424
  15.5 15.6 %collective-permute-done.refs_1_ = bf16[16,8320]{1,0:T(8,128)(2,1)S(1)} collective-permute-done((bf16[16,8320]{1,0:T(8,128)(2,1)S(1)}, bf16[16,8320]{1,0:T(8,128)(2,1)S(1)}, u32[]{:S(2)}, u32[]{:S(2)}) %collective-permute-start) | collective-permute-done | bytes 266272 | tf_op jit(solution)/shard_map/ppermute | solution.py:424
  31.2 2.5 %collective-permute-start.4 = (bf16[16,8320]{1,0:T(8,128)(2,1)S(1)}, bf16[16,8320]{1,0:T(8,128)(2,1)S(1)}, u32[]{:S(2)}, u32[]{:S(2)}) collective-permute-start(bf16[16,8320]{1,0:T(8,128)(2,1)S(1)} %get-tuple-element.40), channel_id=1, source_target_pairs={{0,24},{4,28},{8,16},{12,20},{16,8},{20,12},{24,0},{28,4},{1,25},{... | collective-permute-start | bytes 798728 | tf_op jit(solution)/shard_map/ppermute | solution.py:424
  33.6 9.9 %collective-permute-done.2.refs_3_ = bf16[16,8320]{1,0:T(8,128)(2,1)S(1)} collective-permute-done((bf16[16,8320]{1,0:T(8,128)(2,1)S(1)}, bf16[16,8320]{1,0:T(8,128)(2,1)S(1)}, u32[]{:S(2)}, u32[]{:S(2)}) %collective-permute-start.2) | collective-permute-done | bytes 266272 | tf_op jit(solution)/shard_map/ppermute | solution.py:424
  43.6 2.4 %collective-permute-start.6 = (bf16[16,8320]{1,0:T(8,128)(2,1)S(1)}, bf16[16,8320]{1,0:T(8,128)(2,1)S(1)}, u32[]{:S(2)}, u32[]{:S(2)}) collective-permute-start(bf16[16,8320]{1,0:T(8,128)(2,1)S(1)} %get-tuple-element.42), channel_id=1, source_target_pairs={{0,28},{4,24},{8,20},{12,16},{16,12},{20,8},{24,4},{28,0},{1,29},{... | collective-permute-start | bytes 798728 | tf_op jit(solution)/shard_map/ppermute | solution.py:424
  46.0 7.8 %collective-permute-done.5.refs_6_ = bf16[16,8320]{1,0:T(8,128)(2,1)S(1)} collective-permute-done((bf16[16,8320]{1,0:T(8,128)(2,1)S(1)}, bf16[16,8320]{1,0:T(8,128)(2,1)S(1)}, u32[]{:S(2)}, u32[]{:S(2)}) %collective-permute-start.5) | collective-permute-done | bytes 266272 | tf_op jit(solution)/shard_map/ppermute | solution.py:424
  53.8 3.1 %collective-permute-done.8.refs_9_ = bf16[1056,1024]{1,0:T(8,128)(2,1)S(1)} collective-permute-done((bf16[1056,1024]{1,0:T(8,128)(2,1)S(1)}, bf16[1056,1024]{1,0:T(8,128)(2,1)S(1)}, u32[]{:S(2)}, u32[]{:S(2)}) %collective-permute-start.8) | collective-permute-done | bytes 2162720 | tf_op jit(solution)/shard_map/ppermute | solution.py:417
  56.9 5.7 %weight_grads.1 = (bf16[2,2,256,1024]{3,2,1,0:T(8,128)(2,1)S(1)}, bf16[512,1024]{1,0:T(8,128)(2,1)S(1)}, bf16[512,1024]{1,0:T(8,128)(2,1)S(1)}, bf16[512,1024]{1...) custom-call(bf16[16,8320]{1,0:T(8,128)(2,1)S(1)} %get-tuple-element., ...), custom_call_target="tpu_custom_call" | custom-call | tf_op jit(solution)/shard_map/weight_grads/pallas_call | solution.py:474
  62.7 3.1 %token_grads.1 = (bf16[2,2,256,1024]{3,2,1,0:T(8,128)(2,1)S(1)}, bf16[64,1024]{1,0:T(8,128)(2,1)S(1)}, bf16[64,1024]{1,0:T(8,128)(2,1)S(1)}, bf16[64,1024]{1,0:T...) custom-call(bf16[512,1024]{1,0:T(8,128)(2,1)S(1)} %get-tuple-element, ...), custom_call_target="tpu_custom_call" | custom-call | tf_op jit(solution)/shard_map/token_grads/pallas_call | solution.py:504
  65.8 1.0 %collective-permute-done.9.near_ref = bf16[2,2,256,1024]{3,2,1,0:T(8,128)(2,1)S(1)} collective-permute-done((bf16[2,2,256,1024]{3,2,1,0:T(8,128)(2,1)S(1)}, bf16[2,2,256,1024]{3,2,1,0:T(8,128)(2,1)S(1)}, u32[]{:S(2)}, u32[]{:S(2)}) %collective-permute-start.9) | collective-permute-done | bytes 2097184 | tf_op jit(solution)/shard_map/ppermute | solution.py:417
  66.8 1.2 %far_add.1 = bf16[2,256,2,512]{3,2,1,0:T(2,128)(2,1)S(1)} custom-call(bf16[2,2,256,1024]{3,2,1,0:T(8,128)(2,1)S(1)} %get-tuple-element.52.keep_ref, bf16[2,2,256,1024]{3,2,1,0:T(8,128)(2,1)S(1)} %collective-permute-done.9.near_ref), custom_call_target="tpu_custom_call" | custom-call | tf_op jit(solution)/shard_map/far_add/pallas_call | solution.py:518
  68.0 1.8 %collective-permute-start.10 = (bf16[2,256,2,512]{3,2,1,0:T(2,128)(2,1)S(1)}, bf16[2,256,2,512]{3,2,1,0:T(2,128)(2,1)S(1)}, u32[]{:S(2)}, u32[]{:S(2)}) collective-permute-start(bf16[2,256,2,512]{3,2,1,0:T(2,128)(2,1)S(1)} %far_add.1), channel_id=1, source_target_pairs={{0,2},{1,3},{2,0},{3,1},{4,6},{5,7},{6,4},{7,5},{8,10},{9,11},{10,... | collective-permute-start | bytes 3145736 | tf_op jit(solution)/shard_map/ppermute | solution.py:417
  69.9 4.1 %collective-permute-start.11 = (bf16[64,1024]{1,0:T(8,128)(2,1)S(1)}, bf16[64,1024]{1,0:T(8,128)(2,1)S(1)}, u32[]{:S(2)}, u32[]{:S(2)}) collective-permute-start(bf16[64,1024]{1,0:T(8,128)(2,1)S(1)} %get-tuple-element.55), channel_id=1, source_target_pairs={{0,16},{4,20},{8,24},{12,28},{16,0},{20,4},{24,8},{28,12},{1,17},{... | collective-permute-start | bytes 393224 | tf_op jit(solution)/shard_map/ppermute | solution.py:424
  76.3 6.9 %collective-permute-done.11.refs_1_ = bf16[64,1024]{1,0:T(8,128)(2,1)S(1)} collective-permute-done((bf16[64,1024]{1,0:T(8,128)(2,1)S(1)}, bf16[64,1024]{1,0:T(8,128)(2,1)S(1)}, u32[]{:S(2)}, u32[]{:S(2)}) %collective-permute-start.11) | collective-permute-done | bytes 131104 | tf_op jit(solution)/shard_map/ppermute | solution.py:424
  83.2 3.2 %collective-permute-start.15 = (bf16[64,1024]{1,0:T(8,128)(2,1)S(1)}, bf16[64,1024]{1,0:T(8,128)(2,1)S(1)}, u32[]{:S(2)}, u32[]{:S(2)}) collective-permute-start(bf16[64,1024]{1,0:T(8,128)(2,1)S(1)} %get-tuple-element.59), channel_id=1, source_target_pairs={{0,24},{4,28},{8,16},{12,20},{16,8},{20,12},{24,0},{28,4},{1,25},{... | collective-permute-start | bytes 393224 | tf_op jit(solution)/shard_map/ppermute | solution.py:424
  86.5 5.0 %collective-permute-start.17 = (bf16[64,1024]{1,0:T(8,128)(2,1)S(1)}, bf16[64,1024]{1,0:T(8,128)(2,1)S(1)}, u32[]{:S(2)}, u32[]{:S(2)}) collective-permute-start(bf16[64,1024]{1,0:T(8,128)(2,1)S(1)} %get-tuple-element.61), channel_id=1, source_target_pairs={{0,28},{4,24},{8,20},{12,16},{16,12},{20,8},{24,4},{28,0},{1,29},{... | collective-permute-start | bytes 393224 | tf_op jit(solution)/shard_map/ppermute | solution.py:424
  92.0 3.2 %collective-permute-done.16.refs_6_ = bf16[64,1024]{1,0:T(8,128)(2,1)S(1)} collective-permute-done((bf16[64,1024]{1,0:T(8,128)(2,1)S(1)}, bf16[64,1024]{1,0:T(8,128)(2,1)S(1)}, u32[]{:S(2)}, u32[]{:S(2)}) %collective-permute-start.16) | collective-permute-done | bytes 131104 | tf_op jit(solution)/shard_map/ppermute | solution.py:424
  95.3 2.4 %tail.1 = (bf16[16,32,1024]{2,1,0:T(8,128)(2,1)}, bf16[256,2,512]{2,1,0:T(2,128)(2,1)}, bf16[256,2,512]{2,1,0:T(2,128)(2,1)}) custom-call(s32[16]{0:T(128)S(1)} %get-tuple-element.34.after_ref.source_ref, f32[2,256,2,512]{3,2,1,0:T(2,128)S(1)} %own_add.1.own_ref, bf16[2,256,2,512]{3,2,1,0:T(2,128)(2,1)S(1)} %collective-permute-done.10.far_ref, ...), custom_call_target="tpu_custom_call" | custom-call | tf_op jit(solution)/shard_map/tail/pallas_call | solution.py:534
  (26 shorter events, 4.8 us)
Async XLA Ops:
  0.6 2.3 %copy-start = (bf16[256,2]{0,1:T(2,128)(2,1)S(1)}, bf16[256,2]{0,1:T(2,128)(2,1)}, u32[]{:S(2)}) copy-start(bf16[256,2]{0,1:T(2,128)(2,1)} %param.13) | copy-start | bytes 3076
  3.0 2.9 %collective-permute-start.7 = (bf16[528,1024]{1,0:T(8,128)(2,1)S(1)}, bf16[528,1024]{1,0:T(8,128)(2,1)S(1)}, u32[]{:S(2)}, u32[]{:S(2)}) collective-permute-start(bf16[528,1024]{1,0:T(8,128)(2,1)S(1)} %pad_maximum_fusion.own_hbm), channel_id=1, source_target_pairs={{0,1},{1,0},{2,3},{3,2},{4,5},{5,4},{6,7},{7,6},{8,9},{9,8},{10,11... | collective-permute-start | bytes 3244040 | tf_op jit(solution)/shard_map/ppermute | solution.py:417
  6.6 50.3 %collective-permute-start.8 = (bf16[1056,1024]{1,0:T(8,128)(2,1)S(1)}, bf16[1056,1024]{1,0:T(8,128)(2,1)S(1)}, u32[]{:S(2)}, u32[]{:S(2)}) collective-permute-start(bf16[1056,1024]{1,0:T(8,128)(2,1)S(1)} %pair.1.refs_8_), channel_id=1, source_target_pairs={{0,2},{1,3},{2,0},{3,1},{4,6},{5,7},{6,4},{7,5},{8,10},{9,11},{10,... | collective-permute-start | bytes 6488072 | tf_op jit(solution)/shard_map/ppermute | solution.py:417
  9.6 21.6 %collective-permute-start = (bf16[16,8320]{1,0:T(8,128)(2,1)S(1)}, bf16[16,8320]{1,0:T(8,128)(2,1)S(1)}, u32[]{:S(2)}, u32[]{:S(2)}) collective-permute-start(bf16[16,8320]{1,0:T(8,128)(2,1)S(1)} %get-tuple-element.36), channel_id=1, source_target_pairs={{0,16},{4,20},{8,24},{12,28},{16,0},{20,4},{24,8},{28,12},{1,17},{... | collective-permute-start | bytes 798728 | tf_op jit(solution)/shard_map/ppermute | solution.py:424
  12.2 21.5 %collective-permute-start.1 = (bf16[16,8320]{1,0:T(8,128)(2,1)S(1)}, bf16[16,8320]{1,0:T(8,128)(2,1)S(1)}, u32[]{:S(2)}, u32[]{:S(2)}) collective-permute-start(bf16[16,8320]{1,0:T(8,128)(2,1)S(1)} %get-tuple-element.37), channel_id=1, source_target_pairs={{0,4},{4,0},{8,12},{12,8},{16,20},{20,16},{24,28},{28,24},{1,5},{5... | collective-permute-start | bytes 798728 | tf_op jit(solution)/shard_map/ppermute | solution.py:424
  13.7 29.9 %collective-permute-start.2 = (bf16[16,8320]{1,0:T(8,128)(2,1)S(1)}, bf16[16,8320]{1,0:T(8,128)(2,1)S(1)}, u32[]{:S(2)}, u32[]{:S(2)}) collective-permute-start(bf16[16,8320]{1,0:T(8,128)(2,1)S(1)} %get-tuple-element.38), channel_id=1, source_target_pairs={{0,20},{4,16},{8,28},{12,24},{16,4},{20,0},{24,12},{28,8},{1,21},{... | collective-permute-start | bytes 798728 | tf_op jit(solution)/shard_map/ppermute | solution.py:424
  14.0 32.0 %collective-permute-start.3 = (bf16[16,8320]{1,0:T(8,128)(2,1)S(1)}, bf16[16,8320]{1,0:T(8,128)(2,1)S(1)}, u32[]{:S(2)}, u32[]{:S(2)}) collective-permute-start(bf16[16,8320]{1,0:T(8,128)(2,1)S(1)} %get-tuple-element.39), channel_id=1, source_target_pairs={{0,8},{4,12},{8,0},{12,4},{16,24},{20,28},{24,16},{28,20},{1,9},{5... | collective-permute-start | bytes 798728 | tf_op jit(solution)/shard_map/ppermute | solution.py:424
  31.2 14.8 %collective-permute-start.4 = (bf16[16,8320]{1,0:T(8,128)(2,1)S(1)}, bf16[16,8320]{1,0:T(8,128)(2,1)S(1)}, u32[]{:S(2)}, u32[]{:S(2)}) collective-permute-start(bf16[16,8320]{1,0:T(8,128)(2,1)S(1)} %get-tuple-element.40), channel_id=1, source_target_pairs={{0,24},{4,28},{8,16},{12,20},{16,8},{20,12},{24,0},{28,4},{1,25},{... | collective-permute-start | bytes 798728 | tf_op jit(solution)/shard_map/ppermute | solution.py:424
  33.6 20.2 %collective-permute-start.5 = (bf16[16,8320]{1,0:T(8,128)(2,1)S(1)}, bf16[16,8320]{1,0:T(8,128)(2,1)S(1)}, u32[]{:S(2)}, u32[]{:S(2)}) collective-permute-start(bf16[16,8320]{1,0:T(8,128)(2,1)S(1)} %get-tuple-element.41), channel_id=1, source_target_pairs={{0,12},{4,8},{8,4},{12,0},{16,28},{20,24},{24,20},{28,16},{1,13},{... | collective-permute-start | bytes 798728 | tf_op jit(solution)/shard_map/ppermute | solution.py:424
  43.6 10.3 %collective-permute-start.6 = (bf16[16,8320]{1,0:T(8,128)(2,1)S(1)}, bf16[16,8320]{1,0:T(8,128)(2,1)S(1)}, u32[]{:S(2)}, u32[]{:S(2)}) collective-permute-start(bf16[16,8320]{1,0:T(8,128)(2,1)S(1)} %get-tuple-element.42), channel_id=1, source_target_pairs={{0,28},{4,24},{8,20},{12,16},{16,12},{20,8},{24,4},{28,0},{1,29},{... | collective-permute-start | bytes 798728 | tf_op jit(solution)/shard_map/ppermute | solution.py:424
  62.6 4.2 %collective-permute-start.9 = (bf16[2,2,256,1024]{3,2,1,0:T(8,128)(2,1)S(1)}, bf16[2,2,256,1024]{3,2,1,0:T(8,128)(2,1)S(1)}, u32[]{:S(2)}, u32[]{:S(2)}) collective-permute-start(bf16[2,2,256,1024]{3,2,1,0:T(8,128)(2,1)S(1)} %get-tuple-element.53), channel_id=1, source_target_pairs={{0,1},{1,0},{2,3},{3,2},{4,5},{5,4},{6,7},{7,6},{8,9},{9,8},{10,11... | collective-permute-start | bytes 6291464 | tf_op jit(solution)/shard_map/ppermute | solution.py:417
  68.0 27.2 %collective-permute-start.10 = (bf16[2,256,2,512]{3,2,1,0:T(2,128)(2,1)S(1)}, bf16[2,256,2,512]{3,2,1,0:T(2,128)(2,1)S(1)}, u32[]{:S(2)}, u32[]{:S(2)}) collective-permute-start(bf16[2,256,2,512]{3,2,1,0:T(2,128)(2,1)S(1)} %far_add.1), channel_id=1, source_target_pairs={{0,2},{1,3},{2,0},{3,1},{4,6},{5,7},{6,4},{7,5},{8,10},{9,11},{10,... | collective-permute-start | bytes 3145736 | tf_op jit(solution)/shard_map/ppermute | solution.py:417
  69.9 13.3 %collective-permute-start.11 = (bf16[64,1024]{1,0:T(8,128)(2,1)S(1)}, bf16[64,1024]{1,0:T(8,128)(2,1)S(1)}, u32[]{:S(2)}, u32[]{:S(2)}) collective-permute-start(bf16[64,1024]{1,0:T(8,128)(2,1)S(1)} %get-tuple-element.55), channel_id=1, source_target_pairs={{0,16},{4,20},{8,24},{12,28},{16,0},{20,4},{24,8},{28,12},{1,17},{... | collective-permute-start | bytes 393224 | tf_op jit(solution)/shard_map/ppermute | solution.py:424
  73.9 12.4 %collective-permute-start.12 = (bf16[64,1024]{1,0:T(8,128)(2,1)S(1)}, bf16[64,1024]{1,0:T(8,128)(2,1)S(1)}, u32[]{:S(2)}, u32[]{:S(2)}) collective-permute-start(bf16[64,1024]{1,0:T(8,128)(2,1)S(1)} %get-tuple-element.56), channel_id=1, source_target_pairs={{0,4},{4,0},{8,12},{12,8},{16,20},{20,16},{24,28},{28,24},{1,5},{5... | collective-permute-start | bytes 393224 | tf_op jit(solution)/shard_map/ppermute | solution.py:424
  74.4 12.1 %collective-permute-start.13 = (bf16[64,1024]{1,0:T(8,128)(2,1)S(1)}, bf16[64,1024]{1,0:T(8,128)(2,1)S(1)}, u32[]{:S(2)}, u32[]{:S(2)}) collective-permute-start(bf16[64,1024]{1,0:T(8,128)(2,1)S(1)} %get-tuple-element.57), channel_id=1, source_target_pairs={{0,20},{4,16},{8,28},{12,24},{16,4},{20,0},{24,12},{28,8},{1,21},{... | collective-permute-start | bytes 393224 | tf_op jit(solution)/shard_map/ppermute | solution.py:424
  75.4 16.6 %collective-permute-start.14 = (bf16[64,1024]{1,0:T(8,128)(2,1)S(1)}, bf16[64,1024]{1,0:T(8,128)(2,1)S(1)}, u32[]{:S(2)}, u32[]{:S(2)}) collective-permute-start(bf16[64,1024]{1,0:T(8,128)(2,1)S(1)} %get-tuple-element.58), channel_id=1, source_target_pairs={{0,8},{4,12},{8,0},{12,4},{16,24},{20,28},{24,16},{28,20},{1,9},{5... | collective-permute-start | bytes 393224 | tf_op jit(solution)/shard_map/ppermute | solution.py:424
  83.2 8.8 %collective-permute-start.15 = (bf16[64,1024]{1,0:T(8,128)(2,1)S(1)}, bf16[64,1024]{1,0:T(8,128)(2,1)S(1)}, u32[]{:S(2)}, u32[]{:S(2)}) collective-permute-start(bf16[64,1024]{1,0:T(8,128)(2,1)S(1)} %get-tuple-element.59), channel_id=1, source_target_pairs={{0,24},{4,28},{8,16},{12,20},{16,8},{20,12},{24,0},{28,4},{1,25},{... | collective-permute-start | bytes 393224 | tf_op jit(solution)/shard_map/ppermute | solution.py:424
  86.4 8.9 %collective-permute-start.16 = (bf16[64,1024]{1,0:T(8,128)(2,1)S(1)}, bf16[64,1024]{1,0:T(8,128)(2,1)S(1)}, u32[]{:S(2)}, u32[]{:S(2)}) collective-permute-start(bf16[64,1024]{1,0:T(8,128)(2,1)S(1)} %get-tuple-element.60), channel_id=1, source_target_pairs={{0,12},{4,8},{8,4},{12,0},{16,28},{20,24},{24,20},{28,16},{1,13},{... | collective-permute-start | bytes 393224 | tf_op jit(solution)/shard_map/ppermute | solution.py:424
  86.5 8.8 %collective-permute-start.17 = (bf16[64,1024]{1,0:T(8,128)(2,1)S(1)}, bf16[64,1024]{1,0:T(8,128)(2,1)S(1)}, u32[]{:S(2)}, u32[]{:S(2)}) collective-permute-start(bf16[64,1024]{1,0:T(8,128)(2,1)S(1)} %get-tuple-element.61), channel_id=1, source_target_pairs={{0,28},{4,24},{8,20},{12,16},{16,12},{20,8},{24,4},{28,0},{1,29},{... | collective-permute-start | bytes 393224 | tf_op jit(solution)/shard_map/ppermute | solution.py:424

commit v5 on v4

--- a/solution.py
+++ b/solution.py
@@ -29,6 +29,15 @@
 def wait_all(copies):
     for copy in copies:
         copy.wait()
+
+
+def load_kernel(down_hbm, up_hbm, down_ref, up_ref, sems):
+    copies = [
+        pltpu.make_async_copy(src, dst, sems.at[n])
+        for n, (src, dst) in enumerate(((down_hbm, down_ref), (up_hbm, up_ref)))
+    ]
+    start_all(copies)
+    wait_all(copies)
 
 
 def pair_kernel(after_ref, own_hbm, core_hbm, out_ref, sems):
@@ -217,10 +226,9 @@
     start_all(then)
     start_all(later)
     wait_all(first)
-    gain = gain_buf[0].astype(jnp.float32)
-    for offset in range(1, mp_size):
-        gain = gain + gain_buf[offset].astype(jnp.float32)
-    gain_ref[...] = gain
+    for offset in range(mp_size):
+        here = pl.ds(pl.multiple_of((lax.axis_index("mp") ^ offset) * shard, shard), shard)
+        gain_ref[:, here] = gain_buf[offset, :, pl.ds(0, shard)].astype(jnp.float32)
     tile_chunks = tile // (groups * SLAB)
     per_block = groups // capacity
 
@@ -372,7 +380,8 @@
                     pl.when(source_ref[slot] >= 0)(store(slot, buf.at[slot]).start)
     writes = []
     for kind, grad_hbm in enumerate(grad_hbms):
-        grad[kind] = (own_ref[kind] + far_ref[kind].astype(jnp.float32)).astype(grad.dtype)
+        total = own_ref[kind] + far_ref[kind].astype(jnp.float32).reshape(grad.shape[1:])
+        grad[kind] = total.astype(grad.dtype)
         writes.append(pltpu.make_async_copy(grad.at[kind], grad_hbm, sems.at[2 + kind]))
         writes[-1].start()
     if full:
@@ -447,10 +456,17 @@
         name="pack",
     )(*in_hbm(block_lang, counts, slot_of, tokens, cotangent))
 
-    gain_part = lax.dynamic_update_slice(
-        jnp.zeros((SLAB, features), bf), ln_gain.T, (0, lax.axis_index("mp").astype(jnp.int32) * shard)
-    )
-    own = jnp.concatenate([w_down.reshape(shard, width), w_up.reshape(shard, width), gain_part], axis=0)
+    down_raw, up_raw = pl.pallas_call(
+        load_kernel,
+        out_shape=(vmem_shape(*w_down.shape), vmem_shape(*w_up.shape)),
+        in_specs=[ANYWHERE] * 2,
+        out_specs=(VMEM if resident else ANYWHERE,) * 2,
+        scratch_shapes=[pltpu.SemaphoreType.DMA((2,))],
+        compiler_params=params(2),
+        name="load",
+    )(*in_hbm(w_down, w_up))
+    gain_part = jnp.pad(ln_gain.T, ((0, SLAB - lang_local), (0, width - shard)))
+    own = jnp.concatenate([down_raw.reshape(shard, width), up_raw.reshape(shard, width), gain_part], axis=0)
     core = swap(own, 1)
     pair = pl.pallas_call(
         pair_kernel,
@@ -514,18 +530,18 @@
         name="token_grads",
     )(*in_vmem(*kept))
 
-    def add(place, kind, name):
+    def add(place, extent, kind, name):
         return pl.pallas_call(
             functools.partial(add_kernel, place),
-            out_shape=vmem_shape(2, shard, lang_local, bottleneck, kind=kind),
+            out_shape=vmem_shape(2, *extent, kind=kind),
             in_specs=[VMEM] * 2,
             out_specs=VMEM,
             compiler_params=params(14),
             name=name,
         )(*in_vmem(keep, near))
 
-    far = swap(add(1, bf, "far_add"), 2)
-    own_sum = add(0, jnp.float32, "own_add")
+    far = swap(add(1, (shard, width), bf, "far_add"), 2)
+    own_sum = add(0, (shard, lang_local, bottleneck), jnp.float32, "own_add")
     if direct:
         backs = in_vmem(*swap_all(token_parts))
     else:

time: 97.9 us -> 96.2 us (0.983)
  local copies, waits for them, and re-layouts: 2.24 us -> 0.14 us
    unnamed x4, local copies, waits for them, and re-layouts: 2.22 us -> 0.14 us
    pallas_call x0 -> x1, Pallas kernels: none -> 1.22 us  [shards(): pl.pallas_call(load_kernel, out_shape=(vmem_shape(*w_down.shape), vmem_sh...]
where the time goes in v5:
time: 96.2 us; the launch traced here: 96.1 us
  waiting for transfers between devices  47.8 us (50%)
  starting transfers between devices  30.7 us (32%)
  Pallas kernels  16.5 us (17%)
    ppermute x14, waiting for transfers between devices, swap_all(): lax.ppermute(chunk, 'dp', [(i, i ^ offset) for i in range(dp_size)])  43.7 us
    ppermute x14, starting transfers between devices, swap_all(): lax.ppermute(chunk, 'dp', [(i, i ^ offset) for i in range(dp_size)])  25.4 us
    pallas_call x1, Pallas kernels, shards(): pl.pallas_call(functools.partial(weight_grad_kernel, (capacity, mp_size,...  5.66 us
    ppermute x4, starting transfers between devices, swap(): return lax.ppermute(array, 'mp', [(i, i ^ bit) for i in range(mp_size)])  5.33 us
    ppermute x4, waiting for transfers between devices, swap(): return lax.ppermute(array, 'mp', [(i, i ^ bit) for i in range(mp_size)])  4.15 us
    pallas_call x1, Pallas kernels, shards(): pl.pallas_call(functools.partial(token_grad_kernel, (tile, chunk_rows, di...  3.1 us
    pallas_call x1, Pallas kernels, shards(): pl.pallas_call(functools.partial(tail_kernel, (capacity, full, direct)),...  2.66 us
    pallas_call x1, Pallas kernels, shards(): pl.pallas_call(functools.partial(pack_kernel, (dp_size, capacity, lang_lo...  2.31 us
  transfers between devices with their start and end apart: 18, of which 8 were waited for; matrix products, arithmetic and copies ran while one was open for 0% of the time, Pallas kernels for 6%

profile of v5, /device:TPU:0, one launch (start us, length us, event | category | flops | bytes accessed | tf_op | source)
XLA Modules:
  0.0 96.1 jit_solution(10562381114823698667)
XLA Ops:
  0.6 1.2 %load.1 = (bf16[256,2,512]{2,1,0:T(2,128)(2,1)S(1)}, bf16[256,2,512]{2,1,0:T(2,128)(2,1)S(1)}) custom-call(bf16[256,2,512]{2,1,0:T(2,128)(2,1)} %down_hbm.1, bf16[256,2,512]{2,1,0:T(2,128)(2,1)} %up_hbm.1), custom_call_target="tpu_custom_call" | custom-call | tf_op jit(solution)/shard_map/load/pallas_call | solution.py:459
  2.6 2.3 %pack.1 = (bf16[16,8320]{1,0:T(8,128)(2,1)S(1)}, bf16[16,8320]{1,0:T(8,128)(2,1)S(1)}, bf16[16,8320]{1,0:T(8,128)(2,1)S(1)}, bf16[16,8320]{1,0:T(8,128)(2,1)S(1)...) custom-call(s32[16]{0:T(128)} %lang_hbm.1, ...), custom_call_target="tpu_custom_call" | custom-call | tf_op jit(solution)/shard_map/pack/pallas_call | solution.py:440
  5.8 2.9 %collective-permute-start.8 = (bf16[1056,1024]{1,0:T(8,128)(2,1)S(1)}, bf16[1056,1024]{1,0:T(8,128)(2,1)S(1)}, u32[]{:S(2)}, u32[]{:S(2)}) collective-permute-start(bf16[1056,1024]{1,0:T(8,128)(2,1)S(1)} %pair.1.refs_8_), channel_id=1, source_target_pairs={{0,2},{1,3},{2,0},{3,1},{4,6},{5,7},{6,4},{7,5},{8,10},{9,11},{10,... | collective-permute-start | bytes 6488072 | tf_op jit(solution)/shard_map/ppermute | solution.py:426
  8.7 2.6 %collective-permute-start = (bf16[16,8320]{1,0:T(8,128)(2,1)S(1)}, bf16[16,8320]{1,0:T(8,128)(2,1)S(1)}, u32[]{:S(2)}, u32[]{:S(2)}) collective-permute-start(bf16[16,8320]{1,0:T(8,128)(2,1)S(1)} %get-tuple-element.38), channel_id=1, source_target_pairs={{0,16},{4,20},{8,24},{12,28},{16,0},{20,4},{24,8},{28,12},{1,17},{... | collective-permute-start | bytes 798728 | tf_op jit(solution)/shard_map/ppermute | solution.py:433
  11.3 1.5 %collective-permute-start.1 = (bf16[16,8320]{1,0:T(8,128)(2,1)S(1)}, bf16[16,8320]{1,0:T(8,128)(2,1)S(1)}, u32[]{:S(2)}, u32[]{:S(2)}) collective-permute-start(bf16[16,8320]{1,0:T(8,128)(2,1)S(1)} %get-tuple-element.39), channel_id=1, source_target_pairs={{0,4},{4,0},{8,12},{12,8},{16,20},{20,16},{24,28},{28,24},{1,5},{5... | collective-permute-start | bytes 798728 | tf_op jit(solution)/shard_map/ppermute | solution.py:433
  13.1 1.6 %collective-permute-start.3 = (bf16[16,8320]{1,0:T(8,128)(2,1)S(1)}, bf16[16,8320]{1,0:T(8,128)(2,1)S(1)}, u32[]{:S(2)}, u32[]{:S(2)}) collective-permute-start(bf16[16,8320]{1,0:T(8,128)(2,1)S(1)} %get-tuple-element.41), channel_id=1, source_target_pairs={{0,8},{4,12},{8,0},{12,4},{16,24},{20,28},{24,16},{28,20},{1,9},{5... | collective-permute-start | bytes 798728 | tf_op jit(solution)/shard_map/ppermute | solution.py:433
  14.7 15.6 %collective-permute-done.refs_1_ = bf16[16,8320]{1,0:T(8,128)(2,1)S(1)} collective-permute-done((bf16[16,8320]{1,0:T(8,128)(2,1)S(1)}, bf16[16,8320]{1,0:T(8,128)(2,1)S(1)}, u32[]{:S(2)}, u32[]{:S(2)}) %collective-permute-start) | collective-permute-done | bytes 266272 | tf_op jit(solution)/shard_map/ppermute | solution.py:433
  30.3 2.5 %collective-permute-start.4 = (bf16[16,8320]{1,0:T(8,128)(2,1)S(1)}, bf16[16,8320]{1,0:T(8,128)(2,1)S(1)}, u32[]{:S(2)}, u32[]{:S(2)}) collective-permute-start(bf16[16,8320]{1,0:T(8,128)(2,1)S(1)} %get-tuple-element.42), channel_id=1, source_target_pairs={{0,24},{4,28},{8,16},{12,20},{16,8},{20,12},{24,0},{28,4},{1,25},{... | collective-permute-start | bytes 798728 | tf_op jit(solution)/shard_map/ppermute | solution.py:433
  32.7 9.9 %collective-permute-done.2.refs_3_ = bf16[16,8320]{1,0:T(8,128)(2,1)S(1)} collective-permute-done((bf16[16,8320]{1,0:T(8,128)(2,1)S(1)}, bf16[16,8320]{1,0:T(8,128)(2,1)S(1)}, u32[]{:S(2)}, u32[]{:S(2)}) %collective-permute-start.2) | collective-permute-done | bytes 266272 | tf_op jit(solution)/shard_map/ppermute | solution.py:433
  42.7 2.4 %collective-permute-start.6 = (bf16[16,8320]{1,0:T(8,128)(2,1)S(1)}, bf16[16,8320]{1,0:T(8,128)(2,1)S(1)}, u32[]{:S(2)}, u32[]{:S(2)}) collective-permute-start(bf16[16,8320]{1,0:T(8,128)(2,1)S(1)} %get-tuple-element.44), channel_id=1, source_target_pairs={{0,28},{4,24},{8,20},{12,16},{16,12},{20,8},{24,4},{28,0},{1,29},{... | collective-permute-start | bytes 798728 | tf_op jit(solution)/shard_map/ppermute | solution.py:433
  45.1 7.8 %collective-permute-done.5.refs_6_ = bf16[16,8320]{1,0:T(8,128)(2,1)S(1)} collective-permute-done((bf16[16,8320]{1,0:T(8,128)(2,1)S(1)}, bf16[16,8320]{1,0:T(8,128)(2,1)S(1)}, u32[]{:S(2)}, u32[]{:S(2)}) %collective-permute-start.5) | collective-permute-done | bytes 266272 | tf_op jit(solution)/shard_map/ppermute | solution.py:433
  52.9 3.1 %collective-permute-done.8.refs_9_ = bf16[1056,1024]{1,0:T(8,128)(2,1)S(1)} collective-permute-done((bf16[1056,1024]{1,0:T(8,128)(2,1)S(1)}, bf16[1056,1024]{1,0:T(8,128)(2,1)S(1)}, u32[]{:S(2)}, u32[]{:S(2)}) %collective-permute-start.8) | collective-permute-done | bytes 2162720 | tf_op jit(solution)/shard_map/ppermute | solution.py:426
  56.0 5.7 %weight_grads.1 = (bf16[2,2,256,1024]{3,2,1,0:T(8,128)(2,1)S(1)}, bf16[512,1024]{1,0:T(8,128)(2,1)S(1)}, bf16[512,1024]{1,0:T(8,128)(2,1)S(1)}, bf16[512,1024]{1...) custom-call(bf16[16,8320]{1,0:T(8,128)(2,1)S(1)} %get-tuple-element., ...), custom_call_target="tpu_custom_call" | custom-call | tf_op jit(solution)/shard_map/weight_grads/pallas_call | solution.py:490
  61.8 3.1 %token_grads.1 = (bf16[2,2,256,1024]{3,2,1,0:T(8,128)(2,1)S(1)}, bf16[64,1024]{1,0:T(8,128)(2,1)S(1)}, bf16[64,1024]{1,0:T(8,128)(2,1)S(1)}, bf16[64,1024]{1,0:T...) custom-call(bf16[512,1024]{1,0:T(8,128)(2,1)S(1)} %get-tuple-element, ...), custom_call_target="tpu_custom_call" | custom-call | tf_op jit(solution)/shard_map/token_grads/pallas_call | solution.py:520
  64.9 1.0 %collective-permute-done.9.near_ref = bf16[2,2,256,1024]{3,2,1,0:T(8,128)(2,1)S(1)} collective-permute-done((bf16[2,2,256,1024]{3,2,1,0:T(8,128)(2,1)S(1)}, bf16[2,2,256,1024]{3,2,1,0:T(8,128)(2,1)S(1)}, u32[]{:S(2)}, u32[]{:S(2)}) %collective-permute-start.9) | collective-permute-done | bytes 2097184 | tf_op jit(solution)/shard_map/ppermute | solution.py:426
  66.2 1.8 %collective-permute-start.10 = (bf16[2,256,1024]{2,1,0:T(8,128)(2,1)S(1)}, bf16[2,256,1024]{2,1,0:T(8,128)(2,1)S(1)}, u32[]{:S(2)}, u32[]{:S(2)}) collective-permute-start(bf16[2,256,1024]{2,1,0:T(8,128)(2,1)S(1)} %far_add.1), channel_id=1, source_target_pairs={{0,2},{1,3},{2,0},{3,1},{4,6},{5,7},{6,4},{7,5},{8,10},{9,11},{10,... | collective-permute-start | bytes 3145736 | tf_op jit(solution)/shard_map/ppermute | solution.py:426
  68.0 4.0 %collective-permute-start.11 = (bf16[64,1024]{1,0:T(8,128)(2,1)S(1)}, bf16[64,1024]{1,0:T(8,128)(2,1)S(1)}, u32[]{:S(2)}, u32[]{:S(2)}) collective-permute-start(bf16[64,1024]{1,0:T(8,128)(2,1)S(1)} %get-tuple-element.59), channel_id=1, source_target_pairs={{0,16},{4,20},{8,24},{12,28},{16,0},{20,4},{24,8},{28,12},{1,17},{... | collective-permute-start | bytes 393224 | tf_op jit(solution)/shard_map/ppermute | solution.py:433
  72.5 1.0 collective-permute-start.13
  73.5 0.9 collective-permute-start.14
  74.4 6.9 %collective-permute-done.11.refs_1_ = bf16[64,1024]{1,0:T(8,128)(2,1)S(1)} collective-permute-done((bf16[64,1024]{1,0:T(8,128)(2,1)S(1)}, bf16[64,1024]{1,0:T(8,128)(2,1)S(1)}, u32[]{:S(2)}, u32[]{:S(2)}) %collective-permute-start.11) | collective-permute-done | bytes 131104 | tf_op jit(solution)/shard_map/ppermute | solution.py:433
  81.3 3.2 %collective-permute-start.15 = (bf16[64,1024]{1,0:T(8,128)(2,1)S(1)}, bf16[64,1024]{1,0:T(8,128)(2,1)S(1)}, u32[]{:S(2)}, u32[]{:S(2)}) collective-permute-start(bf16[64,1024]{1,0:T(8,128)(2,1)S(1)} %get-tuple-element.63), channel_id=1, source_target_pairs={{0,24},{4,28},{8,16},{12,20},{16,8},{20,12},{24,0},{28,4},{1,25},{... | collective-permute-start | bytes 393224 | tf_op jit(solution)/shard_map/ppermute | solution.py:433
  84.6 5.0 %collective-permute-start.17 = (bf16[64,1024]{1,0:T(8,128)(2,1)S(1)}, bf16[64,1024]{1,0:T(8,128)(2,1)S(1)}, u32[]{:S(2)}, u32[]{:S(2)}) collective-permute-start(bf16[64,1024]{1,0:T(8,128)(2,1)S(1)} %get-tuple-element.65), channel_id=1, source_target_pairs={{0,28},{4,24},{8,20},{12,16},{16,12},{20,8},{24,4},{28,0},{1,29},{... | collective-permute-start | bytes 393224 | tf_op jit(solution)/shard_map/ppermute | solution.py:433
  90.1 3.2 %collective-permute-done.16.refs_6_ = bf16[64,1024]{1,0:T(8,128)(2,1)S(1)} collective-permute-done((bf16[64,1024]{1,0:T(8,128)(2,1)S(1)}, bf16[64,1024]{1,0:T(8,128)(2,1)S(1)}, u32[]{:S(2)}, u32[]{:S(2)}) %collective-permute-start.16) | collective-permute-done | bytes 131104 | tf_op jit(solution)/shard_map/ppermute | solution.py:433
  93.4 2.7 %tail.1 = (bf16[16,32,1024]{2,1,0:T(8,128)(2,1)}, bf16[256,2,512]{2,1,0:T(2,128)(2,1)}, bf16[256,2,512]{2,1,0:T(2,128)(2,1)}) custom-call(s32[16]{0:T(128)S(1)} %get-tuple-element.36.after_ref.source_ref, f32[2,256,2,512]{3,2,1,0:T(2,128)S(1)} %own_add.1.own_ref, bf16[2,256,1024]{2,1,0:T(8,128)(2,1)S(1)} %collective-permute-done.10.far_ref, ...), custom_call_target="tpu_custom_call" | custom-call | tf_op jit(solution)/shard_map/tail/pallas_call | solution.py:550
  (25 shorter events, 3.3 us)
Async XLA Ops:
  0.6 1.4 %copy-start = (bf16[256,2]{0,1:T(2,128)(2,1)S(1)}, bf16[256,2]{0,1:T(2,128)(2,1)}, u32[]{:S(2)}) copy-start(bf16[256,2]{0,1:T(2,128)(2,1)} %param.13) | copy-start | bytes 3076
  2.1 2.9 %collective-permute-start.7 = (bf16[528,1024]{1,0:T(8,128)(2,1)S(1)}, bf16[528,1024]{1,0:T(8,128)(2,1)S(1)}, u32[]{:S(2)}, u32[]{:S(2)}) collective-permute-start(bf16[528,1024]{1,0:T(8,128)(2,1)S(1)} %fusion.1.own_hbm), channel_id=1, source_target_pairs={{0,1},{1,0},{2,3},{3,2},{4,5},{5,4},{6,7},{7,6},{8,9},{9,8},{10,11... | collective-permute-start | bytes 3244040 | tf_op jit(solution)/shard_map/ppermute | solution.py:426
  5.8 50.3 %collective-permute-start.8 = (bf16[1056,1024]{1,0:T(8,128)(2,1)S(1)}, bf16[1056,1024]{1,0:T(8,128)(2,1)S(1)}, u32[]{:S(2)}, u32[]{:S(2)}) collective-permute-start(bf16[1056,1024]{1,0:T(8,128)(2,1)S(1)} %pair.1.refs_8_), channel_id=1, source_target_pairs={{0,2},{1,3},{2,0},{3,1},{4,6},{5,7},{6,4},{7,5},{8,10},{9,11},{10,... | collective-permute-start | bytes 6488072 | tf_op jit(solution)/shard_map/ppermute | solution.py:426
  8.7 21.6 %collective-permute-start = (bf16[16,8320]{1,0:T(8,128)(2,1)S(1)}, bf16[16,8320]{1,0:T(8,128)(2,1)S(1)}, u32[]{:S(2)}, u32[]{:S(2)}) collective-permute-start(bf16[16,8320]{1,0:T(8,128)(2,1)S(1)} %get-tuple-element.38), channel_id=1, source_target_pairs={{0,16},{4,20},{8,24},{12,28},{16,0},{20,4},{24,8},{28,12},{1,17},{... | collective-permute-start | bytes 798728 | tf_op jit(solution)/shard_map/ppermute | solution.py:433
  11.3 21.5 %collective-permute-start.1 = (bf16[16,8320]{1,0:T(8,128)(2,1)S(1)}, bf16[16,8320]{1,0:T(8,128)(2,1)S(1)}, u32[]{:S(2)}, u32[]{:S(2)}) collective-permute-start(bf16[16,8320]{1,0:T(8,128)(2,1)S(1)} %get-tuple-element.39), channel_id=1, source_target_pairs={{0,4},{4,0},{8,12},{12,8},{16,20},{20,16},{24,28},{28,24},{1,5},{5... | collective-permute-start | bytes 798728 | tf_op jit(solution)/shard_map/ppermute | solution.py:433
  12.8 29.9 %collective-permute-start.2 = (bf16[16,8320]{1,0:T(8,128)(2,1)S(1)}, bf16[16,8320]{1,0:T(8,128)(2,1)S(1)}, u32[]{:S(2)}, u32[]{:S(2)}) collective-permute-start(bf16[16,8320]{1,0:T(8,128)(2,1)S(1)} %get-tuple-element.40), channel_id=1, source_target_pairs={{0,20},{4,16},{8,28},{12,24},{16,4},{20,0},{24,12},{28,8},{1,21},{... | collective-permute-start | bytes 798728 | tf_op jit(solution)/shard_map/ppermute | solution.py:433
  13.1 32.0 %collective-permute-start.3 = (bf16[16,8320]{1,0:T(8,128)(2,1)S(1)}, bf16[16,8320]{1,0:T(8,128)(2,1)S(1)}, u32[]{:S(2)}, u32[]{:S(2)}) collective-permute-start(bf16[16,8320]{1,0:T(8,128)(2,1)S(1)} %get-tuple-element.41), channel_id=1, source_target_pairs={{0,8},{4,12},{8,0},{12,4},{16,24},{20,28},{24,16},{28,20},{1,9},{5... | collective-permute-start | bytes 798728 | tf_op jit(solution)/shard_map/ppermute | solution.py:433
  30.3 14.8 %collective-permute-start.4 = (bf16[16,8320]{1,0:T(8,128)(2,1)S(1)}, bf16[16,8320]{1,0:T(8,128)(2,1)S(1)}, u32[]{:S(2)}, u32[]{:S(2)}) collective-permute-start(bf16[16,8320]{1,0:T(8,128)(2,1)S(1)} %get-tuple-element.42), channel_id=1, source_target_pairs={{0,24},{4,28},{8,16},{12,20},{16,8},{20,12},{24,0},{28,4},{1,25},{... | collective-permute-start | bytes 798728 | tf_op jit(solution)/shard_map/ppermute | solution.py:433
  32.7 20.2 %collective-permute-start.5 = (bf16[16,8320]{1,0:T(8,128)(2,1)S(1)}, bf16[16,8320]{1,0:T(8,128)(2,1)S(1)}, u32[]{:S(2)}, u32[]{:S(2)}) collective-permute-start(bf16[16,8320]{1,0:T(8,128)(2,1)S(1)} %get-tuple-element.43), channel_id=1, source_target_pairs={{0,12},{4,8},{8,4},{12,0},{16,28},{20,24},{24,20},{28,16},{1,13},{... | collective-permute-start | bytes 798728 | tf_op jit(solution)/shard_map/ppermute | solution.py:433
  42.7 10.3 %collective-permute-start.6 = (bf16[16,8320]{1,0:T(8,128)(2,1)S(1)}, bf16[16,8320]{1,0:T(8,128)(2,1)S(1)}, u32[]{:S(2)}, u32[]{:S(2)}) collective-permute-start(bf16[16,8320]{1,0:T(8,128)(2,1)S(1)} %get-tuple-element.44), channel_id=1, source_target_pairs={{0,28},{4,24},{8,20},{12,16},{16,12},{20,8},{24,4},{28,0},{1,29},{... | collective-permute-start | bytes 798728 | tf_op jit(solution)/shard_map/ppermute | solution.py:433
  61.7 4.2 %collective-permute-start.9 = (bf16[2,2,256,1024]{3,2,1,0:T(8,128)(2,1)S(1)}, bf16[2,2,256,1024]{3,2,1,0:T(8,128)(2,1)S(1)}, u32[]{:S(2)}, u32[]{:S(2)}) collective-permute-start(bf16[2,2,256,1024]{3,2,1,0:T(8,128)(2,1)S(1)} %get-tuple-element.57), channel_id=1, source_target_pairs={{0,1},{1,0},{2,3},{3,2},{4,5},{5,4},{6,7},{7,6},{8,9},{9,8},{10,11... | collective-permute-start | bytes 6291464 | tf_op jit(solution)/shard_map/ppermute | solution.py:426
  66.2 27.2 %collective-permute-start.10 = (bf16[2,256,1024]{2,1,0:T(8,128)(2,1)S(1)}, bf16[2,256,1024]{2,1,0:T(8,128)(2,1)S(1)}, u32[]{:S(2)}, u32[]{:S(2)}) collective-permute-start(bf16[2,256,1024]{2,1,0:T(8,128)(2,1)S(1)} %far_add.1), channel_id=1, source_target_pairs={{0,2},{1,3},{2,0},{3,1},{4,6},{5,7},{6,4},{7,5},{8,10},{9,11},{10,... | collective-permute-start | bytes 3145736 | tf_op jit(solution)/shard_map/ppermute | solution.py:426
  68.0 13.3 %collective-permute-start.11 = (bf16[64,1024]{1,0:T(8,128)(2,1)S(1)}, bf16[64,1024]{1,0:T(8,128)(2,1)S(1)}, u32[]{:S(2)}, u32[]{:S(2)}) collective-permute-start(bf16[64,1024]{1,0:T(8,128)(2,1)S(1)} %get-tuple-element.59), channel_id=1, source_target_pairs={{0,16},{4,20},{8,24},{12,28},{16,0},{20,4},{24,8},{28,12},{1,17},{... | collective-permute-start | bytes 393224 | tf_op jit(solution)/shard_map/ppermute | solution.py:433
  72.0 12.4 %collective-permute-start.12 = (bf16[64,1024]{1,0:T(8,128)(2,1)S(1)}, bf16[64,1024]{1,0:T(8,128)(2,1)S(1)}, u32[]{:S(2)}, u32[]{:S(2)}) collective-permute-start(bf16[64,1024]{1,0:T(8,128)(2,1)S(1)} %get-tuple-element.60), channel_id=1, source_target_pairs={{0,4},{4,0},{8,12},{12,8},{16,20},{20,16},{24,28},{28,24},{1,5},{5... | collective-permute-start | bytes 393224 | tf_op jit(solution)/shard_map/ppermute | solution.py:433
  72.5 12.1 %collective-permute-start.13 = (bf16[64,1024]{1,0:T(8,128)(2,1)S(1)}, bf16[64,1024]{1,0:T(8,128)(2,1)S(1)}, u32[]{:S(2)}, u32[]{:S(2)}) collective-permute-start(bf16[64,1024]{1,0:T(8,128)(2,1)S(1)} %get-tuple-element.61), channel_id=1, source_target_pairs={{0,20},{4,16},{8,28},{12,24},{16,4},{20,0},{24,12},{28,8},{1,21},{... | collective-permute-start | bytes 393224 | tf_op jit(solution)/shard_map/ppermute | solution.py:433
  73.5 16.6 %collective-permute-start.14 = (bf16[64,1024]{1,0:T(8,128)(2,1)S(1)}, bf16[64,1024]{1,0:T(8,128)(2,1)S(1)}, u32[]{:S(2)}, u32[]{:S(2)}) collective-permute-start(bf16[64,1024]{1,0:T(8,128)(2,1)S(1)} %get-tuple-element.62), channel_id=1, source_target_pairs={{0,8},{4,12},{8,0},{12,4},{16,24},{20,28},{24,16},{28,20},{1,9},{5... | collective-permute-start | bytes 393224 | tf_op jit(solution)/shard_map/ppermute | solution.py:433
  81.3 8.8 %collective-permute-start.15 = (bf16[64,1024]{1,0:T(8,128)(2,1)S(1)}, bf16[64,1024]{1,0:T(8,128)(2,1)S(1)}, u32[]{:S(2)}, u32[]{:S(2)}) collective-permute-start(bf16[64,1024]{1,0:T(8,128)(2,1)S(1)} %get-tuple-element.63), channel_id=1, source_target_pairs={{0,24},{4,28},{8,16},{12,20},{16,8},{20,12},{24,0},{28,4},{1,25},{... | collective-permute-start | bytes 393224 | tf_op jit(solution)/shard_map/ppermute | solution.py:433
  84.5 8.9 %collective-permute-start.16 = (bf16[64,1024]{1,0:T(8,128)(2,1)S(1)}, bf16[64,1024]{1,0:T(8,128)(2,1)S(1)}, u32[]{:S(2)}, u32[]{:S(2)}) collective-permute-start(bf16[64,1024]{1,0:T(8,128)(2,1)S(1)} %get-tuple-element.64), channel_id=1, source_target_pairs={{0,12},{4,8},{8,4},{12,0},{16,28},{20,24},{24,20},{28,16},{1,13},{... | collective-permute-start | bytes 393224 | tf_op jit(solution)/shard_map/ppermute | solution.py:433
  84.6 8.8 %collective-permute-start.17 = (bf16[64,1024]{1,0:T(8,128)(2,1)S(1)}, bf16[64,1024]{1,0:T(8,128)(2,1)S(1)}, u32[]{:S(2)}, u32[]{:S(2)}) collective-permute-start(bf16[64,1024]{1,0:T(8,128)(2,1)S(1)} %get-tuple-element.65), channel_id=1, source_target_pairs={{0,28},{4,24},{8,20},{12,16},{16,12},{20,8},{24,4},{28,0},{1,29},{... | collective-permute-start | bytes 393224 | tf_op jit(solution)/shard_map/ppermute | solution.py:433

commit v6 on v5

--- a/solution.py
+++ b/solution.py
@@ -11,6 +11,7 @@
 SLAB = 16
 LANES = 128
 MIB = 1024 * 1024
+PIECES = 4
 OFFSETS = (0, 4, 1, 5, 2, 6, 3, 7)
 ANYWHERE = pl.BlockSpec(memory_space=pl.ANY)
 VMEM = pl.BlockSpec(memory_space=pltpu.VMEM)
@@ -195,8 +196,10 @@
     capacity, mp_size, tile, scale, direct = dims
     source_count = len(direct) or 1
     sources, (pair_hbm, far_hbm), refs = refs[:source_count], refs[source_count:][:2], refs[source_count + 2 :]
-    send_ref, x_buf, dy_buf, inner_buf, stats_buf, id_buf, down_ref, gain_ref, normed_buf, act_buf = refs[:10]
-    up_ref, gain_buf, sems, weight_sems, *scratch = refs[10:]
+    half = mp_size // 2
+    send_refs, refs = refs[:half], refs[half:]
+    x_buf, dy_buf, inner_buf, stats_buf, id_buf, down_ref, gain_ref, normed_buf, act_buf = refs[:9]
+    up_ref, gain_buf, sems, weight_sems, *scratch = refs[9:]
     rows, features = x_buf.shape
     shard = features // mp_size
     first, then, later = [], [], []
@@ -283,24 +286,25 @@
         one_tile(0, 0)
     else:
         lax.fori_loop(0, rows // tile, one_tile, 0)
-    products(dy_buf, act_buf, normed_buf, inner_buf, send_ref, 1, scale)
-
-
-def products(dy_ref, act_ref, normed_ref, inner_ref, out_ref, first, scale):
-    half, _, shard, _ = out_ref.shape
-    for n in range(half):
+    products(dy_buf, act_buf, normed_buf, inner_buf, send_refs, 1, scale)
+
+
+def products(dy_ref, act_ref, normed_ref, inner_ref, out_refs, first, scale):
+    shard = out_refs[0].shape[1]
+    for n, out_ref in enumerate(out_refs):
         here = pl.ds(pl.multiple_of((lax.axis_index("mp") ^ (2 * n + first)) * shard, shard), shard)
         for kind, (left, right) in enumerate(((dy_ref, act_ref), (normed_ref, inner_ref))):
             part = lax.dot_general(
                 left[:, here], right[...], (((0,), (0,)), ((), ())), preferred_element_type=jnp.float32
             )
-            out_ref[n, kind] = (part * scale).astype(jnp.bfloat16)
+            out_ref[kind] = (part * scale).astype(jnp.bfloat16)
 
 
 def token_grad_kernel(
-    dims, x_ref, dy_ref, inner_ref, stats_ref, id_ref, down_ref, gain_ref, normed_ref, act_ref, keep_ref, *refs
+    dims, x_ref, dy_ref, inner_ref, stats_ref, id_ref, down_ref, gain_ref, normed_ref, act_ref, *refs
 ):
-    tile, chunk_rows, direct, scale = dims
+    tile, chunk_rows, direct, scale, half = dims
+    keep_refs, refs = refs[:half], refs[half:]
     rows = x_ref.shape[0]
 
     def part(here):
@@ -321,7 +325,7 @@
             token_grad = part(pl.ds(step * tile, tile))
             for n in range(tile // chunk_rows):
                 refs[step * (tile // chunk_rows) + n][...] = token_grad[n * chunk_rows : (n + 1) * chunk_rows]
-        products(dy_ref, act_ref, normed_ref, inner_ref, keep_ref, 0, scale)
+        products(dy_ref, act_ref, normed_ref, inner_ref, keep_refs, 0, scale)
         return
     out_hbm, grad_buf, sem = refs
 
@@ -332,13 +336,14 @@
         return carry
 
     lax.fori_loop(0, rows // tile, one_tile, 0)
-    products(dy_ref, act_ref, normed_ref, inner_ref, keep_ref, 0, scale)
+    products(dy_ref, act_ref, normed_ref, inner_ref, keep_refs, 0, scale)
     pltpu.make_async_copy(grad_buf, out_hbm, sem).wait()
 
 
-def add_kernel(place, keep_ref, near_ref, out_ref):
-    for kind in range(keep_ref.shape[1]):
-        total = keep_ref[place, kind].astype(jnp.float32) + near_ref[place, kind].astype(jnp.float32)
+def add_kernel(keep_ref, near_ref, *refs):
+    out_ref = refs[-1]
+    for kind in range(keep_ref.shape[0]):
+        total = keep_ref[kind].astype(jnp.float32) + near_ref[kind].astype(jnp.float32)
         out_ref[kind] = total.reshape(out_ref.shape[1:]).astype(out_ref.dtype)
 
 
@@ -379,11 +384,14 @@
                 else:
                     pl.when(source_ref[slot] >= 0)(store(slot, buf.at[slot]).start)
     writes = []
-    for kind, grad_hbm in enumerate(grad_hbms):
-        total = own_ref[kind] + far_ref[kind].astype(jnp.float32).reshape(grad.shape[1:])
-        grad[kind] = total.astype(grad.dtype)
-        writes.append(pltpu.make_async_copy(grad.at[kind], grad_hbm, sems.at[2 + kind]))
-        writes[-1].start()
+    piece = grad.shape[1] // PIECES
+    for n in range(PIECES):
+        here = pl.ds(n * piece, piece)
+        for kind, grad_hbm in enumerate(grad_hbms):
+            total = own_ref[kind, here, :] + far_ref[kind, here, :].astype(jnp.float32)
+            grad[kind, here] = total.reshape(piece, *grad.shape[2:]).astype(grad.dtype)
+            writes.append(pltpu.make_async_copy(grad.at[kind, here], grad_hbm.at[here], sems.at[2 + PIECES * kind + n]))
+            writes[-1].start()
     if full:
         pltpu.make_async_copy(out_hbm, out_hbm, out_sems.at[0]).wait()
     else:
@@ -485,12 +493,13 @@
         recv = [exchange(packed[0])]
     inputs = in_vmem(*recv, pair, pair_far) if direct else in_hbm(*recv, pair, pair_far)
 
-    part = vmem_shape(mp_size // 2, 2, shard, width)
+    half = mp_size // 2
+    part = vmem_shape(2, shard, width)
     scale = 1.0 / (block_rows * mp_size)
-    send, *kept = pl.pallas_call(
+    results = pl.pallas_call(
         functools.partial(weight_grad_kernel, (capacity, mp_size, tile, scale, direct)),
         out_shape=(
-            part,
+            *[part] * half,
             vmem_shape(rows, features),
             vmem_shape(rows, features),
             vmem_shape(rows, width),
@@ -502,7 +511,7 @@
             vmem_shape(rows, width),
         ),
         in_specs=[VMEM if direct else ANYWHERE] * len(recv) + [ANYWHERE] * 2,
-        out_specs=(VMEM,) * 10,
+        out_specs=(VMEM,) * (9 + half),
         scratch_shapes=[
             pltpu.VMEM((features, width), bf),
             pltpu.VMEM((mp_size, SLAB, features), bf),
@@ -513,35 +522,45 @@
         compiler_params=params(14 + rows // 48),
         name="weight_grads",
     )(*inputs)
-    near = swap(send, 1)
+    kept = results[half:]
+    near_far, near_own = swap(results[1], 1), swap(results[0], 1)
 
     tile = min(256, rows)
     chunk_rows = capacity * block_rows
-    keep, *token_parts = pl.pallas_call(
-        functools.partial(token_grad_kernel, (tile, chunk_rows, direct, scale)),
+    keep_own, keep_far, *token_parts = pl.pallas_call(
+        functools.partial(token_grad_kernel, (tile, chunk_rows, direct, scale, half)),
         out_shape=[
-            part,
+            *[part] * half,
             *([vmem_shape(chunk_rows, features)] * dp_size if direct else [pltpu.HBM((rows, features), bf)]),
         ],
         in_specs=[VMEM] * 9,
-        out_specs=[VMEM] * (1 + dp_size) if direct else [VMEM, ANYWHERE],
+        out_specs=[VMEM] * half + ([VMEM] * dp_size if direct else [ANYWHERE]),
         scratch_shapes=[] if direct else [pltpu.VMEM((rows, features), bf), pltpu.SemaphoreType.DMA(())],
         compiler_params=params(12 + rows // 64),
         name="token_grads",
     )(*in_vmem(*kept))
 
-    def add(place, extent, kind, name):
-        return pl.pallas_call(
-            functools.partial(add_kernel, place),
-            out_shape=vmem_shape(2, *extent, kind=kind),
-            in_specs=[VMEM] * 2,
-            out_specs=VMEM,
+    def add(keep, near, extent, kind, name, *through):
+        *through, result = pl.pallas_call(
+            add_kernel,
+            out_shape=(
+                *[vmem_shape(*array.shape) for array in through],
+                vmem_shape(2, *extent, kind=kind),
+            ),
+            in_specs=[VMEM] * 2 + [ANYWHERE] * len(through),
+            out_specs=(*[ANYWHERE] * len(through), VMEM),
+            input_output_aliases={2 + n: n for n in range(len(through))},
             compiler_params=params(14),
             name=name,
-        )(*in_vmem(keep, near))
-
-    far = swap(add(1, (shard, width), bf, "far_add"), 2)
-    own_sum = add(0, (shard, lang_local, bottleneck), jnp.float32, "own_add")
+        )(*in_vmem(keep, near, *through))
+        return result, *through
+
+    (far_sum,) = add(keep_far, near_far, (shard, width), bf, "far_add")
+    far = swap(far_sum, 2)
+    own_sum, *sent = add(
+        keep_own, near_own, (shard, width), jnp.float32, "own_add", *token_parts[1 if direct else 2 :]
+    )
+    token_parts = token_parts[:1] + sent
     if direct:
         backs = in_vmem(*swap_all(token_parts))
     else:
@@ -554,7 +573,7 @@
         out_specs=(ANYWHERE,) * 3,
         scratch_shapes=[
             pltpu.VMEM((2, shard, lang_local, bottleneck), bf),
-            pltpu.SemaphoreType.DMA((4,)),
+            pltpu.SemaphoreType.DMA((2 + 2 * PIECES,)),
             pltpu.SemaphoreType.DMA((slots,)),
             *([] if direct else [pltpu.VMEM((slots, block_rows, features), bf)]),
         ],

time: 96.2 us -> 95.8 us (level)
    ppermute x4 -> x5, waiting for transfers between devices: 4.15 us -> 3.12 us  [swap(): return lax.ppermute(array, 'mp', [(i, i ^ bit) for i in range(mp_size)])]
    ppermute x4 -> x5, starting transfers between devices: 5.33 us -> 5.8 us  [swap(): return lax.ppermute(array, 'mp', [(i, i ^ bit) for i in range(mp_size)])]
  transfers between devices with their start and end apart: 18 -> 19, of which waited for: 8 -> 7; matrix products, arithmetic and copies ran while one was open for 0% -> 0% of each run, Pallas kernels for 6% -> 6%
where the time goes in v6:
time: 95.8 us; the launch traced here: 95.6 us
  waiting for transfers between devices  47.2 us (49%)
  starting transfers between devices  31.4 us (33%)
  Pallas kernels  16.1 us (17%)
    ppermute x14, waiting for transfers between devices, swap_all(): lax.ppermute(chunk, 'dp', [(i, i ^ offset) for i in range(dp_size)])  44.1 us
    ppermute x14, starting transfers between devices, swap_all(): lax.ppermute(chunk, 'dp', [(i, i ^ offset) for i in range(dp_size)])  25.5 us
    ppermute x5, starting transfers between devices, swap(): return lax.ppermute(array, 'mp', [(i, i ^ bit) for i in range(mp_size)])  5.8 us
    pallas_call x1, Pallas kernels, shards(): pl.pallas_call(functools.partial(weight_grad_kernel, (capacity, mp_size,...  5.66 us
    ppermute x5, waiting for transfers between devices, swap(): return lax.ppermute(array, 'mp', [(i, i ^ bit) for i in range(mp_size)])  3.12 us
    pallas_call x1, Pallas kernels, shards(): pl.pallas_call(functools.partial(token_grad_kernel, (tile, chunk_rows, di...  3.09 us
    pallas_call x1, Pallas kernels, shards(): pl.pallas_call(functools.partial(tail_kernel, (capacity, full, direct)),...  2.58 us
    pallas_call x1, Pallas kernels, shards(): pl.pallas_call(functools.partial(pack_kernel, (dp_size, capacity, lang_lo...  2.31 us
  transfers between devices with their start and end apart: 19, of which 7 were waited for; matrix products, arithmetic and copies ran while one was open for 0% of the time, Pallas kernels for 6%

profile of v6, /device:TPU:0, one launch (start us, length us, event | category | flops | bytes accessed | tf_op | source)
XLA Modules:
  0.0 95.6 jit_solution(8964455146299131289)
XLA Ops:
  0.6 1.2 %load.1 = (bf16[256,2,512]{2,1,0:T(2,128)(2,1)S(1)}, bf16[256,2,512]{2,1,0:T(2,128)(2,1)S(1)}) custom-call(bf16[256,2,512]{2,1,0:T(2,128)(2,1)} %down_hbm.1, bf16[256,2,512]{2,1,0:T(2,128)(2,1)} %up_hbm.1), custom_call_target="tpu_custom_call" | custom-call | tf_op jit(solution)/shard_map/load/pallas_call | solution.py:467
  2.6 2.3 %pack.1 = (bf16[16,8320]{1,0:T(8,128)(2,1)S(1)}, bf16[16,8320]{1,0:T(8,128)(2,1)S(1)}, bf16[16,8320]{1,0:T(8,128)(2,1)S(1)}, bf16[16,8320]{1,0:T(8,128)(2,1)S(1)...) custom-call(s32[16]{0:T(128)} %lang_hbm.1, ...), custom_call_target="tpu_custom_call" | custom-call | tf_op jit(solution)/shard_map/pack/pallas_call | solution.py:448
  5.0 0.8 pair.1.refs_8_
  5.8 2.9 %collective-permute-start.8 = (bf16[1056,1024]{1,0:T(8,128)(2,1)S(1)}, bf16[1056,1024]{1,0:T(8,128)(2,1)S(1)}, u32[]{:S(2)}, u32[]{:S(2)}) collective-permute-start(bf16[1056,1024]{1,0:T(8,128)(2,1)S(1)} %pair.1.refs_8_), channel_id=1, source_target_pairs={{0,2},{1,3},{2,0},{3,1},{4,6},{5,7},{6,4},{7,5},{8,10},{9,11},{10,... | collective-permute-start | bytes 6488072 | tf_op jit(solution)/shard_map/ppermute | solution.py:434
  8.7 2.6 %collective-permute-start = (bf16[16,8320]{1,0:T(8,128)(2,1)S(1)}, bf16[16,8320]{1,0:T(8,128)(2,1)S(1)}, u32[]{:S(2)}, u32[]{:S(2)}) collective-permute-start(bf16[16,8320]{1,0:T(8,128)(2,1)S(1)} %get-tuple-element.48), channel_id=1, source_target_pairs={{0,16},{4,20},{8,24},{12,28},{16,0},{20,4},{24,8},{28,12},{1,17},{... | collective-permute-start | bytes 798728 | tf_op jit(solution)/shard_map/ppermute | solution.py:441
  11.3 1.5 %collective-permute-start.1 = (bf16[16,8320]{1,0:T(8,128)(2,1)S(1)}, bf16[16,8320]{1,0:T(8,128)(2,1)S(1)}, u32[]{:S(2)}, u32[]{:S(2)}) collective-permute-start(bf16[16,8320]{1,0:T(8,128)(2,1)S(1)} %get-tuple-element.49), channel_id=1, source_target_pairs={{0,4},{4,0},{8,12},{12,8},{16,20},{20,16},{24,28},{28,24},{1,5},{5... | collective-permute-start | bytes 798728 | tf_op jit(solution)/shard_map/ppermute | solution.py:441
  13.1 1.6 %collective-permute-start.3 = (bf16[16,8320]{1,0:T(8,128)(2,1)S(1)}, bf16[16,8320]{1,0:T(8,128)(2,1)S(1)}, u32[]{:S(2)}, u32[]{:S(2)}) collective-permute-start(bf16[16,8320]{1,0:T(8,128)(2,1)S(1)} %get-tuple-element.51), channel_id=1, source_target_pairs={{0,8},{4,12},{8,0},{12,4},{16,24},{20,28},{24,16},{28,20},{1,9},{5... | collective-permute-start | bytes 798728 | tf_op jit(solution)/shard_map/ppermute | solution.py:441
  14.7 15.6 %collective-permute-done.refs_1_ = bf16[16,8320]{1,0:T(8,128)(2,1)S(1)} collective-permute-done((bf16[16,8320]{1,0:T(8,128)(2,1)S(1)}, bf16[16,8320]{1,0:T(8,128)(2,1)S(1)}, u32[]{:S(2)}, u32[]{:S(2)}) %collective-permute-start) | collective-permute-done | bytes 266272 | tf_op jit(solution)/shard_map/ppermute | solution.py:441
  30.3 2.5 %collective-permute-start.4 = (bf16[16,8320]{1,0:T(8,128)(2,1)S(1)}, bf16[16,8320]{1,0:T(8,128)(2,1)S(1)}, u32[]{:S(2)}, u32[]{:S(2)}) collective-permute-start(bf16[16,8320]{1,0:T(8,128)(2,1)S(1)} %get-tuple-element.52), channel_id=1, source_target_pairs={{0,24},{4,28},{8,16},{12,20},{16,8},{20,12},{24,0},{28,4},{1,25},{... | collective-permute-start | bytes 798728 | tf_op jit(solution)/shard_map/ppermute | solution.py:441
  32.7 9.9 %collective-permute-done.2.refs_3_ = bf16[16,8320]{1,0:T(8,128)(2,1)S(1)} collective-permute-done((bf16[16,8320]{1,0:T(8,128)(2,1)S(1)}, bf16[16,8320]{1,0:T(8,128)(2,1)S(1)}, u32[]{:S(2)}, u32[]{:S(2)}) %collective-permute-start.2) | collective-permute-done | bytes 266272 | tf_op jit(solution)/shard_map/ppermute | solution.py:441
  42.7 2.4 %collective-permute-start.6 = (bf16[16,8320]{1,0:T(8,128)(2,1)S(1)}, bf16[16,8320]{1,0:T(8,128)(2,1)S(1)}, u32[]{:S(2)}, u32[]{:S(2)}) collective-permute-start(bf16[16,8320]{1,0:T(8,128)(2,1)S(1)} %get-tuple-element.54), channel_id=1, source_target_pairs={{0,28},{4,24},{8,20},{12,16},{16,12},{20,8},{24,4},{28,0},{1,29},{... | collective-permute-start | bytes 798728 | tf_op jit(solution)/shard_map/ppermute | solution.py:441
  45.1 7.8 %collective-permute-done.5.refs_6_ = bf16[16,8320]{1,0:T(8,128)(2,1)S(1)} collective-permute-done((bf16[16,8320]{1,0:T(8,128)(2,1)S(1)}, bf16[16,8320]{1,0:T(8,128)(2,1)S(1)}, u32[]{:S(2)}, u32[]{:S(2)}) %collective-permute-start.5) | collective-permute-done | bytes 266272 | tf_op jit(solution)/shard_map/ppermute | solution.py:441
  52.9 3.1 %collective-permute-done.8.refs_9_ = bf16[1056,1024]{1,0:T(8,128)(2,1)S(1)} collective-permute-done((bf16[1056,1024]{1,0:T(8,128)(2,1)S(1)}, bf16[1056,1024]{1,0:T(8,128)(2,1)S(1)}, u32[]{:S(2)}, u32[]{:S(2)}) %collective-permute-start.8) | collective-permute-done | bytes 2162720 | tf_op jit(solution)/shard_map/ppermute | solution.py:434
  56.0 5.7 %weight_grads.1 = (bf16[2,256,1024]{2,1,0:T(8,128)(2,1)S(1)}, bf16[2,256,1024]{2,1,0:T(8,128)(2,1)S(1)}, bf16[512,1024]{1,0:T(8,128)(2,1)S(1)}, bf16[512,1024]{1...) custom-call(bf16[16,8320]{1,0:T(8,128)(2,1)S(1)} %get-tuple-element., ...), custom_call_target="tpu_custom_call" | custom-call | tf_op jit(solution)/shard_map/weight_grads/pallas_call | solution.py:499
  62.3 3.1 %token_grads.1 = (bf16[2,256,1024]{2,1,0:T(8,128)(2,1)S(1)}, bf16[2,256,1024]{2,1,0:T(8,128)(2,1)S(1)}, bf16[64,1024]{1,0:T(8,128)(2,1)S(1)}, bf16[64,1024]{1,0:...) custom-call(bf16[512,1024]{1,0:T(8,128)(2,1)S(1)} %get-tuple-element, ...), custom_call_target="tpu_custom_call" | custom-call | tf_op jit(solution)/shard_map/token_grads/pallas_call | solution.py:530
  65.6 1.8 %collective-permute-start.11 = (bf16[2,256,1024]{2,1,0:T(8,128)(2,1)S(1)}, bf16[2,256,1024]{2,1,0:T(8,128)(2,1)S(1)}, u32[]{:S(2)}, u32[]{:S(2)}) collective-permute-start(bf16[2,256,1024]{2,1,0:T(8,128)(2,1)S(1)} %far_add.1), channel_id=1, source_target_pairs={{0,2},{1,3},{2,0},{3,1},{4,6},{5,7},{6,4},{7,5},{8,10},{9,11},{10,... | collective-permute-start | bytes 3145736 | tf_op jit(solution)/shard_map/ppermute | solution.py:434
  67.6 4.1 %collective-permute-start.12 = (bf16[64,1024]{1,0:T(8,128)(2,1)S(1)}, bf16[64,1024]{1,0:T(8,128)(2,1)S(1)}, u32[]{:S(2)}, u32[]{:S(2)}) collective-permute-start(bf16[64,1024]{1,0:T(8,128)(2,1)S(1)} %get-tuple-element.79), channel_id=1, source_target_pairs={{0,16},{4,20},{8,24},{12,28},{16,0},{20,4},{24,8},{28,12},{1,17},{... | collective-permute-start | bytes 393224 | tf_op jit(solution)/shard_map/ppermute | solution.py:441
  72.3 1.0 %collective-permute-start.14 = (bf16[64,1024]{1,0:T(8,128)(2,1)S(1)}, bf16[64,1024]{1,0:T(8,128)(2,1)S(1)}, u32[]{:S(2)}, u32[]{:S(2)}) collective-permute-start(bf16[64,1024]{1,0:T(8,128)(2,1)S(1)} %get-tuple-element.81), channel_id=1, source_target_pairs={{0,20},{4,16},{8,28},{12,24},{16,4},{20,0},{24,12},{28,8},{1,21},{... | collective-permute-start | bytes 393224 | tf_op jit(solution)/shard_map/ppermute | solution.py:441
  73.3 0.8 collective-permute-start.15
  74.1 6.9 %collective-permute-done.12.refs_1_ = bf16[64,1024]{1,0:T(8,128)(2,1)S(1)} collective-permute-done((bf16[64,1024]{1,0:T(8,128)(2,1)S(1)}, bf16[64,1024]{1,0:T(8,128)(2,1)S(1)}, u32[]{:S(2)}, u32[]{:S(2)}) %collective-permute-start.12) | collective-permute-done | bytes 131104 | tf_op jit(solution)/shard_map/ppermute | solution.py:441
  81.0 3.2 %collective-permute-start.16 = (bf16[64,1024]{1,0:T(8,128)(2,1)S(1)}, bf16[64,1024]{1,0:T(8,128)(2,1)S(1)}, u32[]{:S(2)}, u32[]{:S(2)}) collective-permute-start(bf16[64,1024]{1,0:T(8,128)(2,1)S(1)} %get-tuple-element.83), channel_id=1, source_target_pairs={{0,24},{4,28},{8,16},{12,20},{16,8},{20,12},{24,0},{28,4},{1,25},{... | collective-permute-start | bytes 393224 | tf_op jit(solution)/shard_map/ppermute | solution.py:441
  84.3 5.0 %collective-permute-start.18 = (bf16[64,1024]{1,0:T(8,128)(2,1)S(1)}, bf16[64,1024]{1,0:T(8,128)(2,1)S(1)}, u32[]{:S(2)}, u32[]{:S(2)}) collective-permute-start(bf16[64,1024]{1,0:T(8,128)(2,1)S(1)} %get-tuple-element.85), channel_id=1, source_target_pairs={{0,28},{4,24},{8,20},{12,16},{16,12},{20,8},{24,4},{28,0},{1,29},{... | collective-permute-start | bytes 393224 | tf_op jit(solution)/shard_map/ppermute | solution.py:441
  89.3 3.7 %collective-permute-done.17.refs_6_ = bf16[64,1024]{1,0:T(8,128)(2,1)S(1)} collective-permute-done((bf16[64,1024]{1,0:T(8,128)(2,1)S(1)}, bf16[64,1024]{1,0:T(8,128)(2,1)S(1)}, u32[]{:S(2)}, u32[]{:S(2)}) %collective-permute-start.17) | collective-permute-done | bytes 131104 | tf_op jit(solution)/shard_map/ppermute | solution.py:441
  93.0 2.6 %tail.1 = (bf16[16,32,1024]{2,1,0:T(8,128)(2,1)}, bf16[256,2,512]{2,1,0:T(2,128)(2,1)}, bf16[256,2,512]{2,1,0:T(2,128)(2,1)}) custom-call(s32[16]{0:T(128)S(1)} %get-tuple-element.46.after_ref.source_ref, f32[2,256,1024]{2,1,0:T(8,128)S(1)} %get-tuple-element.75.own_ref, bf16[2,256,1024]{2,1,0:T(8,128)(2,1)S(1)} %collective-permute-done.11.far_ref, ...), custom_call_target="tpu_custom_call" | custom-call | tf_op jit(solution)/shard_map/tail/pallas_call | solution.py:569
  (27 shorter events, 2.7 us)
Async XLA Ops:
  0.6 1.4 %copy-start = (bf16[256,2]{0,1:T(2,128)(2,1)S(1)}, bf16[256,2]{0,1:T(2,128)(2,1)}, u32[]{:S(2)}) copy-start(bf16[256,2]{0,1:T(2,128)(2,1)} %param.13) | copy-start | bytes 3076
  2.1 2.9 %collective-permute-start.7 = (bf16[528,1024]{1,0:T(8,128)(2,1)S(1)}, bf16[528,1024]{1,0:T(8,128)(2,1)S(1)}, u32[]{:S(2)}, u32[]{:S(2)}) collective-permute-start(bf16[528,1024]{1,0:T(8,128)(2,1)S(1)} %fusion.1.own_hbm), channel_id=1, source_target_pairs={{0,1},{1,0},{2,3},{3,2},{4,5},{5,4},{6,7},{7,6},{8,9},{9,8},{10,11... | collective-permute-start | bytes 3244040 | tf_op jit(solution)/shard_map/ppermute | solution.py:434
  5.8 50.3 %collective-permute-start.8 = (bf16[1056,1024]{1,0:T(8,128)(2,1)S(1)}, bf16[1056,1024]{1,0:T(8,128)(2,1)S(1)}, u32[]{:S(2)}, u32[]{:S(2)}) collective-permute-start(bf16[1056,1024]{1,0:T(8,128)(2,1)S(1)} %pair.1.refs_8_), channel_id=1, source_target_pairs={{0,2},{1,3},{2,0},{3,1},{4,6},{5,7},{6,4},{7,5},{8,10},{9,11},{10,... | collective-permute-start | bytes 6488072 | tf_op jit(solution)/shard_map/ppermute | solution.py:434
  8.7 21.6 %collective-permute-start = (bf16[16,8320]{1,0:T(8,128)(2,1)S(1)}, bf16[16,8320]{1,0:T(8,128)(2,1)S(1)}, u32[]{:S(2)}, u32[]{:S(2)}) collective-permute-start(bf16[16,8320]{1,0:T(8,128)(2,1)S(1)} %get-tuple-element.48), channel_id=1, source_target_pairs={{0,16},{4,20},{8,24},{12,28},{16,0},{20,4},{24,8},{28,12},{1,17},{... | collective-permute-start | bytes 798728 | tf_op jit(solution)/shard_map/ppermute | solution.py:441
  11.3 21.5 %collective-permute-start.1 = (bf16[16,8320]{1,0:T(8,128)(2,1)S(1)}, bf16[16,8320]{1,0:T(8,128)(2,1)S(1)}, u32[]{:S(2)}, u32[]{:S(2)}) collective-permute-start(bf16[16,8320]{1,0:T(8,128)(2,1)S(1)} %get-tuple-element.49), channel_id=1, source_target_pairs={{0,4},{4,0},{8,12},{12,8},{16,20},{20,16},{24,28},{28,24},{1,5},{5... | collective-permute-start | bytes 798728 | tf_op jit(solution)/shard_map/ppermute | solution.py:441
  12.8 29.9 %collective-permute-start.2 = (bf16[16,8320]{1,0:T(8,128)(2,1)S(1)}, bf16[16,8320]{1,0:T(8,128)(2,1)S(1)}, u32[]{:S(2)}, u32[]{:S(2)}) collective-permute-start(bf16[16,8320]{1,0:T(8,128)(2,1)S(1)} %get-tuple-element.50), channel_id=1, source_target_pairs={{0,20},{4,16},{8,28},{12,24},{16,4},{20,0},{24,12},{28,8},{1,21},{... | collective-permute-start | bytes 798728 | tf_op jit(solution)/shard_map/ppermute | solution.py:441
  13.1 32.0 %collective-permute-start.3 = (bf16[16,8320]{1,0:T(8,128)(2,1)S(1)}, bf16[16,8320]{1,0:T(8,128)(2,1)S(1)}, u32[]{:S(2)}, u32[]{:S(2)}) collective-permute-start(bf16[16,8320]{1,0:T(8,128)(2,1)S(1)} %get-tuple-element.51), channel_id=1, source_target_pairs={{0,8},{4,12},{8,0},{12,4},{16,24},{20,28},{24,16},{28,20},{1,9},{5... | collective-permute-start | bytes 798728 | tf_op jit(solution)/shard_map/ppermute | solution.py:441
  30.3 14.8 %collective-permute-start.4 = (bf16[16,8320]{1,0:T(8,128)(2,1)S(1)}, bf16[16,8320]{1,0:T(8,128)(2,1)S(1)}, u32[]{:S(2)}, u32[]{:S(2)}) collective-permute-start(bf16[16,8320]{1,0:T(8,128)(2,1)S(1)} %get-tuple-element.52), channel_id=1, source_target_pairs={{0,24},{4,28},{8,16},{12,20},{16,8},{20,12},{24,0},{28,4},{1,25},{... | collective-permute-start | bytes 798728 | tf_op jit(solution)/shard_map/ppermute | solution.py:441
  32.7 20.2 %collective-permute-start.5 = (bf16[16,8320]{1,0:T(8,128)(2,1)S(1)}, bf16[16,8320]{1,0:T(8,128)(2,1)S(1)}, u32[]{:S(2)}, u32[]{:S(2)}) collective-permute-start(bf16[16,8320]{1,0:T(8,128)(2,1)S(1)} %get-tuple-element.53), channel_id=1, source_target_pairs={{0,12},{4,8},{8,4},{12,0},{16,28},{20,24},{24,20},{28,16},{1,13},{... | collective-permute-start | bytes 798728 | tf_op jit(solution)/shard_map/ppermute | solution.py:441
  42.7 10.3 %collective-permute-start.6 = (bf16[16,8320]{1,0:T(8,128)(2,1)S(1)}, bf16[16,8320]{1,0:T(8,128)(2,1)S(1)}, u32[]{:S(2)}, u32[]{:S(2)}) collective-permute-start(bf16[16,8320]{1,0:T(8,128)(2,1)S(1)} %get-tuple-element.54), channel_id=1, source_target_pairs={{0,28},{4,24},{8,20},{12,16},{16,12},{20,8},{24,4},{28,0},{1,29},{... | collective-permute-start | bytes 798728 | tf_op jit(solution)/shard_map/ppermute | solution.py:441
  61.7 3.7 %collective-permute-start.10 = (bf16[2,256,1024]{2,1,0:T(8,128)(2,1)S(1)}, bf16[2,256,1024]{2,1,0:T(8,128)(2,1)S(1)}, u32[]{:S(2)}, u32[]{:S(2)}) collective-permute-start(bf16[2,256,1024]{2,1,0:T(8,128)(2,1)S(1)} %get-tuple-element.77), channel_id=1, source_target_pairs={{0,1},{1,0},{2,3},{3,2},{4,5},{5,4},{6,7},{7,6},{8,9},{9,8},{10,11... | collective-permute-start | bytes 3145736 | tf_op jit(solution)/shard_map/ppermute | solution.py:434
  61.8 5.7 %collective-permute-start.9 = (bf16[2,256,1024]{2,1,0:T(8,128)(2,1)S(1)}, bf16[2,256,1024]{2,1,0:T(8,128)(2,1)S(1)}, u32[]{:S(2)}, u32[]{:S(2)}) collective-permute-start(bf16[2,256,1024]{2,1,0:T(8,128)(2,1)S(1)} %get-tuple-element.67), channel_id=1, source_target_pairs={{0,1},{1,0},{2,3},{3,2},{4,5},{5,4},{6,7},{7,6},{8,9},{9,8},{10,11... | collective-permute-start | bytes 3145736 | tf_op jit(solution)/shard_map/ppermute | solution.py:434
  65.6 27.4 %collective-permute-start.11 = (bf16[2,256,1024]{2,1,0:T(8,128)(2,1)S(1)}, bf16[2,256,1024]{2,1,0:T(8,128)(2,1)S(1)}, u32[]{:S(2)}, u32[]{:S(2)}) collective-permute-start(bf16[2,256,1024]{2,1,0:T(8,128)(2,1)S(1)} %far_add.1), channel_id=1, source_target_pairs={{0,2},{1,3},{2,0},{3,1},{4,6},{5,7},{6,4},{7,5},{8,10},{9,11},{10,... | collective-permute-start | bytes 3145736 | tf_op jit(solution)/shard_map/ppermute | solution.py:434
  67.6 13.4 %collective-permute-start.12 = (bf16[64,1024]{1,0:T(8,128)(2,1)S(1)}, bf16[64,1024]{1,0:T(8,128)(2,1)S(1)}, u32[]{:S(2)}, u32[]{:S(2)}) collective-permute-start(bf16[64,1024]{1,0:T(8,128)(2,1)S(1)} %get-tuple-element.79), channel_id=1, source_target_pairs={{0,16},{4,20},{8,24},{12,28},{16,0},{20,4},{24,8},{28,12},{1,17},{... | collective-permute-start | bytes 393224 | tf_op jit(solution)/shard_map/ppermute | solution.py:441
  71.7 12.5 %collective-permute-start.13 = (bf16[64,1024]{1,0:T(8,128)(2,1)S(1)}, bf16[64,1024]{1,0:T(8,128)(2,1)S(1)}, u32[]{:S(2)}, u32[]{:S(2)}) collective-permute-start(bf16[64,1024]{1,0:T(8,128)(2,1)S(1)} %get-tuple-element.80), channel_id=1, source_target_pairs={{0,4},{4,0},{8,12},{12,8},{16,20},{20,16},{24,28},{28,24},{1,5},{5... | collective-permute-start | bytes 393224 | tf_op jit(solution)/shard_map/ppermute | solution.py:441
  72.3 12.0 %collective-permute-start.14 = (bf16[64,1024]{1,0:T(8,128)(2,1)S(1)}, bf16[64,1024]{1,0:T(8,128)(2,1)S(1)}, u32[]{:S(2)}, u32[]{:S(2)}) collective-permute-start(bf16[64,1024]{1,0:T(8,128)(2,1)S(1)} %get-tuple-element.81), channel_id=1, source_target_pairs={{0,20},{4,16},{8,28},{12,24},{16,4},{20,0},{24,12},{28,8},{1,21},{... | collective-permute-start | bytes 393224 | tf_op jit(solution)/shard_map/ppermute | solution.py:441
  73.3 16.0 %collective-permute-start.15 = (bf16[64,1024]{1,0:T(8,128)(2,1)S(1)}, bf16[64,1024]{1,0:T(8,128)(2,1)S(1)}, u32[]{:S(2)}, u32[]{:S(2)}) collective-permute-start(bf16[64,1024]{1,0:T(8,128)(2,1)S(1)} %get-tuple-element.82), channel_id=1, source_target_pairs={{0,8},{4,12},{8,0},{12,4},{16,24},{20,28},{24,16},{28,20},{1,9},{5... | collective-permute-start | bytes 393224 | tf_op jit(solution)/shard_map/ppermute | solution.py:441
  81.0 8.3 %collective-permute-start.16 = (bf16[64,1024]{1,0:T(8,128)(2,1)S(1)}, bf16[64,1024]{1,0:T(8,128)(2,1)S(1)}, u32[]{:S(2)}, u32[]{:S(2)}) collective-permute-start(bf16[64,1024]{1,0:T(8,128)(2,1)S(1)} %get-tuple-element.83), channel_id=1, source_target_pairs={{0,24},{4,28},{8,16},{12,20},{16,8},{20,12},{24,0},{28,4},{1,25},{... | collective-permute-start | bytes 393224 | tf_op jit(solution)/shard_map/ppermute | solution.py:441
  84.2 8.8 %collective-permute-start.17 = (bf16[64,1024]{1,0:T(8,128)(2,1)S(1)}, bf16[64,1024]{1,0:T(8,128)(2,1)S(1)}, u32[]{:S(2)}, u32[]{:S(2)}) collective-permute-start(bf16[64,1024]{1,0:T(8,128)(2,1)S(1)} %get-tuple-element.84), channel_id=1, source_target_pairs={{0,12},{4,8},{8,4},{12,0},{16,28},{20,24},{24,20},{28,16},{1,13},{... | collective-permute-start | bytes 393224 | tf_op jit(solution)/shard_map/ppermute | solution.py:441
  84.3 8.7 %collective-permute-start.18 = (bf16[64,1024]{1,0:T(8,128)(2,1)S(1)}, bf16[64,1024]{1,0:T(8,128)(2,1)S(1)}, u32[]{:S(2)}, u32[]{:S(2)}) collective-permute-start(bf16[64,1024]{1,0:T(8,128)(2,1)S(1)} %get-tuple-element.85), channel_id=1, source_target_pairs={{0,28},{4,24},{8,20},{12,16},{16,12},{20,8},{24,4},{28,0},{1,29},{... | collective-permute-start | bytes 393224 | tf_op jit(solution)/shard_map/ppermute | solution.py:441

commit v7 on v6

--- a/solution.py
+++ b/solution.py
@@ -12,7 +12,8 @@
 LANES = 128
 MIB = 1024 * 1024
 PIECES = 4
-OFFSETS = (0, 4, 1, 5, 2, 6, 3, 7)
+OFFSETS = (0, 4, 2, 5, 1, 6, 3, 7)
+RETURN_OFFSETS = (0, 4, 1, 5, 2, 6, 3, 7)
 ANYWHERE = pl.BlockSpec(memory_space=pl.ANY)
 VMEM = pl.BlockSpec(memory_space=pltpu.VMEM)
 SMEM = pl.BlockSpec(memory_space=pltpu.SMEM)
@@ -562,12 +563,13 @@
     )
     token_parts = token_parts[:1] + sent
     if direct:
-        backs = in_vmem(*swap_all(token_parts))
+        home = dict(zip(OFFSETS, swap_all(token_parts)))
+        backs = in_vmem(*[home[offset] for offset in RETURN_OFFSETS])
     else:
         backs = in_hbm(exchange(token_parts[0].reshape(slots, block_rows, features)))
     grad_shape = shape(shard, lang_local, bottleneck)
     token_grad, grad_up, grad_down = pl.pallas_call(
-        functools.partial(tail_kernel, (capacity, full, direct)),
+        functools.partial(tail_kernel, (capacity, full, RETURN_OFFSETS if direct else ())),
         out_shape=(shape(*tokens.shape), grad_shape, grad_shape),
         in_specs=[SMEM] + [VMEM] * 2 + [VMEM if direct else ANYWHERE] * len(backs),
         out_specs=(ANYWHERE,) * 3,

time: 95.8 us -> 95.8 us (level)
  no operation moved by 1% of the time
where the time goes in v7:
time: 95.8 us; the launch traced here: 95.6 us
  waiting for transfers between devices  47.2 us (49%)
  starting transfers between devices  31.3 us (33%)
  Pallas kernels  16.1 us (17%)
    ppermute x14, waiting for transfers between devices, swap_all(): lax.ppermute(chunk, 'dp', [(i, i ^ offset) for i in range(dp_size)])  43.5 us
    ppermute x14, starting transfers between devices, swap_all(): lax.ppermute(chunk, 'dp', [(i, i ^ offset) for i in range(dp_size)])  25.5 us
    ppermute x5, starting transfers between devices, swap(): return lax.ppermute(array, 'mp', [(i, i ^ bit) for i in range(mp_size)])  5.8 us
    pallas_call x1, Pallas kernels, shards(): pl.pallas_call(functools.partial(weight_grad_kernel, (capacity, mp_size,...  5.66 us
    ppermute x5, waiting for transfers between devices, swap(): return lax.ppermute(array, 'mp', [(i, i ^ bit) for i in range(mp_size)])  3.67 us
    pallas_call x1, Pallas kernels, shards(): pl.pallas_call(functools.partial(token_grad_kernel, (tile, chunk_rows, di...  3.09 us
    pallas_call x1, Pallas kernels, shards(): pl.pallas_call(functools.partial(tail_kernel, (capacity, full, RETURN_OFF...  2.58 us
    pallas_call x1, Pallas kernels, shards(): pl.pallas_call(functools.partial(pack_kernel, (dp_size, capacity, lang_lo...  2.31 us
  transfers between devices with their start and end apart: 19, of which 7 were waited for; matrix products, arithmetic and copies ran while one was open for 0% of the time, Pallas kernels for 6%

profile of v7, /device:TPU:0, one launch (start us, length us, event | category | flops | bytes accessed | tf_op | source)
XLA Modules:
  0.0 95.6 jit_solution(12685289089702923922)
XLA Ops:
  0.6 1.2 %load.1 = (bf16[256,2,512]{2,1,0:T(2,128)(2,1)S(1)}, bf16[256,2,512]{2,1,0:T(2,128)(2,1)S(1)}) custom-call(bf16[256,2,512]{2,1,0:T(2,128)(2,1)} %down_hbm.1, bf16[256,2,512]{2,1,0:T(2,128)(2,1)} %up_hbm.1), custom_call_target="tpu_custom_call" | custom-call | tf_op jit(solution)/shard_map/load/pallas_call | solution.py:468
  2.6 2.3 %pack.1 = (bf16[16,8320]{1,0:T(8,128)(2,1)S(1)}, bf16[16,8320]{1,0:T(8,128)(2,1)S(1)}, bf16[16,8320]{1,0:T(8,128)(2,1)S(1)}, bf16[16,8320]{1,0:T(8,128)(2,1)S(1)...) custom-call(s32[16]{0:T(128)} %lang_hbm.1, ...), custom_call_target="tpu_custom_call" | custom-call | tf_op jit(solution)/shard_map/pack/pallas_call | solution.py:449
  5.0 0.8 pair.1.refs_8_
  5.8 2.9 %collective-permute-start.8 = (bf16[1056,1024]{1,0:T(8,128)(2,1)S(1)}, bf16[1056,1024]{1,0:T(8,128)(2,1)S(1)}, u32[]{:S(2)}, u32[]{:S(2)}) collective-permute-start(bf16[1056,1024]{1,0:T(8,128)(2,1)S(1)} %pair.1.refs_8_), channel_id=1, source_target_pairs={{0,2},{1,3},{2,0},{3,1},{4,6},{5,7},{6,4},{7,5},{8,10},{9,11},{10,... | collective-permute-start | bytes 6488072 | tf_op jit(solution)/shard_map/ppermute | solution.py:435
  8.7 2.6 %collective-permute-start = (bf16[16,8320]{1,0:T(8,128)(2,1)S(1)}, bf16[16,8320]{1,0:T(8,128)(2,1)S(1)}, u32[]{:S(2)}, u32[]{:S(2)}) collective-permute-start(bf16[16,8320]{1,0:T(8,128)(2,1)S(1)} %get-tuple-element.48), channel_id=1, source_target_pairs={{0,16},{4,20},{8,24},{12,28},{16,0},{20,4},{24,8},{28,12},{1,17},{... | collective-permute-start | bytes 798728 | tf_op jit(solution)/shard_map/ppermute | solution.py:442
  11.3 1.6 %collective-permute-start.1 = (bf16[16,8320]{1,0:T(8,128)(2,1)S(1)}, bf16[16,8320]{1,0:T(8,128)(2,1)S(1)}, u32[]{:S(2)}, u32[]{:S(2)}) collective-permute-start(bf16[16,8320]{1,0:T(8,128)(2,1)S(1)} %get-tuple-element.49), channel_id=1, source_target_pairs={{0,8},{4,12},{8,0},{12,4},{16,24},{20,28},{24,16},{28,20},{1,9},{5... | collective-permute-start | bytes 798728 | tf_op jit(solution)/shard_map/ppermute | solution.py:442
  12.9 1.3 %collective-permute-start.2 = (bf16[16,8320]{1,0:T(8,128)(2,1)S(1)}, bf16[16,8320]{1,0:T(8,128)(2,1)S(1)}, u32[]{:S(2)}, u32[]{:S(2)}) collective-permute-start(bf16[16,8320]{1,0:T(8,128)(2,1)S(1)} %get-tuple-element.50), channel_id=1, source_target_pairs={{0,20},{4,16},{8,28},{12,24},{16,4},{20,0},{24,12},{28,8},{1,21},{... | collective-permute-start | bytes 798728 | tf_op jit(solution)/shard_map/ppermute | solution.py:442
  14.7 11.0 %collective-permute-done.refs_1_ = bf16[16,8320]{1,0:T(8,128)(2,1)S(1)} collective-permute-done((bf16[16,8320]{1,0:T(8,128)(2,1)S(1)}, bf16[16,8320]{1,0:T(8,128)(2,1)S(1)}, u32[]{:S(2)}, u32[]{:S(2)}) %collective-permute-start) | collective-permute-done | bytes 266272 | tf_op jit(solution)/shard_map/ppermute | solution.py:442
  25.7 2.5 %collective-permute-start.4 = (bf16[16,8320]{1,0:T(8,128)(2,1)S(1)}, bf16[16,8320]{1,0:T(8,128)(2,1)S(1)}, u32[]{:S(2)}, u32[]{:S(2)}) collective-permute-start(bf16[16,8320]{1,0:T(8,128)(2,1)S(1)} %get-tuple-element.52), channel_id=1, source_target_pairs={{0,24},{4,28},{8,16},{12,20},{16,8},{20,12},{24,0},{28,4},{1,25},{... | collective-permute-start | bytes 798728 | tf_op jit(solution)/shard_map/ppermute | solution.py:442
  28.2 14.5 %collective-permute-done.2.refs_3_ = bf16[16,8320]{1,0:T(8,128)(2,1)S(1)} collective-permute-done((bf16[16,8320]{1,0:T(8,128)(2,1)S(1)}, bf16[16,8320]{1,0:T(8,128)(2,1)S(1)}, u32[]{:S(2)}, u32[]{:S(2)}) %collective-permute-start.2) | collective-permute-done | bytes 266272 | tf_op jit(solution)/shard_map/ppermute | solution.py:442
  42.7 2.4 %collective-permute-start.6 = (bf16[16,8320]{1,0:T(8,128)(2,1)S(1)}, bf16[16,8320]{1,0:T(8,128)(2,1)S(1)}, u32[]{:S(2)}, u32[]{:S(2)}) collective-permute-start(bf16[16,8320]{1,0:T(8,128)(2,1)S(1)} %get-tuple-element.54), channel_id=1, source_target_pairs={{0,28},{4,24},{8,20},{12,16},{16,12},{20,8},{24,4},{28,0},{1,29},{... | collective-permute-start | bytes 798728 | tf_op jit(solution)/shard_map/ppermute | solution.py:442
  45.1 7.3 %collective-permute-done.5.refs_6_ = bf16[16,8320]{1,0:T(8,128)(2,1)S(1)} collective-permute-done((bf16[16,8320]{1,0:T(8,128)(2,1)S(1)}, bf16[16,8320]{1,0:T(8,128)(2,1)S(1)}, u32[]{:S(2)}, u32[]{:S(2)}) %collective-permute-start.5) | collective-permute-done | bytes 266272 | tf_op jit(solution)/shard_map/ppermute | solution.py:442
  52.4 3.6 %collective-permute-done.8.refs_9_ = bf16[1056,1024]{1,0:T(8,128)(2,1)S(1)} collective-permute-done((bf16[1056,1024]{1,0:T(8,128)(2,1)S(1)}, bf16[1056,1024]{1,0:T(8,128)(2,1)S(1)}, u32[]{:S(2)}, u32[]{:S(2)}) %collective-permute-start.8) | collective-permute-done | bytes 2162720 | tf_op jit(solution)/shard_map/ppermute | solution.py:435
  56.0 5.7 %weight_grads.1 = (bf16[2,256,1024]{2,1,0:T(8,128)(2,1)S(1)}, bf16[2,256,1024]{2,1,0:T(8,128)(2,1)S(1)}, bf16[512,1024]{1,0:T(8,128)(2,1)S(1)}, bf16[512,1024]{1...) custom-call(bf16[16,8320]{1,0:T(8,128)(2,1)S(1)} %get-tuple-element., ...), custom_call_target="tpu_custom_call" | custom-call | tf_op jit(solution)/shard_map/weight_grads/pallas_call | solution.py:500
  62.3 3.1 %token_grads.1 = (bf16[2,256,1024]{2,1,0:T(8,128)(2,1)S(1)}, bf16[2,256,1024]{2,1,0:T(8,128)(2,1)S(1)}, bf16[64,1024]{1,0:T(8,128)(2,1)S(1)}, bf16[64,1024]{1,0:...) custom-call(bf16[512,1024]{1,0:T(8,128)(2,1)S(1)} %get-tuple-element, ...), custom_call_target="tpu_custom_call" | custom-call | tf_op jit(solution)/shard_map/token_grads/pallas_call | solution.py:531
  65.6 1.8 %collective-permute-start.11 = (bf16[2,256,1024]{2,1,0:T(8,128)(2,1)S(1)}, bf16[2,256,1024]{2,1,0:T(8,128)(2,1)S(1)}, u32[]{:S(2)}, u32[]{:S(2)}) collective-permute-start(bf16[2,256,1024]{2,1,0:T(8,128)(2,1)S(1)} %far_add.1), channel_id=1, source_target_pairs={{0,2},{1,3},{2,0},{3,1},{4,6},{5,7},{6,4},{7,5},{8,10},{9,11},{10,... | collective-permute-start | bytes 3145736 | tf_op jit(solution)/shard_map/ppermute | solution.py:435
  67.6 4.1 %collective-permute-start.12 = (bf16[64,1024]{1,0:T(8,128)(2,1)S(1)}, bf16[64,1024]{1,0:T(8,128)(2,1)S(1)}, u32[]{:S(2)}, u32[]{:S(2)}) collective-permute-start(bf16[64,1024]{1,0:T(8,128)(2,1)S(1)} %get-tuple-element.79), channel_id=1, source_target_pairs={{0,16},{4,20},{8,24},{12,28},{16,0},{20,4},{24,8},{28,12},{1,17},{... | collective-permute-start | bytes 393224 | tf_op jit(solution)/shard_map/ppermute | solution.py:442
  72.3 1.0 %collective-permute-start.14 = (bf16[64,1024]{1,0:T(8,128)(2,1)S(1)}, bf16[64,1024]{1,0:T(8,128)(2,1)S(1)}, u32[]{:S(2)}, u32[]{:S(2)}) collective-permute-start(bf16[64,1024]{1,0:T(8,128)(2,1)S(1)} %get-tuple-element.81), channel_id=1, source_target_pairs={{0,20},{4,16},{8,28},{12,24},{16,4},{20,0},{24,12},{28,8},{1,21},{... | collective-permute-start | bytes 393224 | tf_op jit(solution)/shard_map/ppermute | solution.py:442
  73.3 0.9 collective-permute-start.15
  74.2 6.9 %collective-permute-done.12.refs_1_ = bf16[64,1024]{1,0:T(8,128)(2,1)S(1)} collective-permute-done((bf16[64,1024]{1,0:T(8,128)(2,1)S(1)}, bf16[64,1024]{1,0:T(8,128)(2,1)S(1)}, u32[]{:S(2)}, u32[]{:S(2)}) %collective-permute-start.12) | collective-permute-done | bytes 131104 | tf_op jit(solution)/shard_map/ppermute | solution.py:442
  81.1 3.1 %collective-permute-start.16 = (bf16[64,1024]{1,0:T(8,128)(2,1)S(1)}, bf16[64,1024]{1,0:T(8,128)(2,1)S(1)}, u32[]{:S(2)}, u32[]{:S(2)}) collective-permute-start(bf16[64,1024]{1,0:T(8,128)(2,1)S(1)} %get-tuple-element.83), channel_id=1, source_target_pairs={{0,24},{4,28},{8,16},{12,20},{16,8},{20,12},{24,0},{28,4},{1,25},{... | collective-permute-start | bytes 393224 | tf_op jit(solution)/shard_map/ppermute | solution.py:442
  84.3 5.0 %collective-permute-start.18 = (bf16[64,1024]{1,0:T(8,128)(2,1)S(1)}, bf16[64,1024]{1,0:T(8,128)(2,1)S(1)}, u32[]{:S(2)}, u32[]{:S(2)}) collective-permute-start(bf16[64,1024]{1,0:T(8,128)(2,1)S(1)} %get-tuple-element.85), channel_id=1, source_target_pairs={{0,28},{4,24},{8,20},{12,16},{16,12},{20,8},{24,4},{28,0},{1,29},{... | collective-permute-start | bytes 393224 | tf_op jit(solution)/shard_map/ppermute | solution.py:442
  89.3 3.7 %collective-permute-done.17.refs_6_ = bf16[64,1024]{1,0:T(8,128)(2,1)S(1)} collective-permute-done((bf16[64,1024]{1,0:T(8,128)(2,1)S(1)}, bf16[64,1024]{1,0:T(8,128)(2,1)S(1)}, u32[]{:S(2)}, u32[]{:S(2)}) %collective-permute-start.17) | collective-permute-done | bytes 131104 | tf_op jit(solution)/shard_map/ppermute | solution.py:442
  93.0 2.6 %tail.1 = (bf16[16,32,1024]{2,1,0:T(8,128)(2,1)}, bf16[256,2,512]{2,1,0:T(2,128)(2,1)}, bf16[256,2,512]{2,1,0:T(2,128)(2,1)}) custom-call(s32[16]{0:T(128)S(1)} %get-tuple-element.46.after_ref.source_ref, f32[2,256,1024]{2,1,0:T(8,128)S(1)} %get-tuple-element.75.own_ref, bf16[2,256,1024]{2,1,0:T(8,128)(2,1)S(1)} %collective-permute-done.11.far_ref, ...), custom_call_target="tpu_custom_call" | custom-call | tf_op jit(solution)/shard_map/tail/pallas_call | solution.py:571
  (27 shorter events, 2.9 us)
Async XLA Ops:
  0.6 1.4 %copy-start = (bf16[256,2]{0,1:T(2,128)(2,1)S(1)}, bf16[256,2]{0,1:T(2,128)(2,1)}, u32[]{:S(2)}) copy-start(bf16[256,2]{0,1:T(2,128)(2,1)} %param.13) | copy-start | bytes 3076
  2.1 2.9 %collective-permute-start.7 = (bf16[528,1024]{1,0:T(8,128)(2,1)S(1)}, bf16[528,1024]{1,0:T(8,128)(2,1)S(1)}, u32[]{:S(2)}, u32[]{:S(2)}) collective-permute-start(bf16[528,1024]{1,0:T(8,128)(2,1)S(1)} %fusion.1.own_hbm), channel_id=1, source_target_pairs={{0,1},{1,0},{2,3},{3,2},{4,5},{5,4},{6,7},{7,6},{8,9},{9,8},{10,11... | collective-permute-start | bytes 3244040 | tf_op jit(solution)/shard_map/ppermute | solution.py:435
  5.8 50.3 %collective-permute-start.8 = (bf16[1056,1024]{1,0:T(8,128)(2,1)S(1)}, bf16[1056,1024]{1,0:T(8,128)(2,1)S(1)}, u32[]{:S(2)}, u32[]{:S(2)}) collective-permute-start(bf16[1056,1024]{1,0:T(8,128)(2,1)S(1)} %pair.1.refs_8_), channel_id=1, source_target_pairs={{0,2},{1,3},{2,0},{3,1},{4,6},{5,7},{6,4},{7,5},{8,10},{9,11},{10,... | collective-permute-start | bytes 6488072 | tf_op jit(solution)/shard_map/ppermute | solution.py:435
  8.7 17.0 %collective-permute-start = (bf16[16,8320]{1,0:T(8,128)(2,1)S(1)}, bf16[16,8320]{1,0:T(8,128)(2,1)S(1)}, u32[]{:S(2)}, u32[]{:S(2)}) collective-permute-start(bf16[16,8320]{1,0:T(8,128)(2,1)S(1)} %get-tuple-element.48), channel_id=1, source_target_pairs={{0,16},{4,20},{8,24},{12,28},{16,0},{20,4},{24,8},{28,12},{1,17},{... | collective-permute-start | bytes 798728 | tf_op jit(solution)/shard_map/ppermute | solution.py:442
  11.3 16.9 %collective-permute-start.1 = (bf16[16,8320]{1,0:T(8,128)(2,1)S(1)}, bf16[16,8320]{1,0:T(8,128)(2,1)S(1)}, u32[]{:S(2)}, u32[]{:S(2)}) collective-permute-start(bf16[16,8320]{1,0:T(8,128)(2,1)S(1)} %get-tuple-element.49), channel_id=1, source_target_pairs={{0,8},{4,12},{8,0},{12,4},{16,24},{20,28},{24,16},{28,20},{1,9},{5... | collective-permute-start | bytes 798728 | tf_op jit(solution)/shard_map/ppermute | solution.py:442
  12.9 29.9 %collective-permute-start.2 = (bf16[16,8320]{1,0:T(8,128)(2,1)S(1)}, bf16[16,8320]{1,0:T(8,128)(2,1)S(1)}, u32[]{:S(2)}, u32[]{:S(2)}) collective-permute-start(bf16[16,8320]{1,0:T(8,128)(2,1)S(1)} %get-tuple-element.50), channel_id=1, source_target_pairs={{0,20},{4,16},{8,28},{12,24},{16,4},{20,0},{24,12},{28,8},{1,21},{... | collective-permute-start | bytes 798728 | tf_op jit(solution)/shard_map/ppermute | solution.py:442
  14.1 30.9 %collective-permute-start.3 = (bf16[16,8320]{1,0:T(8,128)(2,1)S(1)}, bf16[16,8320]{1,0:T(8,128)(2,1)S(1)}, u32[]{:S(2)}, u32[]{:S(2)}) collective-permute-start(bf16[16,8320]{1,0:T(8,128)(2,1)S(1)} %get-tuple-element.51), channel_id=1, source_target_pairs={{0,4},{4,0},{8,12},{12,8},{16,20},{20,16},{24,28},{28,24},{1,5},{5... | collective-permute-start | bytes 798728 | tf_op jit(solution)/shard_map/ppermute | solution.py:442
  25.7 19.4 %collective-permute-start.4 = (bf16[16,8320]{1,0:T(8,128)(2,1)S(1)}, bf16[16,8320]{1,0:T(8,128)(2,1)S(1)}, u32[]{:S(2)}, u32[]{:S(2)}) collective-permute-start(bf16[16,8320]{1,0:T(8,128)(2,1)S(1)} %get-tuple-element.52), channel_id=1, source_target_pairs={{0,24},{4,28},{8,16},{12,20},{16,8},{20,12},{24,0},{28,4},{1,25},{... | collective-permute-start | bytes 798728 | tf_op jit(solution)/shard_map/ppermute | solution.py:442
  28.2 24.2 %collective-permute-start.5 = (bf16[16,8320]{1,0:T(8,128)(2,1)S(1)}, bf16[16,8320]{1,0:T(8,128)(2,1)S(1)}, u32[]{:S(2)}, u32[]{:S(2)}) collective-permute-start(bf16[16,8320]{1,0:T(8,128)(2,1)S(1)} %get-tuple-element.53), channel_id=1, source_target_pairs={{0,12},{4,8},{8,4},{12,0},{16,28},{20,24},{24,20},{28,16},{1,13},{... | collective-permute-start | bytes 798728 | tf_op jit(solution)/shard_map/ppermute | solution.py:442
  42.7 9.7 %collective-permute-start.6 = (bf16[16,8320]{1,0:T(8,128)(2,1)S(1)}, bf16[16,8320]{1,0:T(8,128)(2,1)S(1)}, u32[]{:S(2)}, u32[]{:S(2)}) collective-permute-start(bf16[16,8320]{1,0:T(8,128)(2,1)S(1)} %get-tuple-element.54), channel_id=1, source_target_pairs={{0,28},{4,24},{8,20},{12,16},{16,12},{20,8},{24,4},{28,0},{1,29},{... | collective-permute-start | bytes 798728 | tf_op jit(solution)/shard_map/ppermute | solution.py:442
  61.7 3.7 %collective-permute-start.10 = (bf16[2,256,1024]{2,1,0:T(8,128)(2,1)S(1)}, bf16[2,256,1024]{2,1,0:T(8,128)(2,1)S(1)}, u32[]{:S(2)}, u32[]{:S(2)}) collective-permute-start(bf16[2,256,1024]{2,1,0:T(8,128)(2,1)S(1)} %get-tuple-element.77), channel_id=1, source_target_pairs={{0,1},{1,0},{2,3},{3,2},{4,5},{5,4},{6,7},{7,6},{8,9},{9,8},{10,11... | collective-permute-start | bytes 3145736 | tf_op jit(solution)/shard_map/ppermute | solution.py:435
  61.8 5.7 %collective-permute-start.9 = (bf16[2,256,1024]{2,1,0:T(8,128)(2,1)S(1)}, bf16[2,256,1024]{2,1,0:T(8,128)(2,1)S(1)}, u32[]{:S(2)}, u32[]{:S(2)}) collective-permute-start(bf16[2,256,1024]{2,1,0:T(8,128)(2,1)S(1)} %get-tuple-element.67), channel_id=1, source_target_pairs={{0,1},{1,0},{2,3},{3,2},{4,5},{5,4},{6,7},{7,6},{8,9},{9,8},{10,11... | collective-permute-start | bytes 3145736 | tf_op jit(solution)/shard_map/ppermute | solution.py:435
  65.6 27.4 %collective-permute-start.11 = (bf16[2,256,1024]{2,1,0:T(8,128)(2,1)S(1)}, bf16[2,256,1024]{2,1,0:T(8,128)(2,1)S(1)}, u32[]{:S(2)}, u32[]{:S(2)}) collective-permute-start(bf16[2,256,1024]{2,1,0:T(8,128)(2,1)S(1)} %far_add.1), channel_id=1, source_target_pairs={{0,2},{1,3},{2,0},{3,1},{4,6},{5,7},{6,4},{7,5},{8,10},{9,11},{10,... | collective-permute-start | bytes 3145736 | tf_op jit(solution)/shard_map/ppermute | solution.py:435
  67.6 13.4 %collective-permute-start.12 = (bf16[64,1024]{1,0:T(8,128)(2,1)S(1)}, bf16[64,1024]{1,0:T(8,128)(2,1)S(1)}, u32[]{:S(2)}, u32[]{:S(2)}) collective-permute-start(bf16[64,1024]{1,0:T(8,128)(2,1)S(1)} %get-tuple-element.79), channel_id=1, source_target_pairs={{0,16},{4,20},{8,24},{12,28},{16,0},{20,4},{24,8},{28,12},{1,17},{... | collective-permute-start | bytes 393224 | tf_op jit(solution)/shard_map/ppermute | solution.py:442
  71.7 12.5 %collective-permute-start.13 = (bf16[64,1024]{1,0:T(8,128)(2,1)S(1)}, bf16[64,1024]{1,0:T(8,128)(2,1)S(1)}, u32[]{:S(2)}, u32[]{:S(2)}) collective-permute-start(bf16[64,1024]{1,0:T(8,128)(2,1)S(1)} %get-tuple-element.80), channel_id=1, source_target_pairs={{0,4},{4,0},{8,12},{12,8},{16,20},{20,16},{24,28},{28,24},{1,5},{5... | collective-permute-start | bytes 393224 | tf_op jit(solution)/shard_map/ppermute | solution.py:442
  72.3 12.0 %collective-permute-start.14 = (bf16[64,1024]{1,0:T(8,128)(2,1)S(1)}, bf16[64,1024]{1,0:T(8,128)(2,1)S(1)}, u32[]{:S(2)}, u32[]{:S(2)}) collective-permute-start(bf16[64,1024]{1,0:T(8,128)(2,1)S(1)} %get-tuple-element.81), channel_id=1, source_target_pairs={{0,20},{4,16},{8,28},{12,24},{16,4},{20,0},{24,12},{28,8},{1,21},{... | collective-permute-start | bytes 393224 | tf_op jit(solution)/shard_map/ppermute | solution.py:442
  73.3 16.0 %collective-permute-start.15 = (bf16[64,1024]{1,0:T(8,128)(2,1)S(1)}, bf16[64,1024]{1,0:T(8,128)(2,1)S(1)}, u32[]{:S(2)}, u32[]{:S(2)}) collective-permute-start(bf16[64,1024]{1,0:T(8,128)(2,1)S(1)} %get-tuple-element.82), channel_id=1, source_target_pairs={{0,8},{4,12},{8,0},{12,4},{16,24},{20,28},{24,16},{28,20},{1,9},{5... | collective-permute-start | bytes 393224 | tf_op jit(solution)/shard_map/ppermute | solution.py:442
  81.1 8.3 %collective-permute-start.16 = (bf16[64,1024]{1,0:T(8,128)(2,1)S(1)}, bf16[64,1024]{1,0:T(8,128)(2,1)S(1)}, u32[]{:S(2)}, u32[]{:S(2)}) collective-permute-start(bf16[64,1024]{1,0:T(8,128)(2,1)S(1)} %get-tuple-element.83), channel_id=1, source_target_pairs={{0,24},{4,28},{8,16},{12,20},{16,8},{20,12},{24,0},{28,4},{1,25},{... | collective-permute-start | bytes 393224 | tf_op jit(solution)/shard_map/ppermute | solution.py:442
  84.2 8.8 %collective-permute-start.17 = (bf16[64,1024]{1,0:T(8,128)(2,1)S(1)}, bf16[64,1024]{1,0:T(8,128)(2,1)S(1)}, u32[]{:S(2)}, u32[]{:S(2)}) collective-permute-start(bf16[64,1024]{1,0:T(8,128)(2,1)S(1)} %get-tuple-element.84), channel_id=1, source_target_pairs={{0,12},{4,8},{8,4},{12,0},{16,28},{20,24},{24,20},{28,16},{1,13},{... | collective-permute-start | bytes 393224 | tf_op jit(solution)/shard_map/ppermute | solution.py:442
  84.3 8.7 %collective-permute-start.18 = (bf16[64,1024]{1,0:T(8,128)(2,1)S(1)}, bf16[64,1024]{1,0:T(8,128)(2,1)S(1)}, u32[]{:S(2)}, u32[]{:S(2)}) collective-permute-start(bf16[64,1024]{1,0:T(8,128)(2,1)S(1)} %get-tuple-element.85), channel_id=1, source_target_pairs={{0,28},{4,24},{8,20},{12,16},{16,12},{20,8},{24,4},{28,0},{1,29},{... | collective-permute-start | bytes 393224 | tf_op jit(solution)/shard_map/ppermute | solution.py:442
